TPU v7x, 32 devices: a whole 2x2x4 slice. The times are simulated.
32 devices in a mesh: dp: 8 (over z, x), seq: 4 (over y, core).
Axes of the slice: x: 2, y: 2, z: 4, core: 2. Of those that a mesh axis runs over, the one named last changes fastest.
Arguments:
- hidden_in: bfloat16 [8, 2048, 2048], P('dp', 'seq'), may hold values from -6 to 6
- widths: int32 [8], P('dp'), may hold values from 0 to 3
- norm_gain: bfloat16 [2048], P(('dp', 'seq')), may hold values from 0.099609375 to 1.8984375
- w_in: bfloat16 [2048, 8448], P(('dp', 'seq')), may hold values from -0.125 to 0.125
- w_dt: bfloat16 [2048, 64], P(('dp', 'seq')), may hold values from -0.125 to 0.125
- conv_weight: bfloat16 [4, 4352], replicated, may hold values from -3 to 3
- dt_bias: float32 [64], replicated, may hold values from -3 to 0
- a_log: float32 [64], replicated, may hold values from -9 to -2.3
- skip_gain: float32 [64], replicated, may hold values from 0.5 to 1.5
- gate_gain: bfloat16 [4096], P(('dp', 'seq')), may hold values from 0.099609375 to 1.8984375
- w_out: bfloat16 [4096, 2048], P(('dp', 'seq')), may hold values from -0.125 to 0.125
- grad_out: bfloat16 [8, 2048, 2048], P('dp', 'seq'), may hold values from -6 to 6
Outputs:
- hidden_out: bfloat16 [8, 2048, 2048], P('dp', 'seq')
- grad_in: bfloat16 [8, 2048, 2048], P('dp', 'seq')
- grad_norm_gain: float32 [2048], P(('dp', 'seq'))
- grad_w_in: float32 [2048, 8448], P(('dp', 'seq'))
- grad_w_dt: float32 [2048, 64], P(('dp', 'seq'))
- grad_conv: float32 [4, 4352], replicated
- grad_dt_bias: float32 [64], replicated
- grad_a_log: float32 [64], replicated
- grad_skip: float32 [64], replicated
- grad_gate_gain: float32 [4096], P(('dp', 'seq'))
- grad_w_out: float32 [4096, 2048], P(('dp', 'seq'))
Inputs may be any that keep to these rules, and one draw needn't show every extreme that they name: `widths`: level of the nested width of each sequence: it uses the first 4096 * 2^level / 8 inner units and their heads.
All inputs are finite; a program needn't handle non-finite values.
Results may differ from a plain program's by a relative error of at most 0.0095.
Values may be sent and summed in bfloat16 or wider, within the bound.
No kernel may reach another device: no remote copies, remote signals or barrier semaphores. Data moves between devices by JAX's collectives and lax.ppermute only.
A program may use at most 448 MiB of HBM per device.

v0:
```python
import jax
import jax.numpy as jnp
from jax import lax
from jax.sharding import PartitionSpec as P

D = 2048
INNER = 4096
HEAD_DIM = 64
STATE = 128
CONV = 4
BLOCK = 256
HEADS = 64
CHANNELS = 4352


epsilon = 1e-05
highest = lax.Precision.HIGHEST


def passed_along(value, axis, steps):
    count = lax.axis_size(axis)
    initial, last = (max(0, -steps), min(count, count - steps))
    return lax.ppermute(value, axis, [(source, source + steps) for source in range(initial, last)])


def prefix(shard, axis, join, neutral):
    place = lax.axis_index(axis)
    gathered = jax.tree.map(
        lambda a, kind: lax.all_gather(a.astype(kind), axis), shard, (jnp.bfloat16, jnp.bfloat16)
    )
    state = jax.tree.map(lambda a, e: jnp.zeros_like(a) + jnp.asarray(e, a.dtype), shard, neutral)

    def prefix_one(lap, state):
        return join(
            state,
            jax.tree.map(
                lambda a, own: lax.dynamic_index_in_dim(a, lap, 0, False).astype(own.dtype),
                gathered,
                shard,
            ),
        )

    return lax.fori_loop(0, place, prefix_one, state)


def carried_in(shard, axis, join, neutral):
    count = lax.axis_size(axis)
    place = lax.axis_index(axis)
    ahead = count - 1 - place
    gathered = jax.tree.map(
        lambda a, kind: lax.all_gather(a.astype(kind), axis),
        shard,
        jax.tree.map(lambda a: jnp.bfloat16 if a.dtype == jnp.float32 else a.dtype, shard),
    )
    state = jax.tree.map(lambda a, e: jnp.zeros_like(a) + jnp.asarray(e, a.dtype), shard, neutral)

    def carried_one(lap, state):
        source = count - 1 - lap
        return join(
            state,
            jax.tree.map(
                lambda a, own: lax.dynamic_index_in_dim(a, source, 0, False).astype(own.dtype),
                gathered,
                shard,
            ),
        )

    return lax.fori_loop(0, ahead, carried_one, state)


def bf_dot(first_op, second_op):
    return jnp.dot(first_op, second_op, preferred_element_type=jnp.float32)


def cross_dot(first_op, second_op):
    return lax.dot_general(
        first_op, second_op, (((1,), (1,)), ((), ())), preferred_element_type=jnp.float32
    )


def outer_dot(first_op, second_op):
    return lax.dot_general(
        first_op, second_op, (((0,), (0,)), ((), ())), preferred_element_type=jnp.float32
    )


def silu_slope(argument):
    squashed = jax.nn.sigmoid(argument)
    return squashed * (1.0 + argument * (1.0 - squashed))


def block_step(carry_state, inputs):
    values, keys_b, reads_c, steps_dt, log_decay = inputs
    cumulative = jnp.cumsum(log_decay, axis=0)
    position = jnp.arange(values.shape[0])
    causal = (position[:, None] >= position[None, :])[:, :, None]
    spread = cumulative[:, None, :] - cumulative[None, :, :]
    decays = jnp.where(causal, jnp.exp(jnp.where(causal, spread, 0.0)), 0.0)
    intersection = jnp.dot(reads_c, keys_b.T, precision=highest, preferred_element_type=jnp.float32)
    mixing = decays * intersection[:, :, None] * steps_dt[None, :, :]
    output = jnp.einsum("tsh,shp->thp", mixing, values, precision=highest)
    output = output + jnp.exp(cumulative)[:, :, None] * jnp.einsum(
        "hpn,tn->thp", carry_state, reads_c, precision=highest
    )
    weights_end = jnp.exp(cumulative[-1][None, :] - cumulative) * steps_dt
    updated = jnp.exp(cumulative[-1])[:, None, None] * carry_state + jnp.einsum(
        "sh,shp,sn->hpn", weights_end, values, keys_b, precision=highest
    )
    return (updated, output)


def block_pass(activated, dt_raw, dt_bias, a_log):
    tokens = activated.shape[0]
    values = activated[:, :INNER].reshape(tokens, HEADS, HEAD_DIM)
    keys_b = activated[:, INNER : INNER + STATE]
    reads_c = activated[:, INNER + STATE :]
    steps_dt = jax.nn.softplus(dt_raw + dt_bias)
    log_decay = -jnp.exp(a_log) * steps_dt
    blocks = tokens // BLOCK
    inputs = (
        values.reshape(blocks, BLOCK, HEADS, HEAD_DIM),
        keys_b.reshape(blocks, BLOCK, STATE),
        reads_c.reshape(blocks, BLOCK, STATE),
        steps_dt.reshape(blocks, BLOCK, HEADS),
        log_decay.reshape(blocks, BLOCK, HEADS),
    )
    start_state = jnp.zeros((HEADS, HEAD_DIM, STATE), jnp.float32)
    final_state, outputs = lax.scan(jax.checkpoint(block_step), start_state, inputs)
    running = jnp.cumsum(log_decay, axis=0)
    return (outputs.reshape(tokens, HEADS, HEAD_DIM), final_state, running, values, reads_c)


def local_ssd(activated, dt_raw, dt_bias, a_log, skip_gain, entry_state):
    outputs, final_state, running, values, reads_c = block_pass(activated, dt_raw, dt_bias, a_log)
    carried = jnp.exp(running)[:, :, None] * jnp.einsum(
        "hpn,tn->thp", entry_state, reads_c, precision=highest
    )
    result = outputs + carried + skip_gain[:, None] * values
    leaving = jnp.exp(running[-1])[:, None, None] * entry_state + final_state
    return (result.reshape(result.shape[0], INNER), leaving)


def join_states(earlier, follower):
    return (earlier[0] * follower[0], follower[0][:, None, None] * earlier[1] + follower[1])


def per_device(
    hidden_in,
    widths,
    norm_gain,
    w_in,
    w_dt,
    conv_weight,
    dt_bias,
    a_log,
    skip_gain,
    gate_gain,
    w_out,
    grad_out,
):
    tokens = hidden_in.shape[1]
    width_level = widths[0]
    used_units = INNER // 8 * jnp.left_shift(jnp.int32(1), width_level)
    units_float = used_units.astype(jnp.float32)
    head_mask = (jnp.arange(HEADS) * HEAD_DIM < used_units).astype(jnp.float32)
    prefix_spans = [INNER // 8, INNER // 4, INNER // 2, INNER]
    x_in = hidden_in[0].astype(jnp.float32)
    inverse_rms = lax.rsqrt(jnp.mean(x_in * x_in, axis=1, keepdims=True) + epsilon)
    scaled = x_in * inverse_rms

    def project_rows(partial_sums, pieces):
        gain_piece, in_piece, dt_piece = pieces
        row_count = gain_piece.shape[0]
        normed = (scaled * gain_piece.astype(jnp.float32)).astype(jnp.bfloat16)
        gate_acc, conv_acc, dt_acc = partial_sums

        def widen(span_width):

            def widen_apply_width(operands):
                gate_part, conv_part = operands
                gate_part = gate_part.at[:, :span_width].add(
                    bf_dot(normed, in_piece[:, :span_width])
                )
                conv_part = conv_part.at[:, :span_width].add(
                    bf_dot(normed, in_piece[:, INNER : INNER + span_width])
                )
                return (gate_part, conv_part)

            return widen_apply_width

        gate_acc, conv_acc = lax.switch(
            width_level, [widen(span_width) for span_width in prefix_spans], (gate_acc, conv_acc)
        )
        conv_acc = conv_acc.at[:, INNER:].add(bf_dot(normed, in_piece[:, 2 * INNER :]))
        dt_acc = bf_dot(normed, dt_piece)
        return (gate_acc, conv_acc, dt_acc)

    empty_proj = (
        jnp.zeros((tokens, INNER), jnp.float32),
        jnp.zeros((tokens, CHANNELS), jnp.float32),
        jnp.zeros((tokens, HEADS), jnp.float32),
    )
    z_gate, conv_acc, dt_acc = project_rows(
        empty_proj,
        (
            lax.all_gather(norm_gain, ("dp", "seq"), axis=0, tiled=True),
            lax.all_gather(w_in, ("dp", "seq"), axis=0, tiled=True),
            lax.all_gather(w_dt, ("dp", "seq"), axis=0, tiled=True),
        ),
    )
    conv_input = conv_acc.astype(jnp.bfloat16)
    dt_raw = dt_acc * head_mask
    previous = passed_along(conv_input[tokens - (CONV - 1) :], "seq", 1)
    padded = jnp.concatenate([previous, conv_input], axis=0).astype(jnp.float32)
    conv_float = conv_weight.astype(jnp.float32)
    pre_act = jnp.zeros((tokens, CHANNELS), jnp.float32)
    for offset in range(CONV):
        pre_act = pre_act + conv_float[offset] * padded[offset : offset + tokens]
    activated = lax.optimization_barrier(jax.nn.silu(pre_act).astype(jnp.bfloat16)).astype(
        jnp.float32
    )
    outputs, final_state, running, values, reads_c = block_pass(activated, dt_raw, dt_bias, a_log)
    decay_total = jnp.exp(running[-1])
    identity = (jnp.ones_like(decay_total), jnp.zeros_like(final_state))
    entry_state = prefix((decay_total, final_state), "seq", join_states, identity)[1]
    carried = jnp.exp(running)[:, :, None] * jnp.einsum(
        "hpn,tn->thp", entry_state, reads_c, precision=highest
    )
    y_ssd = (outputs + carried + skip_gain[:, None] * values).reshape(tokens, INNER)
    gate_act = jax.nn.silu(z_gate)
    gated = y_ssd * gate_act
    inverse_gate = lax.rsqrt(jnp.sum(gated * gated, axis=1, keepdims=True) / units_float + epsilon)
    normalized = gated * inverse_gate
    empty_out = jnp.zeros((tokens, D), jnp.float32)
    first_row = jnp.int32(0)
    gain_piece = lax.all_gather(gate_gain, ("dp", "seq"), axis=0, tiled=True)
    out_piece = lax.all_gather(w_out, ("dp", "seq"), axis=0, tiled=True)
    row_count = gain_piece.shape[0]

    def apply_rows(current):
        columns = lax.dynamic_slice_in_dim(normalized, first_row, row_count, 1)
        rounded = (columns * gain_piece.astype(jnp.float32)).astype(jnp.bfloat16)
        return current + bf_dot(rounded, out_piece)

    branch_out = lax.cond(first_row < used_units, apply_rows, lambda current: current, empty_out)
    hidden_out = (x_in + branch_out).astype(jnp.bfloat16)[None]
    cotangent = grad_out[0]
    cot_float = cotangent.astype(jnp.float32)
    pull_gain_piece = lax.all_gather(gate_gain, ("dp", "seq"), axis=0, tiled=True)
    pull_out_piece = lax.all_gather(w_out, ("dp", "seq"), axis=0, tiled=True)
    pull_row_count = pull_gain_piece.shape[0]
    gain_full = pull_gain_piece.astype(jnp.float32)
    slab_grad = lax.cond(
        jnp.int32(0) < used_units,
        lambda rows_piece: cross_dot(cotangent, rows_piece),
        lambda rows_piece: jnp.zeros((tokens, pull_row_count), jnp.float32),
        pull_out_piece,
    )
    d_rounded = slab_grad
    gate_full, d_rounded = (gain_full, d_rounded)
    rounded_out = (normalized * gate_full).astype(jnp.bfloat16)
    summed_w_out = lax.psum_scatter(
        outer_dot(
            lax.slice_in_dim(rounded_out, 0, w_out.shape[0] * lax.axis_size(("dp", "seq")), axis=1),
            cotangent,
        ),
        ("dp", "seq"),
        scatter_dimension=0,
        tiled=True,
    )
    grad_gate_local = jnp.sum(d_rounded * normalized, axis=0)
    d_normal = d_rounded * gate_full
    d_gated = (
        inverse_gate * d_normal
        - gated * inverse_gate**3 * jnp.sum(d_normal * gated, axis=1, keepdims=True) / units_float
    )
    d_ssd = d_gated * gate_act
    d_gate = (d_gated * y_ssd * silu_slope(z_gate)).astype(jnp.bfloat16)
    d_three = d_ssd.reshape(tokens, HEADS, HEAD_DIM)
    direct = jnp.einsum("th,thp,tn->hpn", jnp.exp(running), d_three, reads_c, precision=highest)
    back_identity = (jnp.ones_like(decay_total), jnp.zeros_like(direct))
    leave_grad = carried_in((decay_total, direct), "seq", join_states, back_identity)[1]
    unused_out, pullback = jax.vjp(
        local_ssd, activated, dt_raw, dt_bias, a_log, skip_gain, entry_state
    )
    d_act, d_dt_full, d_bias, d_log, d_skip, unused_entry = pullback((d_ssd, leave_grad))
    d_pre = d_act * silu_slope(pre_act)
    grad_conv_local = jnp.stack(
        [jnp.sum(d_pre * padded[offset : offset + tokens], axis=0) for offset in range(CONV)]
    )
    d_padded = jnp.zeros((tokens + CONV - 1, CHANNELS), jnp.float32)
    for offset in range(CONV):
        d_padded = d_padded.at[offset : offset + tokens].add(conv_float[offset] * d_pre)
    returned = passed_along(d_padded[: CONV - 1].astype(jnp.bfloat16), "seq", -1).astype(
        jnp.float32
    )
    d_conv_in = d_padded[CONV - 1 :].at[tokens - (CONV - 1) :].add(returned).astype(jnp.bfloat16)
    d_dt_round = (d_dt_full * head_mask).astype(jnp.bfloat16)

    def push_rows(partial_sums, pieces, first_row):
        gain_rows, d_normed = partial_sums
        gain_piece, in_piece, dt_piece = pieces
        gain_rows = gain_piece.astype(jnp.float32)

        def narrow(span_width):

            def narrow_apply_width(weight_rows):
                return cross_dot(d_gate[:, :span_width], weight_rows[:, :span_width]) + cross_dot(
                    d_conv_in[:, :span_width], weight_rows[:, INNER : INNER + span_width]
                )

            return narrow_apply_width

        slab_grad = lax.switch(
            width_level, [narrow(span_width) for span_width in prefix_spans], in_piece
        )
        slab_grad = (
            slab_grad
            + cross_dot(d_conv_in[:, INNER:], in_piece[:, 2 * INNER :])
            + cross_dot(d_dt_round, dt_piece)
        )
        d_normed = lax.dynamic_update_slice_in_dim(d_normed, slab_grad, first_row, 1)
        return (gain_rows, d_normed)

    empty_push = (jnp.zeros((D,), jnp.float32), jnp.zeros((tokens, D), jnp.float32))
    gain_rows, d_normed = push_rows(
        empty_push,
        (
            lax.all_gather(norm_gain, ("dp", "seq"), axis=0, tiled=True),
            lax.all_gather(w_in, ("dp", "seq"), axis=0, tiled=True),
            lax.all_gather(w_dt, ("dp", "seq"), axis=0, tiled=True),
        ),
        jnp.int32(0),
    )
    normed_full = (scaled * gain_rows).astype(jnp.bfloat16)
    d_project_all = jnp.concatenate([d_gate, d_conv_in, d_dt_round], axis=1)
    summed_in = lax.psum_scatter(
        outer_dot(normed_full, d_project_all), ("dp", "seq"), scatter_dimension=0, tiled=True
    )
    grad_norm_local = jnp.sum(d_normed * scaled, axis=0)
    d_scaled = d_normed * gain_rows
    d_input = inverse_rms * d_scaled - x_in * inverse_rms**3 * jnp.mean(
        d_scaled * x_in, axis=1, keepdims=True
    )
    grad_in = (cot_float + d_input).astype(jnp.bfloat16)[None]
    summed_small = lax.psum(
        (grad_conv_local, d_bias, d_log, d_skip, grad_norm_local, grad_gate_local), ("dp", "seq")
    )
    shard_number = lax.axis_index(("dp", "seq"))
    norm_rows = norm_gain.shape[0]
    gate_rows = gate_gain.shape[0]
    grad_norm_gain = lax.dynamic_slice_in_dim(
        summed_small[4], shard_number * norm_rows, norm_rows, 0
    )
    grad_gate_gain = lax.dynamic_slice_in_dim(
        summed_small[5], shard_number * gate_rows, gate_rows, 0
    )
    proj_columns = w_in.shape[1]
    return (
        hidden_out,
        grad_in,
        grad_norm_gain,
        summed_in[:, :proj_columns],
        summed_in[:, proj_columns:],
        summed_small[0],
        summed_small[1],
        summed_small[2],
        summed_small[3],
        grad_gate_gain,
        summed_w_out,
    )


def solution(mesh):
    return jax.shard_map(
        per_device,
        mesh=mesh,
        in_specs=(
            P("dp", "seq", None),
            P("dp"),
            P(("dp", "seq")),
            P(("dp", "seq"), None),
            P(("dp", "seq"), None),
            P(),
            P(),
            P(),
            P(),
            P(("dp", "seq")),
            P(("dp", "seq"), None),
            P("dp", "seq", None),
        ),
        out_specs=(
            P("dp", "seq", None),
            P("dp", "seq", None),
            P(("dp", "seq")),
            P(("dp", "seq"), None),
            P(("dp", "seq"), None),
            P(),
            P(),
            P(),
            P(),
            P(("dp", "seq")),
            P(("dp", "seq"), None),
        ),
        check_vma=False,
    )
```

profile of v0, /device:TPU:8, one launch (start us, length us, event | category | flops | bytes accessed | tf_op | source)
XLA Modules:
  0.0 2482.6 jit_solution(9580807050974811758)
XLA Ops:
  10.2 42.7 %all-reduce.14 = bf16[2048]{0:T(1024)(128)(2,1)S(1)} all-reduce(bf16[2048]{0:T(1024)(128)(2,1)S(1)} %dynamic-update-slice.41), channel_id=1, replica_groups=mesh['dp'=8,'seq'=4] {'dp','seq'}, use_global_device_ids=true, to_apply=%add.14 | all-reduce | flops 2048 | bytes 8192
  53.8 37.9 %all_gather.40 = bf16[2048,64]{1,0:T(8,128)(2,1)S(1)} all-gather(bf16[64,64]{1,0:T(8,128)(2,1)} %param.68), channel_id=1, replica_groups=mesh['dp'=8,'seq'=4] {'dp','seq'}, dimensions={0}, use_global_device_ids=true | all-gather | bytes 270336 | tf_op jit(solution)/shard_map/all_gather | solution.py:208
  99.7 114.5 %all-gather.9.cloned.1.call-done = bf16[2048,8448]{1,0:T(8,128)(2,1)} async-done(((bf16[64,8448]{1,0:T(8,128)(2,1)}), bf16[2048,8448]{1,0:T(8,128)(2,1)}) %all-gather.9.cloned.1.call-update) | async-done | bytes 34603024 | tf_op jit(solution)/shard_map/all_gather | solution.py:207
  214.2 20.1 conditional.4
  289.4 250.3 %while.94 = (s32[]{:T(128)}, f32[64,64,128]{2,1,0:T(8,128)S(1)}, f32[2,256,64,64]{1,0,3,2:T(2,128)}, f32[2,256,64]{1,2,0:T(8,128)S(1)}, f32[2,256,64]{1,2,0:T(8,...) while((s32[]{:T(128)}, f32[64,64,128]{2,1,0:T(8,128)S(1)}, ...), condition=%wide.region_15.16_spmd.clone, body=%wide.region_12.15_spmd.clone.sunk | while | flops 6571540480 | bytes 48374480 | solution.py:128
  293.0 20.9 fusion.339
  330.4 84.4 %dynamic_update_slice.74 = f32[2,256,64,64]{1,0,3,2:T(2,128)} dynamic-update-slice(f32[2,256,64,64]{1,0,3,2:T(2,128)} %get-tuple-element.1553, f32[1,256,64,64]{1,0,3,2:T(1,128)} %copy.420, s32[]{:T(128)S(6)} %copy.450, s32[]{:T(128)} %constant.611.clone.1..sunk.3, s32[]{:T(128)} %constant.611.clone.1..sunk.3, s32[]{:T(128)} %constant.611.clone.1..sunk.3) | dynamic-update-slice | bytes 8388612 | tf_op jit(solution)/shard_map/while/body/jit(dynamic_update_index_in_dim)/dynamic_update_slice | solution.py:128
  418.0 20.9 fusion.339
  455.1 84.4 %dynamic_update_slice.74 = f32[2,256,64,64]{1,0,3,2:T(2,128)} dynamic-update-slice(f32[2,256,64,64]{1,0,3,2:T(2,128)} %get-tuple-element.1553, f32[1,256,64,64]{1,0,3,2:T(1,128)} %copy.420, s32[]{:T(128)S(6)} %copy.450, s32[]{:T(128)} %constant.611.clone.1..sunk.3, s32[]{:T(128)} %constant.611.clone.1..sunk.3, s32[]{:T(128)} %constant.611.clone.1..sunk.3) | dynamic-update-slice | bytes 8388612 | tf_op jit(solution)/shard_map/while/body/jit(dynamic_update_index_in_dim)/dynamic_update_slice | solution.py:128
  548.7 53.3 %all-gather.2 = bf16[32,1,128]{2,1,0:T(2,128)(2,1)S(1)} all-gather(bf16[1,1,128]{2,1,0:T(2,128)(2,1)S(1)} %bitcast.537), channel_id=1, replica_groups=mesh['dp'=8,'seq'=4] {'dp','seq'}, dimensions={0}, use_global_device_ids=true | all-gather | bytes 8448 | tf_op jit(solution)/shard_map/all_gather | solution.py:236
  670.0 17.3 multiply_reduce_fusion.9
  775.6 249.6 %while.93 = (s32[]{:T(128)}, f32[64,64,128]{2,1,0:T(8,128)S(1)}, f32[2,256,64,64]{1,3,2,0:T(8,128)}, f32[2,256,128]{2,1,0:T(8,128)}, f32[2,256,128]{2,1,0:T(8,12...) while((s32[]{:T(128)}, f32[64,64,128]{2,1,0:T(8,128)S(1)}, ...), condition=%wide.region_44.45_spmd, body=%wide.region_32.44_spmd.sunk | while | flops 14897364992 | bytes 132263192 | solution.py:128
  820.0 28.1 %fusion.324 = (f32[256,64]{0,1:T(8,128)S(1)}, f32[256,64]{0,1:T(8,128)S(1)}, f32[256,64]{0,1:T(8,128)S(1)}, f32[256,256]{1,0:T(8,128)S(1)}) fusion(f32[256,64]{0,1:T(8,128)S(1)} %copy.405, f32[256,256]{1,0:T(8,128)S(1)} %fusion.323, f32[256,64]{0,1:T(8,128)S(1)} %copy.407, pred[256,256]{1,0:T(8,128)(4,1)} %iota_compare_fusion.4, ...), kind=kOutput, calls=%fused_computation.140.clone.1 | convolution fusion | flops 3284025344 | bytes 9306112 | tf_op jit(solution)/shard_map/transpose(jvp())/while/body/eval_jaxpr/checkpoint/tsh,shp->thp/dot_general | solution.py:101
  889.4 17.2 bitcast_dynamic-update-slice_fusion.6
  931.1 28.1 %fusion.324 = (f32[256,64]{0,1:T(8,128)S(1)}, f32[256,64]{0,1:T(8,128)S(1)}, f32[256,64]{0,1:T(8,128)S(1)}, f32[256,256]{1,0:T(8,128)S(1)}) fusion(f32[256,64]{0,1:T(8,128)S(1)} %copy.405, f32[256,256]{1,0:T(8,128)S(1)} %fusion.323, f32[256,64]{0,1:T(8,128)S(1)} %copy.407, pred[256,256]{1,0:T(8,128)(4,1)} %iota_compare_fusion.4, ...), kind=kOutput, calls=%fused_computation.140.clone.1 | convolution fusion | flops 3284025344 | bytes 9306112 | tf_op jit(solution)/shard_map/transpose(jvp())/while/body/eval_jaxpr/checkpoint/tsh,shp->thp/dot_general | solution.py:101
  1083.9 19.4 multiply_reduce_fusion.7
  1128.8 22.7 scatter-add.52
  1162.2 22.7 scatter-add.53
  1215.3 30.5 %fusion.163 = f32[2048,8512]{1,0:T(8,128)} fusion(bf16[512,2048]{1,0:T(8,128)(2,1)S(1)} %copy-done.14, bf16[512,64]{1,0:T(8,128)(2,1)S(1)} %copy.293, bf16[512,4352]{1,0:T(8,128)(2,1)} %convert_element_type.150, bf16[512,4096]{1,0:T(8,128)(2,1)} %get-tuple-element.1213), kind=kOutput, calls=%fused_computation.212 | convolution fusion | flops 17877106688 | bytes 80543744 | tf_op jit(solution)/shard_map/dot_general | solution.py:82
  1247.4 19.8 fusion.180
  1304.8 71.2 %all-reduce.15 = (f32[2048]{0:T(1024)S(1)}, f32[64]{0:T(128)}, f32[64]{0:T(128)}, f32[64]{0:T(128)}, f32[4096]{0:T(1024)S(1)}) all-reduce(f32[2048]{0:T(1024)S(1)} %get-tuple-element.1097, f32[64]{0:T(128)S(1)} %copy-done.74, f32[64]{0:T(128)S(1)} %negate_multiply_fusion, ...), channel_id=1, replica_groups=mesh['dp'=8,'seq'=4] {'dp','seq'}, use_global_device_ids=true, to_apply=%region_55.56 | all-reduce | flops 6336 | bytes 50688 | tf_op jit(solution)/shard_map/psum | solution.py:346
  1383.5 602.3 %reduce-scatter.3.cloned.1.call-done = f32[64,8512]{1,0:T(8,128)} async-done(((f32[2048,8512]{1,0:T(8,128)}), f32[64,8512]{1,0:T(8,128)}) %reduce-scatter.3.cloned.1.call-update) | async-done | bytes 2179088 | tf_op jit(solution)/shard_map/reduce_scatter | solution.py:337
  1990.2 127.5 %all-reduce.18.cloned.1.call-done = f32[4,4352]{1,0:T(4,128)} async-done(((f32[4,4352]{1,0:T(4,128)}), f32[4,4352]{1,0:T(4,128)}) %all-reduce.18.cloned.1.call-update) | async-done | bytes 69648 | tf_op jit(solution)/shard_map/psum | solution.py:346
  2117.7 356.2 %reduce-scatter.5.cloned.1.call-done = f32[128,2048]{1,0:T(8,128)} async-done(((f32[4096,2048]{1,0:T(8,128)}), f32[128,2048]{1,0:T(8,128)}) %reduce-scatter.5.cloned.1.call-update) | async-done | bytes 1048592 | tf_op jit(solution)/shard_map/reduce_scatter | solution.py:262
  (469 shorter events, 672.0 us)
Async XLA Ops:
  7.2 87.9 %copy-start.6 = (bf16[1,512,2048]{2,1,0:T(8,128)(2,1)S(1)}, bf16[1,512,2048]{2,1,0:T(8,128)(2,1)}, u32[]{:S(2)}) copy-start(bf16[1,512,2048]{2,1,0:T(8,128)(2,1)} %param.64) | copy-start | bytes 6291460
  7.2 89.8 %copy-start.75 = (f32[64]{0:T(128)S(1)}, f32[64]{0:T(128)}, u32[]{:S(2)}) copy-start(f32[64]{0:T(128)} %param.70) | copy-start | bytes 772
  7.2 207.0 %all-gather.9.cloned.1.call-start = ((), (), s32[]{:S(2)}) async-start(), calls=%async_computation.2 | async-start | bytes 35684352 | tf_op jit(solution)/shard_map/all_gather | solution.py:207
  7.9 594.3 %all-gather.11.cloned.1.call-start = ((), (), s32[]{:S(2)}) async-start(), calls=%async_computation.3 | async-start | bytes 17301504 | tf_op jit(solution)/shard_map/all_gather | solution.py:237
  8.7 626.9 %all-gather.13.cloned.1.call-start = ((), (), s32[]{:S(2)}) async-start(), calls=%async_computation.7 | async-start | bytes 5242880 | tf_op jit(solution)/shard_map/all_gather | solution.py:29
  53.0 45.4 %copy-start.55 = (f32[2048]{0:T(1024)}, f32[2048]{0:T(1024)S(1)}, u32[]{:S(2)}) copy-start(f32[2048]{0:T(1024)S(1)} %convert_element_type.133) | copy-start | bytes 24580
  53.8 44.6 %copy-start.71 = (f32[64]{0:T(128)}, f32[64]{0:T(128)S(1)}, u32[]{:S(2)}) copy-start(f32[64]{0:T(128)S(1)} %compare_convert_fusion) | copy-start | bytes 772
  95.1 119.1 %copy-start.62 = (f32[512]{0:T(512)}, f32[512]{0:T(512)S(1)}, u32[]{:S(2)}) copy-start(f32[512]{0:T(512)S(1)} %get-tuple-element.1224) | copy-start | bytes 6148
  238.5 3.0 collective-permute-start
  289.3 251.6 %copy-start.68 = (f32[64]{0:T(128)S(1)}, f32[64]{0:T(128)}, u32[]{:S(2)}) copy-start(f32[64]{0:T(128)} %copy-done.67) | copy-start | bytes 772
  330.4 84.4 %copy-start.11 = (f32[2,256,128]{2,1,0:T(8,128)S(1)}, f32[2,256,128]{2,1,0:T(8,128)}, u32[]{:S(2)}) copy-start(f32[2,256,128]{2,1,0:T(8,128)} %copy-done.10) | copy-start | bytes 786436 | tf_op jit(solution)/shard_map/while
  455.1 84.4 %copy-start.11 = (f32[2,256,128]{2,1,0:T(8,128)S(1)}, f32[2,256,128]{2,1,0:T(8,128)}, u32[]{:S(2)}) copy-start(f32[2,256,128]{2,1,0:T(8,128)} %copy-done.10) | copy-start | bytes 786436 | tf_op jit(solution)/shard_map/while
  539.6 62.6 %copy-start.12 = (f32[2,256,128]{2,1,0:T(8,128)}, f32[2,256,128]{2,1,0:T(8,128)S(1)}, u32[]{:S(2)}) copy-start(f32[2,256,128]{2,1,0:T(8,128)S(1)} %get-tuple-element.1732) | copy-start | bytes 786436
  540.9 219.4 %all-gather.15.cloned.1.call-start = ((), (), s32[]{:S(2)}) async-start(), calls=%async_computation.8 | async-start | bytes 5242880 | tf_op jit(solution)/shard_map/all_gather | solution.py:51
  543.1 59.1 %copy-start.26 = (f32[64,4,128]{2,0,1:T(8,128)}, f32[64,4,128]{2,0,1:T(8,128)S(1)}, u32[]{:S(2)}) copy-start(f32[64,4,128]{2,0,1:T(8,128)S(1)} %reduce-window.84) | copy-start | bytes 393220
  543.4 58.9 %copy-start.64 = (f32[64,4]{0,1:T(4,128)}, f32[64,4]{0,1:T(4,128)S(1)}, u32[]{:S(2)}) copy-start(f32[64,4]{0,1:T(4,128)S(1)} %slice.478) | copy-start | bytes 3076
  543.5 58.8 %copy-start.44 = (f32[512,64]{0,1:T(8,128)}, f32[512,64]{0,1:T(8,128)S(1)}, u32[]{:S(2)}) copy-start(f32[512,64]{0,1:T(8,128)S(1)} %bitcast_bitcast_fusion.4) | copy-start | bytes 393220
  602.1 65.2 %copy-start.53 = (f32[4096]{0:T(1024)}, f32[4096]{0:T(1024)S(1)}, u32[]{:S(2)}) copy-start(f32[4096]{0:T(1024)S(1)} %bitcast_convert_fusion.2) | copy-start | bytes 49156
  602.2 94.2 %copy-start.28 = (f32[512,64]{0,1:T(8,128)}, f32[512,64]{0,1:T(8,128)S(1)}, u32[]{:S(2)}) copy-start(f32[512,64]{0,1:T(8,128)S(1)} %fusion.225) | copy-start | bytes 393220
  704.9 1280.8 %reduce-scatter.3.cloned.1.call-start = ((), (), s32[]{:S(2)}) async-start(), calls=%async_computation.4 | async-start | bytes 72450048 | tf_op jit(solution)/shard_map/reduce_scatter | solution.py:337
  1203.1 3.1 collective-permute-start.1
  1245.8 871.9 %all-reduce.18.cloned.1.call-start = ((), (), s32[]{:S(2)}) async-start(), calls=%async_computation.5 | async-start | bytes 139264 | tf_op jit(solution)/shard_map/psum | solution.py:346
  1246.7 1227.3 %reduce-scatter.5.cloned.1.call-start = ((), (), s32[]{:S(2)}) async-start(), calls=%async_computation.6 | async-start | bytes 34603008 | tf_op jit(solution)/shard_map/reduce_scatter | solution.py:262
  1298.9 78.2 %copy-start.66 = (f32[512]{0:T(512)S(1)}, f32[512]{0:T(512)}, u32[]{:S(2)}) copy-start(f32[512]{0:T(512)} %get-tuple-element.1223) | copy-start | bytes 6148
  (75 other events, 770.6 us)
Sparse Core Ops, SparseCore 0:
  10.9 203.1 all-gather.8
  217.0 113.8 all-gather.10
  541.0 54.3 all-gather.12
  705.1 41.1 all-gather.14
  1245.9 739.7 reduce-scatter.2
  1992.7 124.9 all-reduce.17
  2120.7 353.2 reduce-scatter.4
where the time goes:
time: 2510 us; the launch traced here: 2480 us
  waiting for transfers between devices  1200 us (48%)
  local copies, waits for them, and re-layouts  440 us (18%)
  matrix products  387 us (15%)
  blocking collectives  210 us (8%)
  other arithmetic  185 us (7%)
  loops' own time  38 us (2%)
    reduce_scatter x1, waiting for transfers between devices, per_device(): lax.psum_scatter(outer_dot(normed_full, d_project_all), ('dp', 'seq'), sc...  602 us
    reduce_scatter x1, waiting for transfers between devices, per_device(): lax.psum_scatter(outer_dot(lax.slice_in_dim(rounded_out, 0, w_out.shape[0...  356 us
    dynamic_update_slice x8, local copies, waits for them, and re-layouts, block_pass(): lax.scan(jax.checkpoint(block_step), start_state, inputs)  186 us
    dot_general x6, matrix products, block_step(): output = jnp.einsum('tsh,shp->thp', mixing, values, precision=highest)  132 us
    psum x1, waiting for transfers between devices, per_device(): lax.psum((grad_conv_local, d_bias, d_log, d_skip, grad_norm_local, grad_g...  128 us
    all_gather x1, waiting for transfers between devices, per_device(): lax.all_gather(w_in, ('dp', 'seq'), axis=0, tiled=True)  114 us
    psum x1, blocking collectives, per_device(): lax.psum((grad_conv_local, d_bias, d_log, d_skip, grad_norm_local, grad_g...  71.2 us
    all_gather x1, blocking collectives, per_device(): gain_piece = lax.all_gather(gate_gain, ('dp', 'seq'), axis=0, tiled=True)  53.3 us
  transfers between devices with their start and end apart: 9, of which 6 were waited for; matrix products, arithmetic and copies ran while one was open for 19% of the time, Pallas kernels for 0%

commit v1 on v0

v1 whole, which is shorter than its diff:
```python
import functools

import jax
import jax.numpy as jnp
from jax import lax
from jax.experimental import pallas as pl
from jax.experimental.pallas import tpu as pltpu
from jax.sharding import PartitionSpec as P

D = 2048
INNER = 4096
HEAD_DIM = 64
STATE = 128
CONV = 4
HEADS = 64
CHANNELS = 4352

PART = 4
LANES = 128
STRIPS = INNER // LANES // PART
OWN = STRIPS * LANES
OWN_HEADS = OWN // HEAD_DIM
OWN_BC = 2 * STATE // PART
CONV_COLS = OWN + LANES
Q = 256
HALF = Q // 2

epsilon = 1e-05
highest = lax.Precision.HIGHEST
f32 = jnp.float32
bf16 = jnp.bfloat16
LOG2E = 1.4426950408889634


def swap(value, axis, pairs):
    return lax.ppermute(value, axis, pairs)


def xor_seq(value, bits):
    return lax.ppermute(value, "seq", [(s, s ^ bits) for s in range(PART)])


def seq_gather(block):
    me = lax.axis_index("seq")
    sibling = xor_seq(block, 1)
    across = xor_seq(block, 2)
    corner = xor_seq(across, 1)
    out = jnp.zeros((PART,) + block.shape, block.dtype)
    for bits, piece in ((0, block), (1, sibling), (2, across), (3, corner)):
        out = lax.dynamic_update_index_in_dim(out, piece, me ^ bits, 0)
    return out


def seq_scatter(blocks):
    me = lax.axis_index("seq")
    core, row = me % 2, me // 2
    view = blocks.reshape((2, 2) + blocks.shape[1:])
    mine = lax.dynamic_index_in_dim(view, core, 1, False)
    other = lax.dynamic_index_in_dim(view, 1 - core, 1, False)
    half = mine.astype(f32) + xor_seq(other, 1).astype(f32)
    keep = lax.dynamic_index_in_dim(half, row, 0, False)
    give = lax.dynamic_index_in_dim(half, 1 - row, 0, False).astype(bf16)
    return keep + xor_seq(give, 2).astype(f32)


def seq_transpose(pieces):
    me = lax.axis_index("seq")
    out = jnp.zeros_like(pieces)
    for bits in range(PART):
        piece = lax.dynamic_index_in_dim(pieces, me ^ bits, 0, False)
        if bits:
            piece = xor_seq(piece, bits)
        out = lax.dynamic_update_index_in_dim(out, piece, me ^ bits, 0)
    return out


def seq_total(value):
    value = value + xor_seq(value, 1)
    return value + xor_seq(value, 2)


def fast_mesh():
    return lax.axis_size("dp") == 8


def dp_shift_z(value, steps):
    pairs = [(z * 2 + x, (z + steps) % 4 * 2 + x) for z in range(4) for x in range(2)]
    return lax.ppermute(value, "dp", pairs)


def dp_swap_x(value):
    return lax.ppermute(value, "dp", [(d, d ^ 1) for d in range(8)])


def dp_gather(block):
    me = lax.axis_index("dp")
    z, x = me // 2, me % 2
    out = jnp.zeros((8,) + block.shape, block.dtype)
    for steps in range(4):
        piece = dp_shift_z(block, steps) if steps else block
        source = (z - steps + 4) % 4
        out = lax.dynamic_update_index_in_dim(out, piece, source * 2 + x, 0)
        out = lax.dynamic_update_index_in_dim(out, dp_swap_x(piece), source * 2 + 1 - x, 0)
    return out


def dp_scatter(blocks):
    me = lax.axis_index("dp")
    z, x = me // 2, me % 2
    view = blocks.reshape((4, 2) + blocks.shape[1:])
    mine = lax.dynamic_index_in_dim(view, x, 1, False)
    other = lax.dynamic_index_in_dim(view, 1 - x, 1, False)
    half = mine.astype(f32) + dp_swap_x(other).astype(f32)
    total = lax.dynamic_index_in_dim(half, z, 0, False)
    for steps in range(1, 4):
        give = lax.dynamic_index_in_dim(half, (z + steps) % 4, 0, False).astype(bf16)
        total = total + dp_shift_z(give, steps).astype(f32)
    return total


def dp_total(value):
    if not fast_mesh():
        return lax.psum(value, "dp")
    value = value + dp_swap_x(value)
    return value + dp_shift_z(value, 1) + dp_shift_z(value, 2) + dp_shift_z(value, 3)


def by_owner(columns):
    rows = columns.shape[0]
    return (
        columns.reshape(rows, STRIPS, PART, LANES).transpose(2, 0, 1, 3).reshape(PART, rows, OWN)
    )


def from_owner(pieces):
    rows = pieces.shape[1]
    return (
        pieces.reshape(PART, rows, STRIPS, LANES).transpose(1, 2, 0, 3).reshape(rows, INNER)
    )


def heads_by_owner(columns):
    rows = columns.shape[0]
    return (
        columns.reshape(rows, STRIPS, PART, 2).transpose(2, 0, 1, 3).reshape(PART, rows, OWN_HEADS)
    )


def heads_from_owner(pieces):
    rows = pieces.shape[1]
    return (
        pieces.reshape(PART, rows, STRIPS, 2).transpose(1, 2, 0, 3).reshape(rows, HEADS)
    )


def gather_in(pieces):
    if fast_mesh():
        own = seq_transpose(pieces)
        block = own.reshape(-1, own.shape[2])
        return dp_gather(block).reshape(D, -1)
    full = lax.all_gather(pieces, ("dp", "seq"), axis=1, tiled=True)
    return lax.dynamic_index_in_dim(full, lax.axis_index("seq"), 0, False)


def scatter_in(grads):
    columns = grads.shape[1]
    if fast_mesh():
        total = dp_scatter(grads.reshape(8, -1, columns))
        return seq_transpose(total.reshape(PART, -1, columns).astype(bf16)).astype(f32)
    full = jnp.zeros((PART,) + grads.shape, grads.dtype)
    full = lax.dynamic_update_index_in_dim(full, grads, lax.axis_index("seq"), 0)
    return lax.psum_scatter(full, ("dp", "seq"), scatter_dimension=1, tiled=True).astype(f32)


def gather_out(rows):
    if fast_mesh():
        return dp_gather(rows).reshape(OWN, -1)
    full = lax.all_gather(rows, ("dp", "seq"), axis=0, tiled=True)
    full = full.reshape(STRIPS, PART, LANES, -1)
    return lax.dynamic_index_in_dim(full, lax.axis_index("seq"), 1, False).reshape(OWN, -1)


def scatter_out(grads):
    if fast_mesh():
        return dp_scatter(grads.reshape(8, LANES, -1))
    full = jnp.zeros((STRIPS, PART, LANES, grads.shape[1]), grads.dtype)
    full = lax.dynamic_update_index_in_dim(
        full, grads.reshape(STRIPS, LANES, -1), lax.axis_index("seq"), 1
    )
    full = full.reshape(INNER, -1)
    return lax.psum_scatter(full, ("dp", "seq"), scatter_dimension=0, tiled=True).astype(f32)


def dot_nn(a, b):
    return lax.dot_general(a, b, (((1,), (0,)), ((), ())), preferred_element_type=f32)


def dot_nt(a, b):
    return lax.dot_general(a, b, (((1,), (1,)), ((), ())), preferred_element_type=f32)


def dot_tn(a, b):
    return lax.dot_general(a, b, (((0,), (0,)), ((), ())), preferred_element_type=f32)


def dot_exact(a, b):
    return lax.dot_general(
        a, b, (((1,), (0,)), ((), ())), precision=highest, preferred_element_type=f32
    )


def sigmoid(v):
    return 0.5 + 0.5 * jnp.tanh(0.5 * v)


def decay_terms(dt_ref, rows_ref):
    v = dt_ref[...] * rows_ref[2:3, :] + rows_ref[0:1, :]
    steps = jnp.maximum(v, 0.0) + jnp.log1p(jnp.exp(-jnp.abs(v)))
    log2_decay = rows_ref[1:2, :] * LOG2E * steps
    row = lax.broadcasted_iota(jnp.int32, (Q, Q), 0)
    column = lax.broadcasted_iota(jnp.int32, (Q, Q), 1)
    lower = jnp.where(row >= column, 1.0, 0.0)
    running = dot_exact(lower, log2_decay)
    shifted = running - jnp.log(steps) * LOG2E
    end = running[Q - 1 : Q, :]
    return v, steps, running, shifted, end


def forward_kernel(
    ci_ref, bc_ref, dt_ref, cw_ref, rows_ref, skip_ref, y_ref, act_ref, s_ref, state, xf
):
    @pl.when(pl.program_id(0) == 0)
    def _():
        state[...] = jnp.zeros_like(state)
        xf[0:8, :] = jnp.zeros((8, OWN), f32)

    @pl.when(pl.program_id(0) > 0)
    def _():
        xf[0:8, :] = xf[Q : Q + 8, :]

    xf[8 : Q + 8, :] = ci_ref[...].astype(f32)
    _, _, running, shifted, end = decay_terms(dt_ref, rows_ref)
    shifted_t = shifted.T
    e_run = jnp.exp2(running)
    w_end = jnp.exp2(end - shifted)
    e_end = jnp.exp2(end)
    keys = bc_ref[:, :STATE]
    reads = bc_ref[:, STATE:]
    keys_t = keys.T
    cb = dot_nt(reads, keys)
    causal = lax.broadcasted_iota(jnp.int32, (HALF, HALF), 0) >= lax.broadcasted_iota(
        jnp.int32, (HALF, HALF), 1
    )
    left = lax.broadcasted_iota(jnp.int32, (1, LANES), 1) < HEAD_DIM
    s_ref[0] = state[...].astype(bf16)
    for strip in range(STRIPS):
        at = slice(strip * LANES, (strip + 1) * LANES)
        h0, h1 = 2 * strip, 2 * strip + 1
        pre = cw_ref[0:1, at] * xf[5 : 5 + Q, at]
        for tap in range(1, CONV):
            pre = pre + cw_ref[tap : tap + 1, at] * xf[5 + tap : 5 + tap + Q, at]
        act = (pre * sigmoid(pre)).astype(bf16)
        act_ref[:, at] = act
        actf = act.astype(f32)
        inter = dot_nn(reads, s_ref[0, :, at]) * jnp.where(
            left, e_run[:, h0 : h0 + 1], e_run[:, h1 : h1 + 1]
        )
        inter = inter + skip_ref[0:1, at] * actf
        top, bottom = inter[:HALF], inter[HALF:]
        for h, side in ((h0, left), (h1, jnp.logical_not(left))):
            x_h = jnp.where(side, actf, 0.0).astype(bf16)
            m00 = jnp.where(
                causal,
                jnp.exp2(running[:HALF, h : h + 1] - shifted_t[h : h + 1, :HALF]) * cb[:HALF, :HALF],
                0.0,
            )
            m10 = jnp.exp2(running[HALF:, h : h + 1] - shifted_t[h : h + 1, :HALF]) * cb[HALF:, :HALF]
            m11 = jnp.where(
                causal,
                jnp.exp2(running[HALF:, h : h + 1] - shifted_t[h : h + 1, HALF:]) * cb[HALF:, HALF:],
                0.0,
            )
            top = top + dot_nn(m00.astype(bf16), x_h[:HALF])
            bottom = bottom + dot_nn(
                jnp.concatenate([m10.astype(bf16), m11.astype(bf16)], axis=1), x_h
            )
        y_ref[:HALF, at] = top
        y_ref[HALF:, at] = bottom
        weighted = (actf * jnp.where(left, w_end[:, h0 : h0 + 1], w_end[:, h1 : h1 + 1])).astype(bf16)
        state[:, at] = state[:, at] * jnp.where(
            left, e_end[:, h0 : h0 + 1], e_end[:, h1 : h1 + 1]
        ) + dot_nn(keys_t, weighted)


def recurrence_forward(conv_in, bc, dt_tile, taps, rows, skip_row):
    length = conv_in.shape[0]
    blocks = length // Q
    whole = lambda i: (0, 0)
    along = lambda i: (i, 0)
    return pl.pallas_call(
        forward_kernel,
        grid=(blocks,),
        in_specs=[
            pl.BlockSpec((Q, OWN), along),
            pl.BlockSpec((Q, 2 * STATE), along),
            pl.BlockSpec((Q, LANES), along),
            pl.BlockSpec((8, OWN), whole),
            pl.BlockSpec((8, LANES), whole),
            pl.BlockSpec((8, OWN), whole),
        ],
        out_specs=[
            pl.BlockSpec((Q, OWN), along),
            pl.BlockSpec((Q, OWN), along),
            pl.BlockSpec((1, STATE, OWN), lambda i: (i, 0, 0)),
        ],
        out_shape=[
            jax.ShapeDtypeStruct((length, OWN), f32),
            jax.ShapeDtypeStruct((length, OWN), bf16),
            jax.ShapeDtypeStruct((blocks, STATE, OWN), bf16),
        ],
        scratch_shapes=[pltpu.VMEM((STATE, OWN), f32), pltpu.VMEM((Q + 8, OWN), f32)],
        compiler_params=pltpu.CompilerParams(
            dimension_semantics=("arbitrary",), vmem_limit_bytes=40 * 2**20
        ),
        cost_estimate=pl.CostEstimate(
            flops=12 * 10**9, bytes_accessed=24 * 2**20, transcendentals=10**7
        ),
        name="recurrence_forward",
    )(conv_in, bc, dt_tile, taps, rows, skip_row)


def backward_kernel(
    ci_ref,
    prev_ref,
    act_ref,
    dy_ref,
    y_ref,
    bc_ref,
    dt_ref,
    s_ref,
    cw_ref,
    rows_ref,
    skip_ref,
    dci_ref,
    dbc_ref,
    ddt_ref,
    gconv_ref,
    grow_ref,
    back,
    back16,
    dp,
    xf,
    edy,
    wx,
    dcb,
    p12h,
    p12l,
    p3,
    p23,
    cross,
):
    step = pl.program_id(0)
    last = pl.num_programs(0) - 1

    @pl.when(step == 0)
    def _():
        back[...] = jnp.zeros_like(back)
        dp[Q : Q + 8, :] = jnp.zeros((8, OWN), f32)
        gconv_ref[...] = jnp.zeros_like(gconv_ref)
        grow_ref[...] = jnp.zeros_like(grow_ref)
        cross[...] = jnp.zeros_like(cross)

    @pl.when(step > 0)
    def _():
        dp[Q : Q + 8, :] = dp[0:8, :]

    before = prev_ref[8:16, :].astype(f32)
    xf[0:8, :] = jnp.where(step == last, 0.0, before)
    xf[8 : Q + 8, :] = ci_ref[...].astype(f32)
    v, steps, running, shifted, end = decay_terms(dt_ref, rows_ref)
    running_t = running.T
    e_run = jnp.exp2(running)
    w_end = jnp.exp2(end - shifted)
    e_end = jnp.exp2(end)
    keys = bc_ref[:, :STATE]
    reads = bc_ref[:, STATE:]
    reads_t = reads.T
    cbt = dot_nt(keys, reads)
    ahead = lax.broadcasted_iota(jnp.int32, (HALF, HALF), 0) <= lax.broadcasted_iota(
        jnp.int32, (HALF, HALF), 1
    )
    left = lax.broadcasted_iota(jnp.int32, (1, LANES), 1) < HEAD_DIM
    back16[...] = back[...].astype(bf16)
    dcb[...] = jnp.zeros_like(dcb)
    for strip in range(STRIPS):
        at = slice(strip * LANES, (strip + 1) * LANES)
        h0, h1 = 2 * strip, 2 * strip + 1
        act = act_ref[:, at]
        dy = dy_ref[:, at]
        actf = act.astype(f32)
        dyf = dy.astype(f32)
        skip = skip_ref[0:1, at]
        w_pair = jnp.where(left, w_end[:, h0 : h0 + 1], w_end[:, h1 : h1 + 1])
        e_pair = jnp.where(left, e_run[:, h0 : h0 + 1], e_run[:, h1 : h1 + 1])
        decayed = (dyf * e_pair).astype(bf16)
        edy[:, at] = decayed
        wx[:, at] = (actf * w_pair).astype(bf16)
        inter = dot_nn(keys, back16[:, at]) * w_pair
        top = jnp.zeros((HALF, LANES), f32)
        bottom = jnp.zeros((HALF, LANES), f32)
        for h, side in ((h0, left), (h1, jnp.logical_not(left))):
            x_h = jnp.where(side, actf, 0.0).astype(bf16)
            dy_h = jnp.where(side, dyf, 0.0).astype(bf16)
            g_top = dot_nt(x_h[:HALF], dy)
            g_bottom = dot_nt(x_h[HALF:], dy[HALF:])
            l00 = jnp.exp2(running_t[h : h + 1, :HALF] - shifted[:HALF, h : h + 1])
            l01 = jnp.exp2(running_t[h : h + 1, HALF:] - shifted[:HALF, h : h + 1])
            l11 = jnp.exp2(running_t[h : h + 1, HALF:] - shifted[HALF:, h : h + 1])
            m00 = jnp.where(ahead, l00 * cbt[:HALF, :HALF], 0.0).astype(bf16)
            m01 = (l01 * cbt[:HALF, HALF:]).astype(bf16)
            m11 = jnp.where(ahead, l11 * cbt[HALF:, HALF:], 0.0).astype(bf16)
            top = top + dot_nn(jnp.concatenate([m00, m01], axis=1), dy_h)
            bottom = bottom + dot_nn(m11, dy_h[HALF:])
            dcb[:HALF, :HALF] += jnp.where(ahead, l00 * g_top[:, :HALF], 0.0)
            dcb[:HALF, HALF:] += l01 * g_top[:, HALF:]
            dcb[HALF:, HALF:] += jnp.where(ahead, l11 * g_bottom, 0.0)
        intra = jnp.concatenate([top, bottom], axis=0)
        d_values = intra + inter
        p_12 = dyf * (y_ref[:, at] - skip * actf) - actf * intra
        p_12h = p_12.astype(bf16)
        p12h[:, at] = p_12h
        p12l[:, at] = (p_12 - p_12h.astype(f32)).astype(bf16)
        p3[:, at] = (actf * inter).astype(bf16)
        p23[:, at] = (actf * d_values).astype(bf16)
        d_act = d_values + skip * dyf
        pre = cw_ref[0:1, at] * xf[5 : 5 + Q, at]
        for tap in range(1, CONV):
            pre = pre + cw_ref[tap : tap + 1, at] * xf[5 + tap : 5 + tap + Q, at]
        squashed = sigmoid(pre)
        d_pre = d_act * squashed * (1.0 + pre * (1.0 - squashed))
        dp[0:Q, at] = d_pre
        sums = [
            jnp.sum(d_pre * xf[5 + tap : 5 + tap + Q, at], axis=0, keepdims=True)
            for tap in range(CONV)
        ]
        sums.append(jnp.sum(dyf * actf, axis=0, keepdims=True))
        for place, total in enumerate(sums):
            gconv_ref[place : place + 1, at] += total
        d_in = cw_ref[CONV - 1 : CONV, at] * d_pre
        for tap in range(CONV - 1):
            d_in = d_in + cw_ref[tap : tap + 1, at] * dp[CONV - 1 - tap : CONV - 1 - tap + Q, at]
        dci_ref[:, at] = d_in.astype(bf16)
        kept = back[:, at] * jnp.where(left, e_end[:, h0 : h0 + 1], e_end[:, h1 : h1 + 1])
        cross[0:1, at] = jnp.sum(kept * s_ref[0, :, at].astype(f32), axis=0, keepdims=True)
        back[:, at] = kept + dot_nn(reads_t, decayed)
    dcb_t = dcb[...]
    d_keys = dot_nn(dcb_t.astype(bf16), reads) + dot_nt(wx[...], back16[...])
    d_reads = dot_nn(dcb_t.T.astype(bf16), keys) + dot_nt(edy[...], s_ref[0])
    dbc_ref[:, :STATE] = d_keys.astype(dbc_ref.dtype)
    dbc_ref[:, STATE:] = d_reads.astype(dbc_ref.dtype)
    unit = lax.broadcasted_iota(jnp.int32, (OWN, LANES), 0)
    head = lax.broadcasted_iota(jnp.int32, (OWN, LANES), 1)
    member = jnp.where(unit // HEAD_DIM == head, 1.0, 0.0)
    member16 = member.astype(bf16)
    s_12 = dot_nn(p12h[...], member16) + dot_nn(p12l[...], member16)
    s_3 = dot_nn(p3[...], member16)
    s_23 = dot_nn(p23[...], member16)
    through = dot_exact(cross[...], member)[0:1, :]
    row = lax.broadcasted_iota(jnp.int32, (Q, Q), 0)
    column = lax.broadcasted_iota(jnp.int32, (Q, Q), 1)
    suffix = jnp.where(column >= row, 1.0, 0.0)
    prefix = jnp.where(column < row, 1.0, 0.0)
    d_log = dot_exact(suffix, s_12) + dot_exact(prefix, s_3) + through
    slope = sigmoid(v)
    ratio = jnp.where(steps > 0.0, slope / steps, 0.0)
    rate = rows_ref[1:2, :]
    d_sum = s_23 * ratio + rate * d_log * slope
    ddt_ref[...] = d_sum * rows_ref[2:3, :]
    grow_ref[0:1, :] += jnp.sum(d_sum, axis=0, keepdims=True)
    grow_ref[1:2, :] += jnp.sum(d_log * rate * steps, axis=0, keepdims=True)


def recurrence_backward(conv_in, act, dy, y, bc, dt_tile, entry, taps, rows, skip_row):
    length = conv_in.shape[0]
    blocks = length // Q
    whole = lambda i: (0, 0)
    along = lambda i: (blocks - 1 - i, 0)
    previous = lambda i: (jnp.maximum((blocks - 1 - i) * (Q // 16) - 1, 0), 0)
    return pl.pallas_call(
        backward_kernel,
        grid=(blocks,),
        in_specs=[
            pl.BlockSpec((Q, OWN), along),
            pl.BlockSpec((16, OWN), previous),
            pl.BlockSpec((Q, OWN), along),
            pl.BlockSpec((Q, OWN), along),
            pl.BlockSpec((Q, OWN), along),
            pl.BlockSpec((Q, 2 * STATE), along),
            pl.BlockSpec((Q, LANES), along),
            pl.BlockSpec((1, STATE, OWN), lambda i: (blocks - 1 - i, 0, 0)),
            pl.BlockSpec((8, OWN), whole),
            pl.BlockSpec((8, LANES), whole),
            pl.BlockSpec((8, OWN), whole),
        ],
        out_specs=[
            pl.BlockSpec((Q, OWN), along),
            pl.BlockSpec((Q, 2 * STATE), along),
            pl.BlockSpec((Q, LANES), along),
            pl.BlockSpec((8, OWN), whole),
            pl.BlockSpec((8, LANES), whole),
        ],
        out_shape=[
            jax.ShapeDtypeStruct((length, OWN), bf16),
            jax.ShapeDtypeStruct((length, 2 * STATE), bf16),
            jax.ShapeDtypeStruct((length, LANES), f32),
            jax.ShapeDtypeStruct((8, OWN), f32),
            jax.ShapeDtypeStruct((8, LANES), f32),
        ],
        scratch_shapes=[
            pltpu.VMEM((STATE, OWN), f32),
            pltpu.VMEM((STATE, OWN), bf16),
            pltpu.VMEM((Q + 8, OWN), f32),
            pltpu.VMEM((Q + 8, OWN), f32),
            pltpu.VMEM((Q, OWN), bf16),
            pltpu.VMEM((Q, OWN), bf16),
            pltpu.VMEM((Q, Q), f32),
            pltpu.VMEM((Q, OWN), bf16),
            pltpu.VMEM((Q, OWN), bf16),
            pltpu.VMEM((Q, OWN), bf16),
            pltpu.VMEM((Q, OWN), bf16),
            pltpu.VMEM((8, OWN), f32),
        ],
        compiler_params=pltpu.CompilerParams(
            dimension_semantics=("arbitrary",), vmem_limit_bytes=48 * 2**20
        ),
        cost_estimate=pl.CostEstimate(
            flops=30 * 10**9, bytes_accessed=36 * 2**20, transcendentals=2 * 10**7
        ),
        name="recurrence_backward",
    )(conv_in, conv_in, act, dy, y, bc, dt_tile, entry, taps, rows, skip_row)


def shifted_rows(array, steps):
    length = array.shape[0]
    if steps == 0:
        return array
    zeros = jnp.zeros((abs(steps),) + array.shape[1:], array.dtype)
    if steps > 0:
        return jnp.concatenate([zeros, array[: length - steps]], axis=0)
    return jnp.concatenate([array[-steps:], zeros], axis=0)


def per_device(
    hidden_in,
    widths,
    norm_gain,
    w_in,
    w_dt,
    conv_weight,
    dt_bias,
    a_log,
    skip_gain,
    gate_gain,
    w_out,
    grad_out,
):
    me = lax.axis_index("seq")
    tokens = hidden_in.shape[1]
    length = tokens * PART
    rows_in = w_in.shape[0]
    used_units = INNER // 8 * jnp.left_shift(jnp.int32(1), widths[0])
    units_float = used_units.astype(f32)
    block = jnp.arange(OWN) // LANES * PART + me
    unit_used = block * LANES < used_units
    head_used = ((jnp.arange(OWN_HEADS) // 2 * PART + me) * LANES < used_units).astype(f32)

    tail = jnp.concatenate(
        [
            heads_by_owner(w_dt),
            jnp.broadcast_to(norm_gain[None, :, None], (PART, rows_in, 1)),
            jnp.zeros((PART, rows_in, LANES - OWN_HEADS - 1 - OWN_BC), bf16),
            w_in[:, 2 * INNER :].reshape(rows_in, PART, OWN_BC).transpose(1, 0, 2),
        ],
        axis=2,
    )
    conv_pieces = jnp.concatenate([by_owner(w_in[:, INNER : 2 * INNER]), tail], axis=2)
    gate_pieces = by_owner(w_in[:, :INNER])
    out_rows = jnp.concatenate(
        [w_out, jnp.pad(gate_gain[:, None], ((0, 0), (0, LANES - 1)))], axis=1
    )

    x_all = seq_gather(hidden_in[0]).reshape(length, D)
    w_conv = gather_in(conv_pieces)
    w_gate = gather_in(gate_pieces)
    out_full = gather_out(out_rows)
    cot_all = seq_gather(grad_out[0]).reshape(length, D)
    w_o = out_full[:, :D]
    gate_row = out_full[:, D].astype(f32)[None, :]
    gain_row = w_conv[:, OWN + OWN_HEADS].astype(f32)[None, :]

    def own_heads(array):
        return lax.dynamic_index_in_dim(array.reshape(STRIPS, PART, 2), me, 1, False).reshape(-1)

    bias = own_heads(dt_bias)
    rate = -jnp.exp(own_heads(a_log))
    skip = own_heads(skip_gain)
    pad_heads = lambda a: jnp.pad(a, (0, LANES - OWN_HEADS))
    rows = jnp.stack(
        [pad_heads(bias), pad_heads(rate), pad_heads(head_used)] + [jnp.zeros((LANES,), f32)] * 5
    )
    skip_row = jnp.broadcast_to(jnp.repeat(skip, HEAD_DIM)[None, :], (8, OWN))
    taps = lax.dynamic_index_in_dim(
        conv_weight[:, :INNER].reshape(CONV, STRIPS, PART, LANES), me, 2, False
    ).reshape(CONV, OWN)
    taps = jnp.pad(taps.astype(f32), ((0, 8 - CONV), (0, 0)))
    taps_bc = lax.dynamic_slice_in_dim(conv_weight[:, INNER:], me * OWN_BC, OWN_BC, 1).astype(f32)

    x_float = x_all.astype(f32)
    inverse_rms = lax.rsqrt(jnp.mean(x_float * x_float, axis=1, keepdims=True) + epsilon)
    normed = (x_float * inverse_rms * gain_row).astype(bf16)
    dt_tile = dot_nn(normed, w_conv[:, OWN:])
    conv_bc = dt_tile[:, LANES - OWN_BC :].astype(bf16)
    conv_bc_float = conv_bc.astype(f32)
    pre_bc = sum(
        taps_bc[tap] * shifted_rows(conv_bc_float, CONV - 1 - tap) for tap in range(CONV)
    )
    act_bc = (pre_bc * sigmoid(pre_bc)).astype(bf16)
    bc = seq_gather(act_bc).transpose(1, 0, 2).reshape(length, 2 * STATE)
    conv_in = jnp.where(unit_used, dot_nn(normed, w_conv[:, :OWN]), 0.0).astype(bf16)
    y, act, entry = recurrence_forward(conv_in, bc, dt_tile, taps, rows, skip_row)
    z = jnp.where(unit_used, dot_nn(normed, w_gate), 0.0)
    d_rounded = dot_nt(cot_all, w_o)
    squashed = sigmoid(z)
    gate_act = z * squashed
    gated = y * gate_act
    e_gate = d_rounded * gate_row
    sums = jnp.stack(
        [jnp.sum(gated * gated, axis=1), jnp.sum(e_gate * gated, axis=1)]
    ).reshape(2, length // LANES, LANES)
    sums = seq_total(sums).reshape(2, length)
    inverse_gate = lax.rsqrt(sums[0] / units_float + epsilon)
    pull = (inverse_gate**3 * sums[1] / units_float)[:, None]
    inverse_gate = inverse_gate[:, None]
    normalized = gated * inverse_gate
    rounded_out = (normalized * gate_row).astype(bf16)
    grad_gate_local = jnp.sum(d_rounded * normalized, axis=0)
    d_gated = inverse_gate * e_gate - gated * pull
    d_y = (d_gated * gate_act).astype(bf16)
    d_z = (d_gated * y * squashed * (1.0 + z * (1.0 - squashed))).astype(bf16)

    grad_w_out = scatter_out(dot_tn(rounded_out, cot_all).astype(bf16))
    branch = dot_nn(rounded_out, w_o).astype(bf16).reshape(PART, tokens, D)
    x_own = hidden_in[0].astype(f32)
    hidden_out = (x_own + seq_scatter(branch)).astype(bf16)[None]
    grad_gate_in = scatter_in(dot_tn(normed, d_z).astype(bf16))

    d_conv_in, d_bc, d_dt, g_conv, g_rows = recurrence_backward(
        conv_in, act, d_y, y, bc, dt_tile, entry, taps, rows, skip_row
    )
    d_act_bc = seq_scatter(d_bc.reshape(length, PART, OWN_BC).transpose(1, 0, 2))
    squashed_bc = sigmoid(pre_bc)
    d_pre_bc = d_act_bc * squashed_bc * (1.0 + pre_bc * (1.0 - squashed_bc))
    g_conv_bc = jnp.stack(
        [
            jnp.sum(d_pre_bc * shifted_rows(conv_bc_float, CONV - 1 - tap), axis=0)
            for tap in range(CONV)
        ]
    )
    d_conv_bc = sum(
        taps_bc[tap] * shifted_rows(d_pre_bc, tap - (CONV - 1)) for tap in range(CONV)
    ).astype(bf16)
    d_project = jnp.concatenate(
        [
            d_conv_in,
            d_dt[:, :OWN_HEADS].astype(bf16),
            jnp.zeros((length, LANES - OWN_HEADS - OWN_BC), bf16),
            d_conv_bc,
        ],
        axis=1,
    )
    grad_conv_in = scatter_in(dot_tn(normed, d_project).astype(bf16))
    d_normed = dot_nt(d_z, w_gate) + dot_nt(d_project, w_conv)
    grad_norm_local = jnp.sum(d_normed * (x_float * inverse_rms), axis=0)
    d_own = seq_scatter(d_normed.astype(bf16).reshape(PART, tokens, D))
    own_rms = lax.rsqrt(jnp.mean(x_own * x_own, axis=1, keepdims=True) + epsilon)
    d_scaled = d_own * gain_row
    d_input = own_rms * d_scaled - x_own * own_rms**3 * jnp.mean(
        d_scaled * x_own, axis=1, keepdims=True
    )
    grad_in = (grad_out[0].astype(f32) + d_input).astype(bf16)[None]

    g_skip = jnp.sum(g_conv[4].reshape(OWN_HEADS, HEAD_DIM), axis=1)
    small = jnp.concatenate(
        [
            g_conv[:CONV].reshape(-1),
            g_conv_bc.reshape(-1),
            pad_heads(g_rows[0, :OWN_HEADS]),
            pad_heads(g_rows[1, :OWN_HEADS]),
            pad_heads(g_skip),
            grad_norm_local,
            grad_gate_local,
        ]
    )
    count = small.shape[0]
    padded = -(-count // (8 * LANES)) * 8 * LANES
    small = jnp.pad(small, (0, padded - count)).reshape(-1, LANES)
    every = seq_gather(dp_total(small)).reshape(PART, padded)
    start = 0

    def take(size):
        nonlocal start
        start += size
        return every[:, start - size : start]

    all_conv = take(CONV * OWN).reshape(PART, CONV, OWN)
    all_conv_bc = take(CONV * OWN_BC).reshape(PART, CONV, OWN_BC)
    head_sums = [heads_from_owner(take(LANES)[:, None, :OWN_HEADS]).reshape(HEADS) for _ in range(3)]
    grad_norm = jnp.sum(take(D), axis=0)
    grad_gate = lax.dynamic_index_in_dim(take(OWN), me, 0, False)
    grad_conv = jnp.concatenate(
        [from_owner(all_conv), all_conv_bc.transpose(1, 0, 2).reshape(CONV, 2 * STATE)], axis=1
    )
    place = lax.axis_index(("dp", "seq"))
    norm_rows = norm_gain.shape[0]
    grad_norm_gain = lax.dynamic_slice_in_dim(grad_norm, place * norm_rows, norm_rows, 0)
    gate_rows = gate_gain.shape[0]
    if gate_rows == LANES:
        grad_gate_gain = lax.dynamic_slice_in_dim(
            grad_gate, lax.axis_index("dp") * gate_rows, gate_rows, 0
        )
    else:
        start = CONV * OWN + CONV * OWN_BC + 3 * LANES + D
        whole_gate = from_owner(take(OWN)[:, None, :]).reshape(INNER)
        grad_gate_gain = lax.dynamic_slice_in_dim(whole_gate, place * gate_rows, gate_rows, 0)

    grad_w_in = jnp.concatenate(
        [
            from_owner(grad_gate_in),
            from_owner(grad_conv_in[:, :, :OWN]),
            grad_conv_in[:, :, CONV_COLS - OWN_BC :].transpose(1, 0, 2).reshape(rows_in, 2 * STATE),
        ],
        axis=1,
    )
    grad_w_dt = heads_from_owner(grad_conv_in[:, :, OWN : OWN + OWN_HEADS])
    return (
        hidden_out,
        grad_in,
        grad_norm_gain,
        grad_w_in,
        grad_w_dt,
        grad_conv,
        head_sums[0],
        head_sums[1],
        head_sums[2],
        grad_gate_gain,
        grad_w_out,
    )


def solution(mesh):
    return jax.shard_map(
        per_device,
        mesh=mesh,
        in_specs=(
            P("dp", "seq", None),
            P("dp"),
            P(("dp", "seq")),
            P(("dp", "seq"), None),
            P(("dp", "seq"), None),
            P(),
            P(),
            P(),
            P(),
            P(("dp", "seq")),
            P(("dp", "seq"), None),
            P("dp", "seq", None),
        ),
        out_specs=(
            P("dp", "seq", None),
            P("dp", "seq", None),
            P(("dp", "seq")),
            P(("dp", "seq"), None),
            P(("dp", "seq"), None),
            P(),
            P(),
            P(),
            P(),
            P(("dp", "seq")),
            P(("dp", "seq"), None),
        ),
        check_vma=False,
    )
```

time: 2510 us -> 1190 us (0.47)
  waiting for transfers between devices: 1200 us -> 344 us
  matrix products: 387 us -> 153 us
  blocking collectives: 210 us -> 0 us
  other arithmetic: 185 us -> 88 us
  Pallas kernels: 0 us -> 91 us
  starting transfers between devices: 3.74 us -> 59.5 us
  loops' own time: 38 us -> 0 us
    reduce_scatter x2 -> x0, waiting for transfers between devices: 959 us -> none  [the longest x1 602 us: per_device(): lax.psum_scatter(outer_dot(normed_full, d_project_all), ('dp', 'seq'), sc...]
    ppermute x2 -> x69, waiting for transfers between devices: 1.39 us -> 344 us  [the longest x21 196 us: dp_shift_z(): return lax.ppermute(value, 'dp', pairs)]
    dot_general x45 -> x10, matrix products: 387 us -> 153 us  [the longest x3 60.8 us: dot_nt(): lax.dot_general(a, b, (((1,), (1,)), ((), ())), preferred_element_type=f32)]
    psum x1 -> x0, waiting for transfers between devices: 128 us -> none  [per_device(): lax.psum((grad_conv_local, d_bias, d_log, d_skip, grad_norm_local, grad_g...]
    dynamic_update_slice x8 -> x52, local copies, waits for them, and re-layouts: 186 us -> 309 us  [the longest x12 144 us: dp_gather(): lax.dynamic_update_index_in_dim(out, dp_swap_x(piece), source * 2 + 1 - x...]
    all_gather x4 -> x0, waiting for transfers between devices: 114 us -> none  [the longest x1 114 us: per_device(): lax.all_gather(w_in, ('dp', 'seq'), axis=0, tiled=True)]
    all_gather x3 -> x0, blocking collectives: 96.3 us -> none  [the longest x1 53.3 us: per_device(): gain_piece = lax.all_gather(gate_gain, ('dp', 'seq'), axis=0, tiled=True)]
    pallas_call x0 -> x2, Pallas kernels: none -> 91 us  [the longest x1 60.7 us: recurrence_backward(): pl.pallas_call(backward_kernel, grid=(blocks,), in_specs=[pl.BlockSpec((Q...]
  transfers between devices with their start and end apart: 9 -> 69, of which waited for: 6 -> 27; matrix products, arithmetic and copies ran while one was open for 19% -> 51% of each run, Pallas kernels for 0% -> 5%
where the time goes in v1:
time: 1190 us; the launch traced here: 1180 us
  local copies, waits for them, and re-layouts  438 us (37%)
  waiting for transfers between devices  344 us (29%)
  matrix products  153 us (13%)
  Pallas kernels  91 us (8%)
  other arithmetic  88 us (7%)
  starting transfers between devices  59.5 us (5%)
    ppermute x21, waiting for transfers between devices, dp_shift_z(): return lax.ppermute(value, 'dp', pairs)  196 us
    dynamic_update_slice x12, local copies, waits for them, and re-layouts, dp_gather(): lax.dynamic_update_index_in_dim(out, dp_swap_x(piece), source * 2 + 1 - x...  144 us
    dynamic_update_slice x12, local copies, waits for them, and re-layouts, dp_gather(): out = lax.dynamic_update_index_in_dim(out, piece, source * 2 + x, 0)  122 us
    ppermute x32, waiting for transfers between devices, xor_seq(): return lax.ppermute(value, 'seq', [(s, s ^ bits) for s in range(PART)])  99.4 us
    dot_general x3, matrix products, dot_nt(): lax.dot_general(a, b, (((1,), (1,)), ((), ())), preferred_element_type=f32)  60.8 us
    pallas_call x1, Pallas kernels, recurrence_backward(): pl.pallas_call(backward_kernel, grid=(blocks,), in_specs=[pl.BlockSpec((Q...  60.7 us
    dot_general x4, matrix products, dot_nn(): lax.dot_general(a, b, (((1,), (0,)), ((), ())), preferred_element_type=f32)  48.6 us
    ppermute x16, waiting for transfers between devices, dp_swap_x(): return lax.ppermute(value, 'dp', [(d, d ^ 1) for d in range(8)])  48.1 us
  transfers between devices with their start and end apart: 69, of which 27 were waited for; matrix products, arithmetic and copies ran while one was open for 51% of the time, Pallas kernels for 5%

profile of v1, /device:TPU:8, one launch (start us, length us, event | category | flops | bytes accessed | tf_op | source)
XLA Modules:
  0.0 1176.6 jit_solution(10123269297389412202)
XLA Ops:
  52.2 25.5 %dynamic_update_slice.184 = bf16[8,256,1152]{1,0,2:T(8,128)(2,1)} dynamic-update-slice(bf16[8,256,1152]{1,0,2:T(8,128)(2,1)} %broadcast_in_dim.231, bf16[1,256,1152]{1,0,2:T(2,128)(2,1)S(1)} %copy.143, s32[]{:T(128)S(6)} %select_n.301, s32[]{:T(128)} %constant.477.clone.1, s32[]{:T(128)} %constant.477.clone.1) | dynamic-update-slice | bytes 1179652 | tf_op jit(solution)/shard_map/jit(dynamic_update_index_in_dim)/dynamic_update_slice | solution.py:102
  106.2 58.3 %collective-permute-done.9 = bf16[256,1152]{1,0:T(8,128)(2,1)S(1)} collective-permute-done((bf16[256,1152]{1,0:T(8,128)(2,1)}, bf16[256,1152]{1,0:T(8,128)(2,1)S(1)}, u32[]{:S(2)}, u32[]{:S(2)}) %collective-permute-start.9) | collective-permute-done | bytes 589856 | tf_op jit(solution)/shard_map/ppermute | solution.py:88
  175.6 25.6 %dynamic_update_slice.185 = bf16[8,256,1152]{1,0,2:T(8,128)(2,1)} dynamic-update-slice(bf16[8,256,1152]{1,0,2:T(8,128)(2,1)} %dynamic_update_slice.184, bf16[1,256,1152]{1,0,2:T(2,128)(2,1)} %copy.144, s32[]{:T(128)S(6)} %select_n.302, s32[]{:T(128)} %constant.477.clone.1, s32[]{:T(128)} %constant.477.clone.1) | dynamic-update-slice | bytes 1179652 | tf_op jit(solution)/shard_map/jit(dynamic_update_index_in_dim)/dynamic_update_slice | solution.py:103
  201.2 25.6 %dynamic_update_slice.186 = bf16[8,256,1152]{1,0,2:T(8,128)(2,1)} dynamic-update-slice(bf16[8,256,1152]{1,0,2:T(8,128)(2,1)} %dynamic_update_slice.185, bf16[1,256,1152]{1,0,2:T(2,128)(2,1)} %copy.145, s32[]{:T(128)S(6)} %select_n.304, s32[]{:T(128)} %constant.477.clone.1, s32[]{:T(128)} %constant.477.clone.1) | dynamic-update-slice | bytes 1179652 | tf_op jit(solution)/shard_map/jit(dynamic_update_index_in_dim)/dynamic_update_slice | solution.py:102
  279.7 28.8 %dynamic_update_slice.219 = bf16[8,128,2176]{1,0,2:T(8,128)(2,1)} dynamic-update-slice(bf16[8,128,2176]{1,0,2:T(8,128)(2,1)} %copy.162, bf16[1,128,2176]{1,0,2:T(2,128)(2,1)} %copy.163, s32[]{:T(128)S(6)} %select_n.311, s32[]{:T(128)} %constant.477.clone.1, s32[]{:T(128)} %constant.477.clone.1) | dynamic-update-slice | bytes 1114116 | tf_op jit(solution)/shard_map/jit(dynamic_update_index_in_dim)/dynamic_update_slice | solution.py:103
  355.6 25.6 %dynamic_update_slice.187 = bf16[8,256,1152]{1,0,2:T(8,128)(2,1)} dynamic-update-slice(bf16[8,256,1152]{1,0,2:T(8,128)(2,1)} %dynamic_update_slice.186, bf16[1,256,1152]{1,0,2:T(2,128)(2,1)} %copy.146, s32[]{:T(128)S(6)} %select_n.305, s32[]{:T(128)} %constant.477.clone.1, s32[]{:T(128)} %constant.477.clone.1) | dynamic-update-slice | bytes 1179652 | tf_op jit(solution)/shard_map/jit(dynamic_update_index_in_dim)/dynamic_update_slice | solution.py:103
  381.2 25.5 %dynamic_update_slice.188 = bf16[8,256,1152]{1,0,2:T(8,128)(2,1)} dynamic-update-slice(bf16[8,256,1152]{1,0,2:T(8,128)(2,1)} %dynamic_update_slice.187, bf16[1,256,1152]{1,0,2:T(2,128)(2,1)S(1)} %copy.147, s32[]{:T(128)S(6)} %select_n.307, s32[]{:T(128)} %constant.477.clone.1, s32[]{:T(128)} %constant.477.clone.1) | dynamic-update-slice | bytes 1179652 | tf_op jit(solution)/shard_map/jit(dynamic_update_index_in_dim)/dynamic_update_slice | solution.py:102
  406.7 25.7 %dynamic_update_slice.189 = bf16[8,256,1152]{1,0,2:T(8,128)(2,1)} dynamic-update-slice(bf16[8,256,1152]{1,0,2:T(8,128)(2,1)} %dynamic_update_slice.188, bf16[1,256,1152]{1,0,2:T(2,128)(2,1)} %copy.148, s32[]{:T(128)S(6)} %select_n.308, s32[]{:T(128)} %constant.477.clone.1, s32[]{:T(128)} %constant.477.clone.1) | dynamic-update-slice | bytes 1179652 | tf_op jit(solution)/shard_map/jit(dynamic_update_index_in_dim)/dynamic_update_slice | solution.py:103
  432.4 25.6 %dynamic_update_slice.190 = bf16[8,256,1152]{1,0,2:T(8,128)(2,1)} dynamic-update-slice(bf16[8,256,1152]{1,0,2:T(8,128)(2,1)} %dynamic_update_slice.189, bf16[1,256,1152]{1,0,2:T(2,128)(2,1)} %copy.149, s32[]{:T(128)S(6)} %select_n.310, s32[]{:T(128)} %constant.477.clone.1, s32[]{:T(128)} %constant.477.clone.1) | dynamic-update-slice | bytes 1179652 | tf_op jit(solution)/shard_map/jit(dynamic_update_index_in_dim)/dynamic_update_slice | solution.py:102
  458.0 25.9 %dynamic_update_slice.191 = bf16[8,256,1152]{1,0,2:T(8,128)(2,1)} dynamic-update-slice(bf16[8,256,1152]{1,0,2:T(8,128)(2,1)} %dynamic_update_slice.190, bf16[1,256,1152]{1,0,2:T(2,128)(2,1)S(1)} %copy-done.15, s32[]{:T(128)S(6)} %select_n.311, s32[]{:T(128)} %constant.477.clone.1, s32[]{:T(128)} %constant.477.clone.1) | dynamic-update-slice | bytes 1179652 | tf_op jit(solution)/shard_map/jit(dynamic_update_index_in_dim)/dynamic_update_slice | solution.py:103
  574.0 30.3 %recurrence_forward.1 = (f32[2048,1024]{1,0:T(8,128)}, bf16[2048,1024]{1,0:T(8,128)(2,1)S(1)}, bf16[8,128,1024]{2,1,0:T(8,128)(2,1)S(1)}) custom-call(bf16[2048,1024]{1,0:T(8,128)(2,1)S(1)} %copy-done.2, bf16[2048,256]{1,0:T(8,128)(2,1)S(1)} %copy.157.bc_ref, f32[2048,128]{1,0:T(8,128)S(1)} %fusion.44.dt_ref, f32[8,1024]{1,0:T(8,128)S(1)} %pad_convert_fusion.cw_ref, ...), custom_call_target="tpu_custom_call" | custom-call | flops 12000000000 | bytes 25165824 | tf_op jit(solution)/shard_map/recurrence_forward/pallas_call | solution.py:300
  607.6 22.7 %multiply_reduce_fusion.4 = (f32[2048]{0:T(1024)S(1)}, f32[2048]{0:T(1024)S(1)}, f32[2048,1024]{1,0:T(8,128)}, f32[2048,1024]{1,0:T(8,128)}) fusion(f32[1024]{0:T(1024)S(1)} %bitcast.471, f32[2048,1024]{1,0:T(8,128)} %get-tuple-element.19.y_ref, f32[2048,1024]{1,0:T(8,128)} %fusion.77, pred[1024]{0:T(1024)(128)(4,1)S(1)} %fusion.55, ...), kind=kOutput, calls=%fused_computation.13 | convolution fusion | flops 8612999168 | bytes 46158848 | tf_op jit(solution)/shard_map/dot_general | solution.py:199
  635.2 15.0 %convolution_convert_fusion.2 = bf16[1024,2048]{1,0:T(8,128)(2,1)S(1)} fusion(bf16[2048,2048]{1,0:T(8,128)(2,1)} %bitcast.63, f32[2048,1024]{1,0:T(8,128)} %get-tuple-element.71, f32[2048]{0:T(1024)S(1)} %fusion.51, f32[1024]{0:T(1024)S(1)} %bitcast.472), kind=kOutput, calls=%fused_computation.45 | convolution fusion | flops 8598323200 | bytes 20983808 | tf_op jit(solution)/shard_map/dot_general | solution.py:203
  650.3 16.1 %convolution_convert_fusion.1 = bf16[2048,2048]{1,0:T(8,128)(2,1)} fusion(bf16[1024,2176]{0,1:T(8,128)(2,1)} %bitcast.422, f32[2048,1024]{1,0:T(8,128)} %get-tuple-element.71, f32[2048]{0:T(1024)S(1)} %fusion.51, f32[1024]{0:T(1024)S(1)} %bitcast.473), kind=kOutput, calls=%fused_computation.18 | convolution fusion | flops 8600420352 | bytes 20983808 | tf_op jit(solution)/shard_map/dot_general | solution.py:195
  669.0 14.8 %multiply_convert_fusion.3 = (bf16[2048,1024]{1,0:T(8,128)(2,1)}, bf16[2048,1024]{1,0:T(8,128)(2,1)}, f32[1024]{0:T(1024)S(1)}) fusion(f32[2048,1024]{1,0:T(8,128)} %get-tuple-element.19.y_ref, f32[2048,1024]{1,0:T(8,128)S(1)} %bitcast.411, f32[2048,1024]{1,0:T(8,128)} %get-tuple-element.71, f32[2048]{0:T(1024)S(1)} %fusion.48, ...), kind=kLoop, calls=%fused_computation.9 | loop fusion | flops 44039168 | bytes 41968640 | tf_op jit(solution)/shard_map/convert_element_type | solution.py:649
  683.8 60.7 %recurrence_backward.1 = (bf16[2048,1024]{1,0:T(8,128)(2,1)}, bf16[2048,256]{1,0:T(8,128)(2,1)S(1)}, f32[2048,128]{1,0:T(8,128)S(1)}, f32[8,1024]{1,0:T(8,128)S(1)}, f32[8,128]{1,0:T(8,128)S(1)}) custom-call(bf16[2048,1024]{1,0:T(8,128)(2,1)} %select_convert_fusion.ci_ref.prev_ref, bf16[2048,1024]{1,0:T(8,128)(2,1)} %select_convert_fusion.ci_ref.prev_ref, ...), custom_call_target="tpu_custom_call" | custom-call | flops 30000001024 | bytes 37748736 | tf_op jit(solution)/shard_map/recurrence_backward/pallas_call | solution.py:489
  805.2 17.9 %fusion.78 = f32[2048,2048]{1,0:T(8,128)} fusion(bf16[2048,1152]{1,0:T(8,128)(2,1)} %concatenate.48, bf16[2048,1152]{0,1:T(8,128)(2,1)} %bitcast.415), kind=kOutput, calls=%fused_computation.253 | convolution fusion | flops 9663676416 | bytes 26214400 | tf_op jit(solution)/shard_map/dot_general | solution.py:199
  823.1 20.2 %multiply_reduce_fusion = (f32[2048]{0:T(1024)S(1)}, bf16[2048,2048]{1,0:T(8,128)(2,1)}) fusion(bf16[4,512,2048]{2,1,0:T(8,128)(2,1)} %bitcast_dynamic-update-slice_fusion.3, f32[2048]{0:T(1024)S(1)} %bitcast.464, f32[2048,2048]{1,0:T(8,128)} %fusion.78, bf16[2048,1024]{1,0:T(8,128)(2,1)} %get-tuple-element.74, bf16[2048,1024]{1,0:T(8,128)(2,1)} %bitcast.57), kind=kOutput, calls=%fused_computation.1 | convolution fusion | flops 8615098368 | bytes 41959424 | tf_op jit(solution)/shard_map/dot_general | solution.py:199
  844.4 15.7 %convolution_convert_fusion = bf16[2048,1152]{1,0:T(8,128)(2,1)S(1)} fusion(bf16[2048,2048]{1,0:T(8,128)(2,1)} %multiply_convert_fusion.1, bf16[2048,1152]{1,0:T(8,128)(2,1)} %concatenate.48), kind=kOutput, calls=%fused_computation.17 | convolution fusion | flops 9666035712 | bytes 17825792 | tf_op jit(solution)/shard_map/dot_general | solution.py:203
  921.9 28.5 %collective-permute-done.53 = bf16[256,1024]{1,0:T(8,128)(2,1)S(1)} collective-permute-done((bf16[256,1024]{1,0:T(8,128)(2,1)S(1)}, bf16[256,1024]{1,0:T(8,128)(2,1)S(1)}, u32[]{:S(2)}, u32[]{:S(2)}) %collective-permute-start.53) | collective-permute-done | bytes 524320 | tf_op jit(solution)/shard_map/ppermute | solution.py:88
  953.5 22.4 %collective-permute-done.54 = bf16[256,1024]{1,0:T(8,128)(2,1)S(1)} collective-permute-done((bf16[256,1024]{1,0:T(8,128)(2,1)S(1)}, bf16[256,1024]{1,0:T(8,128)(2,1)S(1)}, u32[]{:S(2)}, u32[]{:S(2)}) %collective-permute-start.54) | collective-permute-done | bytes 524320 | tf_op jit(solution)/shard_map/ppermute | solution.py:88
  1017.9 34.5 %collective-permute-done.60 = bf16[256,1152]{1,0:T(8,128)(2,1)S(1)} collective-permute-done((bf16[256,1152]{1,0:T(8,128)(2,1)S(1)}, bf16[256,1152]{1,0:T(8,128)(2,1)S(1)}, u32[]{:S(2)}, u32[]{:S(2)}) %collective-permute-start.60) | collective-permute-done | bytes 589856 | tf_op jit(solution)/shard_map/ppermute | solution.py:88
  1093.1 32.4 %collective-permute-done.43 = bf16[512,2048]{1,0:T(8,128)(2,1)} collective-permute-done((bf16[512,2048]{1,0:T(8,128)(2,1)}, bf16[512,2048]{1,0:T(8,128)(2,1)}, u32[]{:S(2)}, u32[]{:S(2)}) %collective-permute-start.43) | collective-permute-done | bytes 2097184 | tf_op jit(solution)/shard_map/ppermute | solution.py:40
  1129.6 40.2 %collective-permute-done.39 = bf16[512,2048]{1,0:T(8,128)(2,1)} collective-permute-done((bf16[512,2048]{1,0:T(8,128)(2,1)}, bf16[512,2048]{1,0:T(8,128)(2,1)}, u32[]{:S(2)}, u32[]{:S(2)}) %collective-permute-start.39) | collective-permute-done | bytes 2097184 | tf_op jit(solution)/shard_map/ppermute | solution.py:40
  (470 shorter events, 510.1 us)
Async XLA Ops:
  3.4 74.3 %collective-permute-start.29 = (bf16[128,2176]{1,0:T(8,128)(2,1)}, bf16[128,2176]{1,0:T(8,128)(2,1)}, u32[]{:S(2)}, u32[]{:S(2)}) collective-permute-start(bf16[128,2176]{1,0:T(8,128)(2,1)} %fusion.35), channel_id=1, source_target_pairs={{0,4},{4,0},{8,12},{12,8},{16,20},{20,16},{24,28},{28,24},{1,5},{5... | collective-permute-start | bytes 1671176 | tf_op jit(solution)/shard_map/ppermute | solution.py:92
  4.8 74.9 %collective-permute-start.30 = (bf16[128,2176]{1,0:T(8,128)(2,1)}, bf16[128,2176]{1,0:T(8,128)(2,1)}, u32[]{:S(2)}, u32[]{:S(2)}) collective-permute-start(bf16[128,2176]{1,0:T(8,128)(2,1)} %fusion.35), channel_id=1, source_target_pairs={{0,8},{4,12},{8,16},{12,20},{16,24},{20,28},{24,0},{28,4},{1,9},{5... | collective-permute-start | bytes 1671176 | tf_op jit(solution)/shard_map/ppermute | solution.py:88
  79.8 147.0 %collective-permute-start.32 = (bf16[128,2176]{1,0:T(8,128)(2,1)}, bf16[128,2176]{1,0:T(8,128)(2,1)}, u32[]{:S(2)}, u32[]{:S(2)}) collective-permute-start(bf16[128,2176]{1,0:T(8,128)(2,1)} %fusion.35), channel_id=1, source_target_pairs={{0,16},{4,20},{8,24},{12,28},{16,0},{20,4},{24,8},{28,12},{1,17},{... | collective-permute-start | bytes 1671176 | tf_op jit(solution)/shard_map/ppermute | solution.py:88
  82.3 144.7 %collective-permute-start.34 = (bf16[128,2176]{1,0:T(8,128)(2,1)}, bf16[128,2176]{1,0:T(8,128)(2,1)}, u32[]{:S(2)}, u32[]{:S(2)}) collective-permute-start(bf16[128,2176]{1,0:T(8,128)(2,1)} %fusion.35), channel_id=1, source_target_pairs={{0,24},{4,28},{8,0},{12,4},{16,8},{20,12},{24,16},{28,20},{1,25},{... | collective-permute-start | bytes 1671176 | tf_op jit(solution)/shard_map/ppermute | solution.py:88
  82.8 81.6 %collective-permute-start.9 = (bf16[256,1152]{1,0:T(8,128)(2,1)}, bf16[256,1152]{1,0:T(8,128)(2,1)S(1)}, u32[]{:S(2)}, u32[]{:S(2)}) collective-permute-start(bf16[256,1152]{1,0:T(8,128)(2,1)} %bitcast.435), channel_id=1, source_target_pairs={{0,16},{4,20},{8,24},{12,28},{16,0},{20,4},{24,8},{28,12},{1,17},{... | collective-permute-start | bytes 1769480 | tf_op jit(solution)/shard_map/ppermute | solution.py:88
  84.5 84.1 %collective-permute-start.11 = (bf16[256,1152]{1,0:T(8,128)(2,1)}, bf16[256,1152]{1,0:T(8,128)(2,1)}, u32[]{:S(2)}, u32[]{:S(2)}) collective-permute-start(bf16[256,1152]{1,0:T(8,128)(2,1)} %bitcast.436), channel_id=1, source_target_pairs={{0,24},{4,28},{8,0},{12,4},{16,8},{20,12},{24,16},{28,20},{1,25},{... | collective-permute-start | bytes 1769480 | tf_op jit(solution)/shard_map/ppermute | solution.py:88
  94.1 134.1 %collective-permute-start.31 = (bf16[128,2176]{1,0:T(8,128)(2,1)}, bf16[128,2176]{1,0:T(8,128)(2,1)}, u32[]{:S(2)}, u32[]{:S(2)}) collective-permute-start(bf16[128,2176]{1,0:T(8,128)(2,1)} %collective-permute-done.30), channel_id=1, source_target_pairs={{0,4},{4,0},{8,12},{12,8},{16,20},{20,16},{24,28},{28,24},{1,5},{5... | collective-permute-start | bytes 1671176 | tf_op jit(solution)/shard_map/ppermute | solution.py:92
  164.4 324.4 %collective-permute-start = (bf16[512,2048]{1,0:T(8,128)(2,1)S(1)}, bf16[512,2048]{1,0:T(8,128)(2,1)}, u32[]{:S(2)}, u32[]{:S(2)}) collective-permute-start(bf16[512,2048]{1,0:T(8,128)(2,1)S(1)} %bitcast.393), channel_id=1, source_target_pairs={{0,1},{1,0},{2,3},{3,2},{4,5},{5,4},{6,7},{7,6},{8,9},{9,8},{10,11... | collective-permute-start | bytes 6291464 | tf_op jit(solution)/shard_map/ppermute | solution.py:40
  168.6 76.3 %collective-permute-start.22 = (bf16[256,1024]{1,0:T(8,128)(2,1)}, bf16[256,1024]{1,0:T(8,128)(2,1)}, u32[]{:S(2)}, u32[]{:S(2)}) collective-permute-start(bf16[256,1024]{1,0:T(8,128)(2,1)} %bitcast.49), channel_id=1, source_target_pairs={{0,16},{4,20},{8,24},{12,28},{16,0},{20,4},{24,8},{28,12},{1,17},{... | collective-permute-start | bytes 1572872 | tf_op jit(solution)/shard_map/ppermute | solution.py:88
  244.9 243.4 %collective-permute-start.1 = (bf16[512,2048]{1,0:T(8,128)(2,1)S(1)}, bf16[512,2048]{1,0:T(8,128)(2,1)}, u32[]{:S(2)}, u32[]{:S(2)}) collective-permute-start(bf16[512,2048]{1,0:T(8,128)(2,1)S(1)} %bitcast.394), channel_id=1, source_target_pairs={{0,2},{1,3},{2,0},{3,1},{4,6},{5,7},{6,4},{7,5},{8,10},{9,11},{10,... | collective-permute-start | bytes 6291464 | tf_op jit(solution)/shard_map/ppermute | solution.py:40
  246.4 242.0 %collective-permute-start.27 = (bf16[512,2048]{1,0:T(8,128)(2,1)}, bf16[512,2048]{1,0:T(8,128)(2,1)}, u32[]{:S(2)}, u32[]{:S(2)}) collective-permute-start(bf16[512,2048]{1,0:T(8,128)(2,1)} %bitcast.59), channel_id=1, source_target_pairs={{0,2},{1,3},{2,0},{3,1},{4,6},{5,7},{6,4},{7,5},{8,10},{9,11},{10,... | collective-permute-start | bytes 6291464 | tf_op jit(solution)/shard_map/ppermute | solution.py:40
  254.9 57.1 %collective-permute-start.23 = (bf16[256,1024]{1,0:T(8,128)(2,1)}, bf16[256,1024]{1,0:T(8,128)(2,1)}, u32[]{:S(2)}, u32[]{:S(2)}) collective-permute-start(bf16[256,1024]{1,0:T(8,128)(2,1)} %collective-permute-done.22), channel_id=1, source_target_pairs={{0,4},{4,0},{8,12},{12,8},{16,20},{20,16},{24,28},{28,24},{1,5},{5... | collective-permute-start | bytes 1572872 | tf_op jit(solution)/shard_map/ppermute | solution.py:92
  328.4 167.8 %collective-permute-start.26 = (bf16[512,2048]{1,0:T(8,128)(2,1)}, bf16[512,2048]{1,0:T(8,128)(2,1)}, u32[]{:S(2)}, u32[]{:S(2)}) collective-permute-start(bf16[512,2048]{1,0:T(8,128)(2,1)} %bitcast.59), channel_id=1, source_target_pairs={{0,1},{1,0},{2,3},{3,2},{4,5},{5,4},{6,7},{7,6},{8,9},{9,8},{10,11... | collective-permute-start | bytes 6291464 | tf_op jit(solution)/shard_map/ppermute | solution.py:40
  488.3 74.6 %collective-permute-start.28 = (bf16[512,2048]{1,0:T(8,128)(2,1)}, bf16[512,2048]{1,0:T(8,128)(2,1)}, u32[]{:S(2)}, u32[]{:S(2)}) collective-permute-start(bf16[512,2048]{1,0:T(8,128)(2,1)} %collective-permute-done.27), channel_id=1, source_target_pairs={{0,1},{1,0},{2,3},{3,2},{4,5},{5,4},{6,7},{7,6},{8,9},{9,8},{10,11... | collective-permute-start | bytes 6291464 | tf_op jit(solution)/shard_map/ppermute | solution.py:40
  667.9 240.6 %collective-permute-start.65 = (bf16[4,128,2048]{2,1,0:T(8,128)(2,1)}, bf16[4,128,2048]{2,1,0:T(8,128)(2,1)}, u32[]{:S(2)}, u32[]{:S(2)}) collective-permute-start(bf16[4,128,2048]{2,1,0:T(8,128)(2,1)} %dynamic-slice_bitcast_fusion.3), channel_id=1, source_target_pairs={{0,4},{4,0},{8,12},{12,8},{16,20},{20,16},{24,28},{28,24},{1,5},{5... | collective-permute-start | bytes 6291464 | tf_op jit(solution)/shard_map/ppermute | solution.py:92
  763.0 136.9 %collective-permute-start.51 = (bf16[4,256,1024]{2,1,0:T(8,128)(2,1)}, bf16[4,256,1024]{2,1,0:T(8,128)(2,1)}, u32[]{:S(2)}, u32[]{:S(2)}) collective-permute-start(bf16[4,256,1024]{2,1,0:T(8,128)(2,1)} %dynamic-slice_bitcast_fusion.4), channel_id=1, source_target_pairs={{0,4},{4,0},{8,12},{12,8},{16,20},{20,16},{24,28},{28,24},{1,5},{5... | collective-permute-start | bytes 6291464 | tf_op jit(solution)/shard_map/ppermute | solution.py:92
  865.7 133.5 %collective-permute-start.58 = (bf16[4,256,1152]{2,1,0:T(8,128)(2,1)}, bf16[4,256,1152]{2,1,0:T(8,128)(2,1)}, u32[]{:S(2)}, u32[]{:S(2)}) collective-permute-start(bf16[4,256,1152]{2,1,0:T(8,128)(2,1)} %dynamic-slice_bitcast_fusion.2), channel_id=1, source_target_pairs={{0,4},{4,0},{8,12},{12,8},{16,20},{20,16},{24,28},{28,24},{1,5},{5... | collective-permute-start | bytes 7077896 | tf_op jit(solution)/shard_map/ppermute | solution.py:92
  907.2 68.6 %collective-permute-start.54 = (bf16[256,1024]{1,0:T(8,128)(2,1)S(1)}, bf16[256,1024]{1,0:T(8,128)(2,1)S(1)}, u32[]{:S(2)}, u32[]{:S(2)}) collective-permute-start(bf16[256,1024]{1,0:T(8,128)(2,1)S(1)} %get-tuple-element.89), channel_id=1, source_target_pairs={{0,24},{4,28},{8,0},{12,4},{16,8},{20,12},{24,16},{28,20},{1,25},{... | collective-permute-start | bytes 1572872 | tf_op jit(solution)/shard_map/ppermute | solution.py:88
  911.1 72.9 %collective-permute-start.66 = (bf16[128,2048]{1,0:T(8,128)(2,1)S(1)}, bf16[128,2048]{1,0:T(8,128)(2,1)S(1)}, u32[]{:S(2)}, u32[]{:S(2)}) collective-permute-start(bf16[128,2048]{1,0:T(8,128)(2,1)S(1)} %get-tuple-element.82), channel_id=1, source_target_pairs={{0,8},{4,12},{8,16},{12,20},{16,24},{20,28},{24,0},{28,4},{1,9},{5... | collective-permute-start | bytes 1572872 | tf_op jit(solution)/shard_map/ppermute | solution.py:88
  918.2 76.6 %collective-permute-start.67 = (bf16[128,2048]{1,0:T(8,128)(2,1)S(1)}, bf16[128,2048]{1,0:T(8,128)(2,1)S(1)}, u32[]{:S(2)}, u32[]{:S(2)}) collective-permute-start(bf16[128,2048]{1,0:T(8,128)(2,1)S(1)} %get-tuple-element.84), channel_id=1, source_target_pairs={{0,16},{4,20},{8,24},{12,28},{16,0},{20,4},{24,8},{28,12},{1,17},{... | collective-permute-start | bytes 1572872 | tf_op jit(solution)/shard_map/ppermute | solution.py:88
  975.9 93.6 %collective-permute-start.42 = (bf16[2,512,2048]{2,1,0:T(8,128)(2,1)}, bf16[2,512,2048]{2,1,0:T(8,128)(2,1)}, u32[]{:S(2)}, u32[]{:S(2)}) collective-permute-start(bf16[2,512,2048]{2,1,0:T(8,128)(2,1)} %dynamic-slice_bitcast_fusion), channel_id=1, source_target_pairs={{0,1},{1,0},{2,3},{3,2},{4,5},{5,4},{6,7},{7,6},{8,9},{9,8},{10,11... | collective-permute-start | bytes 12582920 | tf_op jit(solution)/shard_map/ppermute | solution.py:40
  1003.0 52.1 %collective-permute-start.61 = (bf16[256,1152]{1,0:T(8,128)(2,1)S(1)}, bf16[256,1152]{1,0:T(8,128)(2,1)S(1)}, u32[]{:S(2)}, u32[]{:S(2)}) collective-permute-start(bf16[256,1152]{1,0:T(8,128)(2,1)S(1)} %get-tuple-element.80), channel_id=1, source_target_pairs={{0,24},{4,28},{8,0},{12,4},{16,8},{20,12},{24,16},{28,20},{1,25},{... | collective-permute-start | bytes 1769480 | tf_op jit(solution)/shard_map/ppermute | solution.py:88
  1005.0 72.1 %collective-permute-start.38 = (bf16[2,512,2048]{2,1,0:T(8,128)(2,1)}, bf16[2,512,2048]{2,1,0:T(8,128)(2,1)}, u32[]{:S(2)}, u32[]{:S(2)}) collective-permute-start(bf16[2,512,2048]{2,1,0:T(8,128)(2,1)} %dynamic-slice_bitcast_fusion.1), channel_id=1, source_target_pairs={{0,1},{1,0},{2,3},{3,2},{4,5},{5,4},{6,7},{7,6},{8,9},{9,8},{10,11... | collective-permute-start | bytes 12582920 | tf_op jit(solution)/shard_map/ppermute | solution.py:40
  1088.0 81.8 %collective-permute-start.39 = (bf16[512,2048]{1,0:T(8,128)(2,1)}, bf16[512,2048]{1,0:T(8,128)(2,1)}, u32[]{:S(2)}, u32[]{:S(2)}) collective-permute-start(bf16[512,2048]{1,0:T(8,128)(2,1)} %fusion.17), channel_id=1, source_target_pairs={{0,2},{1,3},{2,0},{3,1},{4,6},{5,7},{6,4},{7,5},{8,10},{9,11},{10,... | collective-permute-start | bytes 6291464 | tf_op jit(solution)/shard_map/ppermute | solution.py:40
  (100 other events, 3711.4 us)

commit v2 on v1

--- a/solution.py
+++ b/solution.py
@@ -40,38 +40,48 @@
     return lax.ppermute(value, "seq", [(s, s ^ bits) for s in range(PART)])
 
 
-def seq_gather(block):
-    me = lax.axis_index("seq")
-    sibling = xor_seq(block, 1)
-    across = xor_seq(block, 2)
-    corner = xor_seq(across, 1)
-    out = jnp.zeros((PART,) + block.shape, block.dtype)
-    for bits, piece in ((0, block), (1, sibling), (2, across), (3, corner)):
-        out = lax.dynamic_update_index_in_dim(out, piece, me ^ bits, 0)
-    return out
-
-
-def seq_scatter(blocks):
-    me = lax.axis_index("seq")
-    core, row = me % 2, me // 2
+def core_halves(blocks):
+    core = lax.axis_index("seq") % 2
     view = blocks.reshape((2, 2) + blocks.shape[1:])
     mine = lax.dynamic_index_in_dim(view, core, 1, False)
     other = lax.dynamic_index_in_dim(view, 1 - core, 1, False)
-    half = mine.astype(f32) + xor_seq(other, 1).astype(f32)
-    keep = lax.dynamic_index_in_dim(half, row, 0, False)
-    give = lax.dynamic_index_in_dim(half, 1 - row, 0, False).astype(bf16)
-    return keep + xor_seq(give, 2).astype(f32)
+    return mine, xor_seq(other, 1)
+
+
+def halves_sum(mine, received):
+    row = lax.axis_index("seq") // 2
+
+    def of(which):
+        a = lax.dynamic_index_in_dim(mine, which, 0, False)
+        return a.astype(f32) + lax.dynamic_index_in_dim(received, which, 0, False).astype(f32)
+
+    return of(row), of(1 - row).astype(bf16)
+
+
+def seq_scatter_relative(blocks):
+    view = blocks.reshape((2, 2) + blocks.shape[1:])
+    half = view[:, 0].astype(f32) + xor_seq(view[:, 1], 1).astype(f32)
+    return half[0] + xor_seq(half[1].astype(bf16), 2).astype(f32)
+
+
+def by_partner(pieces):
+    me = lax.axis_index("seq")
+    odd, lower = me % 2 == 1, me >= 2
+    a, b, c, d = pieces
+    a, b = jnp.where(odd, b, a), jnp.where(odd, a, b)
+    c, d = jnp.where(odd, d, c), jnp.where(odd, c, d)
+    return (
+        jnp.where(lower, c, a),
+        jnp.where(lower, d, b),
+        jnp.where(lower, a, c),
+        jnp.where(lower, b, d),
+    )
 
 
 def seq_transpose(pieces):
-    me = lax.axis_index("seq")
-    out = jnp.zeros_like(pieces)
-    for bits in range(PART):
-        piece = lax.dynamic_index_in_dim(pieces, me ^ bits, 0, False)
-        if bits:
-            piece = xor_seq(piece, bits)
-        out = lax.dynamic_update_index_in_dim(out, piece, me ^ bits, 0)
-    return out
+    turned = by_partner([pieces[k] for k in range(PART)])
+    moved = [turned[0]] + [xor_seq(turned[k], k) for k in range(1, PART)]
+    return jnp.stack(by_partner(moved))
 
 
 def seq_total(value):
@@ -92,30 +102,178 @@
     return lax.ppermute(value, "dp", [(d, d ^ 1) for d in range(8)])
 
 
-def dp_gather(block):
-    me = lax.axis_index("dp")
-    z, x = me // 2, me % 2
-    out = jnp.zeros((8,) + block.shape, block.dtype)
-    for steps in range(4):
-        piece = dp_shift_z(block, steps) if steps else block
-        source = (z - steps + 4) % 4
-        out = lax.dynamic_update_index_in_dim(out, piece, source * 2 + x, 0)
-        out = lax.dynamic_update_index_in_dim(out, dp_swap_x(piece), source * 2 + 1 - x, 0)
-    return out
-
-
-def dp_scatter(blocks):
-    me = lax.axis_index("dp")
-    z, x = me // 2, me % 2
+def tie_kernel(*refs):
+    del refs
+
+
+def tie(*values):
+    anywhere = pl.BlockSpec(memory_space=pl.ANY)
+    return pl.pallas_call(
+        tie_kernel,
+        in_specs=[anywhere] * len(values),
+        out_specs=[anywhere] * len(values),
+        out_shape=[jax.ShapeDtypeStruct(v.shape, v.dtype) for v in values],
+        input_output_aliases={k: k for k in range(len(values))},
+        name="tie",
+    )(*values)
+
+
+def after(values, needed):
+    anywhere = pl.BlockSpec(memory_space=pl.ANY)
+    return pl.pallas_call(
+        tie_kernel,
+        in_specs=[anywhere] * (len(values) + len(needed)),
+        out_specs=[anywhere] * len(values),
+        out_shape=[jax.ShapeDtypeStruct(v.shape, v.dtype) for v in values],
+        input_output_aliases={k: k for k in range(len(values))},
+        name="after",
+    )(*values, *needed)
+
+
+def assemble_kernel(places_ref, *refs):
+    rows = refs[0].shape[0]
+    for k, piece in enumerate(refs[:-1]):
+        refs[-1][pl.ds(pl.multiple_of(places_ref[k] * rows, rows), rows), :] = piece[...]
+
+
+def assemble(pieces, places, tile):
+    rows, columns = pieces[0].shape
+    count = len(pieces)
+    along = lambda i, places: (0, i)
+    return pl.pallas_call(
+        assemble_kernel,
+        grid_spec=pltpu.PrefetchScalarGridSpec(
+            num_scalar_prefetch=1,
+            grid=(columns // tile,),
+            in_specs=[pl.BlockSpec((rows, tile), along)] * count,
+            out_specs=pl.BlockSpec((rows * count, tile), along),
+        ),
+        out_shape=jax.ShapeDtypeStruct((rows * count, columns), pieces[0].dtype),
+        compiler_params=pltpu.CompilerParams(vmem_limit_bytes=24 * 2**20),
+        cost_estimate=pl.CostEstimate(
+            flops=0, bytes_accessed=4 * rows * count * columns, transcendentals=0
+        ),
+        name="assemble",
+    )(places, *pieces)
+
+
+def seq_pass(pieces):
+    me = lax.axis_index("seq")
+    core, row = me % 2, me // 2
+    view = pieces.reshape((2, 2) + pieces.shape[1:])
+    give = lax.dynamic_index_in_dim(view, 1 - row, 0, False)
+    keep = lax.dynamic_index_in_dim(view, row, 0, False)
+    got = xor_seq(give, 2)
+    lower = jnp.where(row == 0, keep, got)
+    upper = jnp.where(row == 0, got, keep)
+    both = jnp.stack([lower, upper])
+    mine = lax.dynamic_index_in_dim(both, core, 1, False)
+    other = xor_seq(lax.dynamic_index_in_dim(both, 1 - core, 1, False), 1)
+    first = jnp.where(core == 0, mine, other)
+    second = jnp.where(core == 0, other, mine)
+    return jnp.stack([first, second], axis=1).reshape(pieces.shape)
+
+
+def seq_pieces(block, after=None):
+    source = block if after is None else tie(block, after)[0]
+    across = xor_seq(source, 2)
+    return block, xor_seq(block, 1), across, xor_seq(across, 1)
+
+
+def gather_everything(conv_pieces, gate_pieces, o, x_block):
+    c = seq_pass(conv_pieces).reshape(-1, CONV_COLS)
+    w_conv = lax.all_gather(c, "dp", axis=0, tiled=True)
+    x_across, gate_pieces = after([xor_seq(after([x_block], [c])[0], 2), gate_pieces], [])
+    g = seq_pass(gate_pieces).reshape(-1, OWN)
+    o_x, g, x_across, o = after([dp_swap_x(o), g, x_across, o], [w_conv])
+    x_pieces = (x_block, xor_seq(x_block, 1), x_across, xor_seq(x_across, 1))
+    w_gate = lax.all_gather(g, "dp", axis=0, tiled=True)
+    out_rows = [o] + [dp_shift_z(o, steps) for steps in range(1, 4)] + [o_x]
+    return w_conv, w_gate, out_rows, x_pieces
+
+
+def out_places():
+    dp = lax.axis_index("dp")
+    sources = (dp // 2 - jnp.arange(4, dtype=jnp.int32) + 4) % 4 * 2
+    return jnp.concatenate([sources + dp % 2, sources + 1 - dp % 2]).astype(jnp.int32)
+
+
+def norm_rows(x, gain):
+    x = x.astype(f32)
+    inverse = lax.rsqrt(jnp.mean(x * x, axis=1, keepdims=True) + epsilon)
+    return (x * inverse * gain).astype(bf16)
+
+
+def positions_kernel(shares, with_norm, order_ref, *refs):
+    step = pl.program_id(0)
+    first = 0
+    for k, share in enumerate(shares):
+
+        @pl.when((step >= first) & (step < first + share))
+        def _():
+            if with_norm:
+                refs[-1][...] = norm_rows(refs[k][...], refs[-2][0:1, :])
+            else:
+                refs[-1][...] = refs[k][...]
+
+        first += share
+
+
+def all_positions(pieces, order, gain_rows=None):
+    tile = min(256, min(p.shape[0] for p in pieces))
+    shares = [p.shape[0] // tile for p in pieces]
+    steps = sum(shares)
+    each = steps // PART
+
+    def place(first, share):
+        return lambda i, order: (jnp.clip(i - first, 0, share - 1), 0)
+
+    specs, first = [], 0
+    for share in shares:
+        specs.append(pl.BlockSpec((tile, D), place(first, share)))
+        first += share
+    extra = []
+    if gain_rows is not None:
+        specs.append(pl.BlockSpec((8, D), lambda i, order: (0, 0)))
+        extra.append(gain_rows)
+    return pl.pallas_call(
+        functools.partial(positions_kernel, shares, gain_rows is not None),
+        grid_spec=pltpu.PrefetchScalarGridSpec(
+            num_scalar_prefetch=1,
+            grid=(steps,),
+            in_specs=specs,
+            out_specs=pl.BlockSpec((tile, D), lambda i, order: (order[i // each] * each + i % each, 0)),
+        ),
+        out_shape=jax.ShapeDtypeStruct((tile * steps, D), bf16),
+        compiler_params=pltpu.CompilerParams(vmem_limit_bytes=32 * 2**20),
+        cost_estimate=pl.CostEstimate(
+            flops=4 * tile * steps * D, bytes_accessed=4 * tile * steps * D, transcendentals=0
+        ),
+        name="all_positions",
+    )(order, *pieces, *extra)
+
+
+def x_parts(blocks):
+    x = lax.axis_index("dp") % 2
     view = blocks.reshape((4, 2) + blocks.shape[1:])
     mine = lax.dynamic_index_in_dim(view, x, 1, False)
-    other = lax.dynamic_index_in_dim(view, 1 - x, 1, False)
-    half = mine.astype(f32) + dp_swap_x(other).astype(f32)
-    total = lax.dynamic_index_in_dim(half, z, 0, False)
-    for steps in range(1, 4):
-        give = lax.dynamic_index_in_dim(half, (z + steps) % 4, 0, False).astype(bf16)
-        total = total + dp_shift_z(give, steps).astype(f32)
-    return total
+    return mine, lax.dynamic_index_in_dim(view, 1 - x, 1, False)
+
+
+def x_halves(blocks):
+    mine, other = x_parts(blocks)
+    return mine, dp_swap_x(other)
+
+
+def z_gives(mine, received):
+    z = lax.axis_index("dp") // 2
+
+    def of(steps):
+        which = (z + steps) % 4
+        a = lax.dynamic_index_in_dim(mine, which, 0, False)
+        return a.astype(f32) + lax.dynamic_index_in_dim(received, which, 0, False).astype(f32)
+
+    return of(0), [of(steps).astype(bf16) for steps in range(1, 4)]
 
 
 def dp_total(value):
@@ -154,35 +312,40 @@
 
 
 def gather_in(pieces):
-    if fast_mesh():
-        own = seq_transpose(pieces)
-        block = own.reshape(-1, own.shape[2])
-        return dp_gather(block).reshape(D, -1)
     full = lax.all_gather(pieces, ("dp", "seq"), axis=1, tiled=True)
     return lax.dynamic_index_in_dim(full, lax.axis_index("seq"), 0, False)
 
 
+def dp_sum(product):
+    return lax.psum_scatter(product, "dp", scatter_dimension=0, tiled=True)
+
+
+def owners_rows(total):
+    return seq_transpose(total.astype(bf16).reshape(PART, -1, total.shape[1])).astype(f32)
+
+
 def scatter_in(grads):
-    columns = grads.shape[1]
-    if fast_mesh():
-        total = dp_scatter(grads.reshape(8, -1, columns))
-        return seq_transpose(total.reshape(PART, -1, columns).astype(bf16)).astype(f32)
     full = jnp.zeros((PART,) + grads.shape, grads.dtype)
     full = lax.dynamic_update_index_in_dim(full, grads, lax.axis_index("seq"), 0)
     return lax.psum_scatter(full, ("dp", "seq"), scatter_dimension=1, tiled=True).astype(f32)
 
 
 def gather_out(rows):
-    if fast_mesh():
-        return dp_gather(rows).reshape(OWN, -1)
     full = lax.all_gather(rows, ("dp", "seq"), axis=0, tiled=True)
     full = full.reshape(STRIPS, PART, LANES, -1)
     return lax.dynamic_index_in_dim(full, lax.axis_index("seq"), 1, False).reshape(OWN, -1)
 
 
+def gather_plainly(conv_pieces, gate_pieces, out_rows, x_block):
+    return (
+        gather_in(conv_pieces),
+        gather_in(gate_pieces),
+        gather_out(out_rows),
+        seq_pieces(x_block),
+    )
+
+
 def scatter_out(grads):
-    if fast_mesh():
-        return dp_scatter(grads.reshape(8, LANES, -1))
     full = jnp.zeros((STRIPS, PART, LANES, grads.shape[1]), grads.dtype)
     full = lax.dynamic_update_index_in_dim(
         full, grads.reshape(STRIPS, LANES, -1), lax.axis_index("seq"), 1
@@ -211,6 +374,127 @@
 
 def sigmoid(v):
     return 0.5 + 0.5 * jnp.tanh(0.5 * v)
+
+
+def bc_forward_kernel(tile_ref, taps_ref, out_ref, padded):
+    length = tile_ref.shape[0]
+    padded[0:8, :] = jnp.zeros((8, LANES), f32)
+    padded[8 : 8 + length, :] = tile_ref[...].astype(bf16).astype(f32)
+    left = lax.broadcasted_iota(jnp.int32, (1, LANES), 1) < OWN_BC
+    for block in range(length // Q):
+        start = block * Q
+        pre = taps_ref[0:1, :] * padded[start + 5 : start + 5 + Q, :]
+        for tap in range(1, CONV):
+            pre = pre + taps_ref[tap : tap + 1, :] * padded[start + 5 + tap : start + 5 + tap + Q, :]
+        act = pre * sigmoid(pre)
+        packed = jnp.where(left, pltpu.roll(act[HALF:], OWN_BC, 1), act[:HALF])
+        out_ref[block * HALF : (block + 1) * HALF, :] = packed.astype(bf16)
+
+
+def bc_forward(dt_tile, taps_tile):
+    length = dt_tile.shape[0]
+    return pl.pallas_call(
+        bc_forward_kernel,
+        out_shape=jax.ShapeDtypeStruct((length // 2, LANES), bf16),
+        scratch_shapes=[pltpu.VMEM((8 + length, LANES), f32)],
+        compiler_params=pltpu.CompilerParams(vmem_limit_bytes=16 * 2**20),
+        cost_estimate=pl.CostEstimate(
+            flops=20 * length * LANES, bytes_accessed=5 * length * LANES, transcendentals=0
+        ),
+        name="bc_forward",
+    )(dt_tile, taps_tile)
+
+
+def tail_kernel(tile_ref, grad_ref, ddt_ref, taps_ref, into_ref, out_ref, sums_ref, padded, dp):
+    del into_ref
+    length = tile_ref.shape[0]
+    padded[0:8, :] = jnp.zeros((8, LANES), f32)
+    padded[8 : 8 + length, :] = tile_ref[...].astype(bf16).astype(f32)
+    dp[length : length + 8, :] = jnp.zeros((8, LANES), f32)
+    lane = lax.broadcasted_iota(jnp.int32, (1, LANES), 1)
+    left = lane < OWN_BC
+    sums_ref[...] = jnp.zeros_like(sums_ref)
+    for block in reversed(range(length // Q)):
+        start = block * Q
+        taken = [padded[start + 5 + tap : start + 5 + tap + Q, :] for tap in range(CONV)]
+        pre = taps_ref[0:1, :] * taken[0]
+        for tap in range(1, CONV):
+            pre = pre + taps_ref[tap : tap + 1, :] * taken[tap]
+        packed = grad_ref[block * HALF : (block + 1) * HALF, :]
+        grad = jnp.concatenate([packed, pltpu.roll(packed, OWN_BC, 1)], axis=0)
+        squashed = sigmoid(pre)
+        d_pre = jnp.where(left, 0.0, grad * squashed * (1.0 + pre * (1.0 - squashed)))
+        dp[start : start + Q, :] = d_pre
+        for tap in range(CONV):
+            sums_ref[tap : tap + 1, :] += jnp.sum(d_pre * taken[tap], axis=0, keepdims=True)
+        d_in = taps_ref[CONV - 1 : CONV, :] * d_pre
+        for tap in range(CONV - 1):
+            first = start + CONV - 1 - tap
+            d_in = d_in + taps_ref[tap : tap + 1, :] * dp[first : first + Q, :]
+        d_dt = jnp.where(lane < OWN_HEADS, ddt_ref[start : start + Q, :], 0.0)
+        out_ref[start : start + Q, :] = jnp.where(left, d_dt, d_in).astype(bf16)
+
+
+def tail_backward(dt_tile, grad, d_dt, taps_tile, into):
+    length = dt_tile.shape[0]
+    whole = lambda i: (0, 0)
+    return pl.pallas_call(
+        tail_kernel,
+        grid=(1,),
+        in_specs=[
+            pl.BlockSpec((length, LANES), whole),
+            pl.BlockSpec((length // 2, LANES), whole),
+            pl.BlockSpec((length, LANES), whole),
+            pl.BlockSpec((8, LANES), whole),
+            pl.BlockSpec(memory_space=pl.ANY),
+        ],
+        out_specs=[
+            pl.BlockSpec((length, LANES), lambda i: (0, STRIPS)),
+            pl.BlockSpec((8, LANES), whole),
+        ],
+        out_shape=[
+            jax.ShapeDtypeStruct(into.shape, bf16),
+            jax.ShapeDtypeStruct((8, LANES), f32),
+        ],
+        input_output_aliases={4: 0},
+        scratch_shapes=[pltpu.VMEM((8 + length, LANES), f32), pltpu.VMEM((8 + length, LANES), f32)],
+        compiler_params=pltpu.CompilerParams(vmem_limit_bytes=24 * 2**20),
+        cost_estimate=pl.CostEstimate(
+            flops=40 * length * LANES, bytes_accessed=14 * length * LANES, transcendentals=0
+        ),
+        name="tail_backward",
+    )(dt_tile, grad, d_dt, taps_tile, into)
+
+
+def keys_and_reads(me, refs):
+    odd, lower = me % 2 == 1, me >= 2
+    p = [ref[...].astype(f32) for ref in refs]
+    r0, r1 = jnp.where(odd, p[1], p[0]), jnp.where(odd, p[0], p[1])
+    r2, r3 = jnp.where(odd, p[3], p[2]), jnp.where(odd, p[2], p[3])
+    q = (
+        jnp.where(lower, r2, r0),
+        jnp.where(lower, r3, r1),
+        jnp.where(lower, r0, r2),
+        jnp.where(lower, r1, r3),
+    )
+    left = lax.broadcasted_iota(jnp.int32, (1, LANES), 1) < OWN_BC
+
+    def join(a, b):
+        top = jnp.where(left, pltpu.roll(a, OWN_BC, 1), b)
+        bottom = jnp.where(left, a, pltpu.roll(b, OWN_BC, 1))
+        return jnp.concatenate([top, bottom], axis=0).astype(bf16)
+
+    return join(q[0], q[1]), join(q[2], q[3])
+
+
+def give_back(me, d_keys, d_reads, out_ref):
+    left = lax.broadcasted_iota(jnp.int32, (1, LANES), 1) < OWN_BC
+    for pair, array in enumerate((d_keys, d_reads)):
+        top, bottom = array[:HALF], array[HALF:]
+        low = jnp.where(left, bottom, pltpu.roll(top, OWN_BC, 1))
+        high = jnp.where(left, pltpu.roll(bottom, OWN_BC, 1), top)
+        out_ref[jnp.bitwise_xor(me, 2 * pair)] = low.astype(bf16)
+        out_ref[jnp.bitwise_xor(me, 2 * pair + 1)] = high.astype(bf16)
 
 
 def decay_terms(dt_ref, rows_ref):
@@ -227,7 +511,7 @@
 
 
 def forward_kernel(
-    ci_ref, bc_ref, dt_ref, cw_ref, rows_ref, skip_ref, y_ref, act_ref, s_ref, state, xf
+    me_ref, ci_ref, b0, b1, b2, b3, dt_ref, cw_ref, rows_ref, skip_ref, y_ref, act_ref, s_ref, state, xf
 ):
     @pl.when(pl.program_id(0) == 0)
     def _():
@@ -244,8 +528,7 @@
     e_run = jnp.exp2(running)
     w_end = jnp.exp2(end - shifted)
     e_end = jnp.exp2(end)
-    keys = bc_ref[:, :STATE]
-    reads = bc_ref[:, STATE:]
+    keys, reads = keys_and_reads(me_ref[0], (b0, b1, b2, b3))
     keys_t = keys.T
     cb = dot_nt(reads, keys)
     causal = lax.broadcasted_iota(jnp.int32, (HALF, HALF), 0) >= lax.broadcasted_iota(
@@ -292,50 +575,57 @@
         ) + dot_nn(keys_t, weighted)
 
 
-def recurrence_forward(conv_in, bc, dt_tile, taps, rows, skip_row):
+def recurrence_forward(me, conv_in, bc, dt_tile, taps, rows, skip_row):
     length = conv_in.shape[0]
     blocks = length // Q
-    whole = lambda i: (0, 0)
-    along = lambda i: (i, 0)
+    whole = lambda i, me: (0, 0)
+    along = lambda i, me: (i, 0)
     return pl.pallas_call(
         forward_kernel,
-        grid=(blocks,),
-        in_specs=[
-            pl.BlockSpec((Q, OWN), along),
-            pl.BlockSpec((Q, 2 * STATE), along),
-            pl.BlockSpec((Q, LANES), along),
-            pl.BlockSpec((8, OWN), whole),
-            pl.BlockSpec((8, LANES), whole),
-            pl.BlockSpec((8, OWN), whole),
-        ],
-        out_specs=[
-            pl.BlockSpec((Q, OWN), along),
-            pl.BlockSpec((Q, OWN), along),
-            pl.BlockSpec((1, STATE, OWN), lambda i: (i, 0, 0)),
-        ],
+        grid_spec=pltpu.PrefetchScalarGridSpec(
+            num_scalar_prefetch=1,
+            grid=(blocks,),
+            in_specs=[pl.BlockSpec((Q, OWN), along)]
+            + [pl.BlockSpec((HALF, LANES), along)] * PART
+            + [
+                pl.BlockSpec((Q, LANES), along),
+                pl.BlockSpec((8, OWN), whole),
+                pl.BlockSpec((8, LANES), whole),
+                pl.BlockSpec((8, OWN), whole),
+            ],
+            out_specs=[
+                pl.BlockSpec((Q, OWN), along),
+                pl.BlockSpec((Q, OWN), along),
+                pl.BlockSpec((1, STATE, OWN), lambda i, me: (i, 0, 0)),
+            ],
+            scratch_shapes=[pltpu.VMEM((STATE, OWN), f32), pltpu.VMEM((Q + 8, OWN), f32)],
+        ),
         out_shape=[
             jax.ShapeDtypeStruct((length, OWN), f32),
             jax.ShapeDtypeStruct((length, OWN), bf16),
             jax.ShapeDtypeStruct((blocks, STATE, OWN), bf16),
         ],
-        scratch_shapes=[pltpu.VMEM((STATE, OWN), f32), pltpu.VMEM((Q + 8, OWN), f32)],
         compiler_params=pltpu.CompilerParams(
             dimension_semantics=("arbitrary",), vmem_limit_bytes=40 * 2**20
         ),
         cost_estimate=pl.CostEstimate(
-            flops=12 * 10**9, bytes_accessed=24 * 2**20, transcendentals=10**7
+            flops=30 * 10**9, bytes_accessed=2**24, transcendentals=10**7
         ),
         name="recurrence_forward",
-    )(conv_in, bc, dt_tile, taps, rows, skip_row)
+    )(me, conv_in, *bc, dt_tile, taps, rows, skip_row)
 
 
 def backward_kernel(
+    me_ref,
     ci_ref,
     prev_ref,
     act_ref,
     dy_ref,
     y_ref,
-    bc_ref,
+    b0,
+    b1,
+    b2,
+    b3,
     dt_ref,
     s_ref,
     cw_ref,
@@ -382,8 +672,7 @@
     e_run = jnp.exp2(running)
     w_end = jnp.exp2(end - shifted)
     e_end = jnp.exp2(end)
-    keys = bc_ref[:, :STATE]
-    reads = bc_ref[:, STATE:]
+    keys, reads = keys_and_reads(me_ref[0], (b0, b1, b2, b3))
     reads_t = reads.T
     cbt = dot_nt(keys, reads)
     ahead = lax.broadcasted_iota(jnp.int32, (HALF, HALF), 0) <= lax.broadcasted_iota(
@@ -456,8 +745,7 @@
     dcb_t = dcb[...]
     d_keys = dot_nn(dcb_t.astype(bf16), reads) + dot_nt(wx[...], back16[...])
     d_reads = dot_nn(dcb_t.T.astype(bf16), keys) + dot_nt(edy[...], s_ref[0])
-    dbc_ref[:, :STATE] = d_keys.astype(dbc_ref.dtype)
-    dbc_ref[:, STATE:] = d_reads.astype(dbc_ref.dtype)
+    give_back(me_ref[0], d_keys, d_reads, dbc_ref)
     unit = lax.broadcasted_iota(jnp.int32, (OWN, LANES), 0)
     head = lax.broadcasted_iota(jnp.int32, (OWN, LANES), 1)
     member = jnp.where(unit // HEAD_DIM == head, 1.0, 0.0)
@@ -480,74 +768,189 @@
     grow_ref[1:2, :] += jnp.sum(d_log * rate * steps, axis=0, keepdims=True)
 
 
-def recurrence_backward(conv_in, act, dy, y, bc, dt_tile, entry, taps, rows, skip_row):
+def recurrence_backward(me, conv_in, act, dy, y, bc, dt_tile, entry, taps, rows, skip_row):
     length = conv_in.shape[0]
     blocks = length // Q
-    whole = lambda i: (0, 0)
-    along = lambda i: (blocks - 1 - i, 0)
-    previous = lambda i: (jnp.maximum((blocks - 1 - i) * (Q // 16) - 1, 0), 0)
+    whole = lambda i, me: (0, 0)
+    along = lambda i, me: (blocks - 1 - i, 0)
+    previous = lambda i, me: (jnp.maximum((blocks - 1 - i) * (Q // 16) - 1, 0), 0)
     return pl.pallas_call(
         backward_kernel,
-        grid=(blocks,),
+        grid_spec=pltpu.PrefetchScalarGridSpec(
+            num_scalar_prefetch=1,
+            grid=(blocks,),
+            in_specs=[
+                pl.BlockSpec((Q, OWN), along),
+                pl.BlockSpec((16, OWN), previous),
+                pl.BlockSpec((Q, OWN), along),
+                pl.BlockSpec((Q, OWN), along),
+                pl.BlockSpec((Q, OWN), along),
+            ]
+            + [pl.BlockSpec((HALF, LANES), along)] * PART
+            + [
+                pl.BlockSpec((Q, LANES), along),
+                pl.BlockSpec((1, STATE, OWN), lambda i, me: (blocks - 1 - i, 0, 0)),
+                pl.BlockSpec((8, OWN), whole),
+                pl.BlockSpec((8, LANES), whole),
+                pl.BlockSpec((8, OWN), whole),
+            ],
+            out_specs=[
+                pl.BlockSpec((Q, OWN), along),
+                pl.BlockSpec((PART, HALF, LANES), lambda i, me: (0, blocks - 1 - i, 0)),
+                pl.BlockSpec((Q, LANES), along),
+                pl.BlockSpec((8, OWN), whole),
+                pl.BlockSpec((8, LANES), whole),
+            ],
+            scratch_shapes=[
+                pltpu.VMEM((STATE, OWN), f32),
+                pltpu.VMEM((STATE, OWN), bf16),
+                pltpu.VMEM((Q + 8, OWN), f32),
+                pltpu.VMEM((Q + 8, OWN), f32),
+                pltpu.VMEM((Q, OWN), bf16),
+                pltpu.VMEM((Q, OWN), bf16),
+                pltpu.VMEM((Q, Q), f32),
+                pltpu.VMEM((Q, OWN), bf16),
+                pltpu.VMEM((Q, OWN), bf16),
+                pltpu.VMEM((Q, OWN), bf16),
+                pltpu.VMEM((Q, OWN), bf16),
+                pltpu.VMEM((8, OWN), f32),
+            ],
+        ),
+        out_shape=[
+            jax.ShapeDtypeStruct((length, CONV_COLS), bf16),
+            jax.ShapeDtypeStruct((PART, length // 2, LANES), bf16),
+            jax.ShapeDtypeStruct((length, LANES), f32),
+            jax.ShapeDtypeStruct((8, OWN), f32),
+            jax.ShapeDtypeStruct((8, LANES), f32),
+        ],
+        compiler_params=pltpu.CompilerParams(
+            dimension_semantics=("arbitrary",), vmem_limit_bytes=48 * 2**20
+        ),
+        cost_estimate=pl.CostEstimate(
+            flops=70 * 10**9, bytes_accessed=2**24, transcendentals=10**7
+        ),
+        name="recurrence_backward",
+    )(me, conv_in, conv_in, act, dy, y, *bc, dt_tile, entry, taps, rows, skip_row)
+
+
+def gate_forward_kernel(n_ref, t_ref, y_ref, wg_ref, wo_ref, row_ref, z_ref, d_ref, sums_ref):
+    z = dot_nn(n_ref[...], wg_ref[...]) * row_ref[1:2, :]
+    d = dot_nt(t_ref[...], wo_ref[...])
+    z_ref[...] = z
+    d_ref[...] = d
+    gated = y_ref[...] * (z * sigmoid(z))
+    squares = jnp.sum(gated * gated, axis=1, keepdims=True)
+    cross = jnp.sum(d * row_ref[0:1, :] * gated, axis=1, keepdims=True)
+    lane = lax.broadcasted_iota(jnp.int32, (1, LANES), 1)
+    both = jnp.where(lane == 0, squares, jnp.where(lane == 1, cross, 0.0))
+    sums_ref[...] = both.T[0:8, :]
+
+
+def gate_forward(normed, cot, y, w_gate, w_o, row):
+    length = normed.shape[0]
+    whole = lambda i: (0, 0)
+    along = lambda i: (i, 0)
+    return pl.pallas_call(
+        gate_forward_kernel,
+        grid=(length // Q,),
         in_specs=[
+            pl.BlockSpec((Q, D), along),
+            pl.BlockSpec((Q, D), along),
             pl.BlockSpec((Q, OWN), along),
-            pl.BlockSpec((16, OWN), previous),
-            pl.BlockSpec((Q, OWN), along),
-            pl.BlockSpec((Q, OWN), along),
-            pl.BlockSpec((Q, OWN), along),
-            pl.BlockSpec((Q, 2 * STATE), along),
-            pl.BlockSpec((Q, LANES), along),
-            pl.BlockSpec((1, STATE, OWN), lambda i: (blocks - 1 - i, 0, 0)),
-            pl.BlockSpec((8, OWN), whole),
-            pl.BlockSpec((8, LANES), whole),
+            pl.BlockSpec((D, OWN), whole),
+            pl.BlockSpec((OWN, D), whole),
             pl.BlockSpec((8, OWN), whole),
         ],
         out_specs=[
             pl.BlockSpec((Q, OWN), along),
-            pl.BlockSpec((Q, 2 * STATE), along),
-            pl.BlockSpec((Q, LANES), along),
-            pl.BlockSpec((8, OWN), whole),
-            pl.BlockSpec((8, LANES), whole),
+            pl.BlockSpec((Q, OWN), along),
+            pl.BlockSpec((8, Q), lambda i: (0, i)),
         ],
         out_shape=[
-            jax.ShapeDtypeStruct((length, OWN), bf16),
-            jax.ShapeDtypeStruct((length, 2 * STATE), bf16),
-            jax.ShapeDtypeStruct((length, LANES), f32),
-            jax.ShapeDtypeStruct((8, OWN), f32),
-            jax.ShapeDtypeStruct((8, LANES), f32),
+            jax.ShapeDtypeStruct((length, OWN), f32),
+            jax.ShapeDtypeStruct((length, OWN), f32),
+            jax.ShapeDtypeStruct((8, length), f32),
         ],
-        scratch_shapes=[
-            pltpu.VMEM((STATE, OWN), f32),
-            pltpu.VMEM((STATE, OWN), bf16),
-            pltpu.VMEM((Q + 8, OWN), f32),
-            pltpu.VMEM((Q + 8, OWN), f32),
-            pltpu.VMEM((Q, OWN), bf16),
-            pltpu.VMEM((Q, OWN), bf16),
-            pltpu.VMEM((Q, Q), f32),
-            pltpu.VMEM((Q, OWN), bf16),
-            pltpu.VMEM((Q, OWN), bf16),
-            pltpu.VMEM((Q, OWN), bf16),
-            pltpu.VMEM((Q, OWN), bf16),
-            pltpu.VMEM((8, OWN), f32),
+        compiler_params=pltpu.CompilerParams(vmem_limit_bytes=48 * 2**20),
+        cost_estimate=pl.CostEstimate(
+            flops=4 * length * D * OWN, bytes_accessed=2**25, transcendentals=length * OWN
+        ),
+        name="gate_forward",
+    )(normed, cot, y, w_gate, w_o, row)
+
+
+def gate_backward_kernel(y_ref, z_ref, d_ref, sums_ref, row_ref, out_ref, dy_ref, dz_ref, gain_ref):
+    @pl.when(pl.program_id(0) == 0)
+    def _():
+        gain_ref[...] = jnp.zeros_like(gain_ref)
+
+    units = row_ref[2:3, 0:1]
+    sums = sums_ref[...]
+    inverse = lax.rsqrt(sums[0:1, :] / units + epsilon)
+    pull = inverse * inverse * inverse * sums[1:2, :] / units
+    row = lax.broadcasted_iota(jnp.int32, (LANES, 1), 0)
+    columns = jnp.where(row == 0, inverse, jnp.where(row == 1, pull, 0.0)).T
+    inverse, pull = columns[:, 0:1], columns[:, 1:2]
+    for strip in range(STRIPS):
+        at = slice(strip * LANES, (strip + 1) * LANES)
+        y, z, d = y_ref[:, at], z_ref[:, at], d_ref[:, at]
+        gain = row_ref[0:1, at]
+        squashed = sigmoid(z)
+        act = z * squashed
+        gated = y * act
+        normalized = gated * inverse
+        out_ref[:, at] = (normalized * gain).astype(bf16)
+        gain_ref[0:1, at] += jnp.sum(d * normalized, axis=0, keepdims=True)
+        d_gated = inverse * (d * gain) - gated * pull
+        dy_ref[:, at] = (d_gated * act).astype(bf16)
+        dz_ref[:, at] = (d_gated * y * squashed * (1.0 + z * (1.0 - squashed))).astype(bf16)
+
+
+def gate_backward(y, z, d, sums, row):
+    length = y.shape[0]
+    whole = lambda i: (0, 0)
+    along = lambda i: (i, 0)
+    return pl.pallas_call(
+        gate_backward_kernel,
+        grid=(length // Q,),
+        in_specs=[pl.BlockSpec((Q, OWN), along)] * 3
+        + [pl.BlockSpec((8, Q), lambda i: (0, i)), pl.BlockSpec((8, OWN), whole)],
+        out_specs=[pl.BlockSpec((Q, OWN), along)] * 3 + [pl.BlockSpec((8, OWN), whole)],
+        out_shape=[jax.ShapeDtypeStruct((length, OWN), bf16)] * 3
+        + [jax.ShapeDtypeStruct((8, OWN), f32)],
+        compiler_params=pltpu.CompilerParams(vmem_limit_bytes=32 * 2**20),
+        cost_estimate=pl.CostEstimate(
+            flops=30 * length * OWN, bytes_accessed=18 * length * OWN, transcendentals=length * OWN
+        ),
+        name="gate_backward",
+    )(y, z, d, sums, row)
+
+
+def input_gradient_kernel(z_ref, p_ref, wg_ref, wc_ref, out_ref):
+    out_ref[...] = (dot_nt(z_ref[...], wg_ref[...]) + dot_nt(p_ref[...], wc_ref[...])).astype(bf16)
+
+
+def input_gradient(d_z, d_project, w_gate, w_conv):
+    length = d_z.shape[0]
+    whole = lambda i: (0, 0)
+    along = lambda i: (i, 0)
+    return pl.pallas_call(
+        input_gradient_kernel,
+        grid=(length // Q,),
+        in_specs=[
+            pl.BlockSpec((Q, OWN), along),
+            pl.BlockSpec((Q, CONV_COLS), along),
+            pl.BlockSpec((D, OWN), whole),
+            pl.BlockSpec((D, CONV_COLS), whole),
         ],
-        compiler_params=pltpu.CompilerParams(
-            dimension_semantics=("arbitrary",), vmem_limit_bytes=48 * 2**20
-        ),
+        out_specs=pl.BlockSpec((Q, D), along),
+        out_shape=jax.ShapeDtypeStruct((length, D), bf16),
+        compiler_params=pltpu.CompilerParams(vmem_limit_bytes=48 * 2**20),
         cost_estimate=pl.CostEstimate(
-            flops=30 * 10**9, bytes_accessed=36 * 2**20, transcendentals=2 * 10**7
-        ),
-        name="recurrence_backward",
-    )(conv_in, conv_in, act, dy, y, bc, dt_tile, entry, taps, rows, skip_row)
-
-
-def shifted_rows(array, steps):
-    length = array.shape[0]
-    if steps == 0:
-        return array
-    zeros = jnp.zeros((abs(steps),) + array.shape[1:], array.dtype)
-    if steps > 0:
-        return jnp.concatenate([zeros, array[: length - steps]], axis=0)
-    return jnp.concatenate([array[-steps:], zeros], axis=0)
+            flops=200 * 10**9, bytes_accessed=2**25, transcendentals=0
+        ),
+        name="input_gradient",
+    )(d_z, d_project, w_gate, w_conv)
 
 
 def per_device(
@@ -574,28 +977,26 @@
     unit_used = block * LANES < used_units
     head_used = ((jnp.arange(OWN_HEADS) // 2 * PART + me) * LANES < used_units).astype(f32)
 
+    every = lambda a: jnp.broadcast_to(a[None], (PART,) + a.shape)
     tail = jnp.concatenate(
         [
             heads_by_owner(w_dt),
-            jnp.broadcast_to(norm_gain[None, :, None], (PART, rows_in, 1)),
-            jnp.zeros((PART, rows_in, LANES - OWN_HEADS - 1 - OWN_BC), bf16),
+            every(norm_gain[:, None]),
+            every(gate_gain.reshape(2, rows_in).T),
+            jnp.zeros((PART, rows_in, LANES - OWN_HEADS - 3 - OWN_BC), bf16),
             w_in[:, 2 * INNER :].reshape(rows_in, PART, OWN_BC).transpose(1, 0, 2),
         ],
         axis=2,
     )
     conv_pieces = jnp.concatenate([by_owner(w_in[:, INNER : 2 * INNER]), tail], axis=2)
     gate_pieces = by_owner(w_in[:, :INNER])
-    out_rows = jnp.concatenate(
-        [w_out, jnp.pad(gate_gain[:, None], ((0, 0), (0, LANES - 1)))], axis=1
-    )
-
-    x_all = seq_gather(hidden_in[0]).reshape(length, D)
-    w_conv = gather_in(conv_pieces)
-    w_gate = gather_in(gate_pieces)
-    out_full = gather_out(out_rows)
-    cot_all = seq_gather(grad_out[0]).reshape(length, D)
-    w_o = out_full[:, :D]
-    gate_row = out_full[:, D].astype(f32)[None, :]
+    gather = gather_everything if fast_mesh() else gather_plainly
+    w_conv, w_gate, w_o, x_pieces = gather(conv_pieces, gate_pieces, w_out, hidden_in[0])
+    order = jnp.stack([me, me ^ 1, me ^ 2, me ^ 3]).astype(jnp.int32)
+    gate_all = w_conv[:, OWN + OWN_HEADS + 1 : OWN + OWN_HEADS + 3]
+    gate_all = gate_all.reshape(D // rows_in, rows_in, 2).transpose(0, 2, 1)
+    gate_row = lax.dynamic_index_in_dim(gate_all.reshape(STRIPS, PART, LANES), me, 1, False)
+    gate_row = gate_row.reshape(1, OWN).astype(f32)
     gain_row = w_conv[:, OWN + OWN_HEADS].astype(f32)[None, :]
 
     def own_heads(array):
@@ -614,74 +1015,95 @@
     ).reshape(CONV, OWN)
     taps = jnp.pad(taps.astype(f32), ((0, 8 - CONV), (0, 0)))
     taps_bc = lax.dynamic_slice_in_dim(conv_weight[:, INNER:], me * OWN_BC, OWN_BC, 1).astype(f32)
-
-    x_float = x_all.astype(f32)
-    inverse_rms = lax.rsqrt(jnp.mean(x_float * x_float, axis=1, keepdims=True) + epsilon)
-    normed = (x_float * inverse_rms * gain_row).astype(bf16)
+    taps_tile = jnp.pad(taps_bc, ((0, 8 - CONV), (LANES - OWN_BC, 0)))
+    place_me = me.astype(jnp.int32).reshape(1)
+
+    normed = all_positions(x_pieces, order, jnp.broadcast_to(gain_row, (8, D)))
     dt_tile = dot_nn(normed, w_conv[:, OWN:])
-    conv_bc = dt_tile[:, LANES - OWN_BC :].astype(bf16)
-    conv_bc_float = conv_bc.astype(f32)
-    pre_bc = sum(
-        taps_bc[tap] * shifted_rows(conv_bc_float, CONV - 1 - tap) for tap in range(CONV)
-    )
-    act_bc = (pre_bc * sigmoid(pre_bc)).astype(bf16)
-    bc = seq_gather(act_bc).transpose(1, 0, 2).reshape(length, 2 * STATE)
+    bc = seq_pieces(bc_forward(dt_tile, taps_tile))
+    cot_across = xor_seq(tie(grad_out[0], bc[2])[0], 2)
     conv_in = jnp.where(unit_used, dot_nn(normed, w_conv[:, :OWN]), 0.0).astype(bf16)
-    y, act, entry = recurrence_forward(conv_in, bc, dt_tile, taps, rows, skip_row)
-    z = jnp.where(unit_used, dot_nn(normed, w_gate), 0.0)
-    d_rounded = dot_nt(cot_all, w_o)
-    squashed = sigmoid(z)
-    gate_act = z * squashed
-    gated = y * gate_act
-    e_gate = d_rounded * gate_row
-    sums = jnp.stack(
-        [jnp.sum(gated * gated, axis=1), jnp.sum(e_gate * gated, axis=1)]
-    ).reshape(2, length // LANES, LANES)
-    sums = seq_total(sums).reshape(2, length)
-    inverse_gate = lax.rsqrt(sums[0] / units_float + epsilon)
-    pull = (inverse_gate**3 * sums[1] / units_float)[:, None]
-    inverse_gate = inverse_gate[:, None]
-    normalized = gated * inverse_gate
-    rounded_out = (normalized * gate_row).astype(bf16)
-    grad_gate_local = jnp.sum(d_rounded * normalized, axis=0)
-    d_gated = inverse_gate * e_gate - gated * pull
-    d_y = (d_gated * gate_act).astype(bf16)
-    d_z = (d_gated * y * squashed * (1.0 + z * (1.0 - squashed))).astype(bf16)
-
-    grad_w_out = scatter_out(dot_tn(rounded_out, cot_all).astype(bf16))
+    if fast_mesh():
+        w_o[1], conv_in = tie(w_o[1], conv_in)
+        w_o.append(dp_swap_x(w_o[1]))
+    y, act, entry = recurrence_forward(place_me, conv_in, bc, dt_tile, taps, rows, skip_row)
+    if fast_mesh():
+        cot_across, *w_o[2:] = after([cot_across, *w_o[2:]], [entry])
+        w_o += [dp_swap_x(w_o[2]), dp_swap_x(w_o[3])]
+        w_o = assemble(w_o, out_places(), 512)
+    cot_pieces = (grad_out[0], xor_seq(grad_out[0], 1), cot_across, xor_seq(cot_across, 1))
+    cot_all = all_positions(cot_pieces, order)
+    row = jnp.concatenate(
+        [
+            gate_row,
+            unit_used.astype(f32)[None, :],
+            jnp.full((6, OWN), units_float),
+        ],
+        axis=0,
+    )
+    z, d_rounded, sums = gate_forward(normed, cot_all, y, w_gate, w_o, row)
+    rounded_out, d_y, d_z, grad_gate_rows = gate_backward(y, z, d_rounded, seq_total(sums), row)
+    grad_gate_local = grad_gate_rows[0]
+
+    out_product = dot_tn(rounded_out, cot_all).astype(bf16)
+    gate_product = dot_tn(normed, d_z).astype(bf16)
+    d_y, out_product, gate_product = tie(d_y, out_product, gate_product)
+    if fast_mesh():
+        out_mine, out_got = x_halves(out_product.reshape(8, LANES, D))
+        gate_total = dp_sum(gate_product)
+
+    d_values, d_bc, d_dt, g_conv, g_rows = recurrence_backward(
+        place_me, conv_in, act, d_y, y, bc, dt_tile, entry, taps, rows, skip_row
+    )
+    if fast_mesh():
+        d_values, d_bc, out_got, rounded_out = tie(d_values, d_bc, out_got, rounded_out)
     branch = dot_nn(rounded_out, w_o).astype(bf16).reshape(PART, tokens, D)
+    branch_mine, branch_got = core_halves(branch)
+    d_project, g_tail = tail_backward(
+        dt_tile, seq_scatter_relative(d_bc), d_dt, taps_tile, d_values
+    )
+    g_skip = jnp.sum(g_conv[4].reshape(OWN_HEADS, HEAD_DIM), axis=1)
+    small = jnp.concatenate(
+        [
+            g_conv[:CONV].reshape(-1),
+            g_tail[:CONV, LANES - OWN_BC :].reshape(-1),
+            pad_heads(g_rows[0, :OWN_HEADS]),
+            pad_heads(g_rows[1, :OWN_HEADS]),
+            pad_heads(g_skip),
+            grad_gate_local,
+        ]
+    )
+    count = small.shape[0]
+    padded = -(-count // (8 * LANES)) * 8 * LANES
+    small = jnp.pad(small, (0, padded - count)).reshape(-1, LANES)
+    if fast_mesh():
+        conv_product = dot_tn(normed, d_project).astype(bf16)
+        d_project, conv_product, out_got = tie(d_project, conv_product, out_got)
+        conv_total = dp_sum(conv_product)
+        out_keep, out_gives = z_gives(out_mine, out_got)
+        out_parts = [dp_shift_z(give, steps + 1) for steps, give in enumerate(out_gives)]
+    branch_keep, branch_give = halves_sum(branch_mine, branch_got)
+    branch_across = xor_seq(branch_give, 2)
+    d_normed = input_gradient(d_z, d_project, w_gate, w_conv)
+    if fast_mesh():
+        *out_parts, branch_across, d_normed = tie(*out_parts, branch_across, d_normed)
+        grad_w_out = out_keep + sum(part.astype(f32) for part in out_parts)
+    else:
+        grad_w_out = scatter_out(out_product)
+    mine, got = core_halves(d_normed.reshape(PART, tokens, D))
+    keep, give = halves_sum(mine, got)
+    small, give = tie(small, give)
+    across = xor_seq(give, 2)
+    d_own = keep + across.astype(f32)
+    if fast_mesh():
+        (conv_total,) = after([conv_total], [across])
+        grad_gate_in = owners_rows(gate_total)
+        grad_conv_in = owners_rows(conv_total)
+    else:
+        grad_gate_in = scatter_in(gate_product)
+        grad_conv_in = scatter_in(dot_tn(normed, d_project).astype(bf16))
     x_own = hidden_in[0].astype(f32)
-    hidden_out = (x_own + seq_scatter(branch)).astype(bf16)[None]
-    grad_gate_in = scatter_in(dot_tn(normed, d_z).astype(bf16))
-
-    d_conv_in, d_bc, d_dt, g_conv, g_rows = recurrence_backward(
-        conv_in, act, d_y, y, bc, dt_tile, entry, taps, rows, skip_row
-    )
-    d_act_bc = seq_scatter(d_bc.reshape(length, PART, OWN_BC).transpose(1, 0, 2))
-    squashed_bc = sigmoid(pre_bc)
-    d_pre_bc = d_act_bc * squashed_bc * (1.0 + pre_bc * (1.0 - squashed_bc))
-    g_conv_bc = jnp.stack(
-        [
-            jnp.sum(d_pre_bc * shifted_rows(conv_bc_float, CONV - 1 - tap), axis=0)
-            for tap in range(CONV)
-        ]
-    )
-    d_conv_bc = sum(
-        taps_bc[tap] * shifted_rows(d_pre_bc, tap - (CONV - 1)) for tap in range(CONV)
-    ).astype(bf16)
-    d_project = jnp.concatenate(
-        [
-            d_conv_in,
-            d_dt[:, :OWN_HEADS].astype(bf16),
-            jnp.zeros((length, LANES - OWN_HEADS - OWN_BC), bf16),
-            d_conv_bc,
-        ],
-        axis=1,
-    )
-    grad_conv_in = scatter_in(dot_tn(normed, d_project).astype(bf16))
-    d_normed = dot_nt(d_z, w_gate) + dot_nt(d_project, w_conv)
-    grad_norm_local = jnp.sum(d_normed * (x_float * inverse_rms), axis=0)
-    d_own = seq_scatter(d_normed.astype(bf16).reshape(PART, tokens, D))
+    hidden_out = (x_own + branch_keep + branch_across.astype(f32)).astype(bf16)[None]
     own_rms = lax.rsqrt(jnp.mean(x_own * x_own, axis=1, keepdims=True) + epsilon)
     d_scaled = d_own * gain_row
     d_input = own_rms * d_scaled - x_own * own_rms**3 * jnp.mean(
@@ -689,22 +1111,7 @@
     )
     grad_in = (grad_out[0].astype(f32) + d_input).astype(bf16)[None]
 
-    g_skip = jnp.sum(g_conv[4].reshape(OWN_HEADS, HEAD_DIM), axis=1)
-    small = jnp.concatenate(
-        [
-            g_conv[:CONV].reshape(-1),
-            g_conv_bc.reshape(-1),
-            pad_heads(g_rows[0, :OWN_HEADS]),
-            pad_heads(g_rows[1, :OWN_HEADS]),
-            pad_heads(g_skip),
-            grad_norm_local,
-            grad_gate_local,
-        ]
-    )
-    count = small.shape[0]
-    padded = -(-count // (8 * LANES)) * 8 * LANES
-    small = jnp.pad(small, (0, padded - count)).reshape(-1, LANES)
-    every = seq_gather(dp_total(small)).reshape(PART, padded)
+    every = jnp.stack(by_partner(seq_pieces(dp_total(small)))).reshape(PART, padded)
     start = 0
 
     def take(size):
@@ -715,21 +1122,18 @@
     all_conv = take(CONV * OWN).reshape(PART, CONV, OWN)
     all_conv_bc = take(CONV * OWN_BC).reshape(PART, CONV, OWN_BC)
     head_sums = [heads_from_owner(take(LANES)[:, None, :OWN_HEADS]).reshape(HEADS) for _ in range(3)]
-    grad_norm = jnp.sum(take(D), axis=0)
     grad_gate = lax.dynamic_index_in_dim(take(OWN), me, 0, False)
     grad_conv = jnp.concatenate(
         [from_owner(all_conv), all_conv_bc.transpose(1, 0, 2).reshape(CONV, 2 * STATE)], axis=1
     )
     place = lax.axis_index(("dp", "seq"))
-    norm_rows = norm_gain.shape[0]
-    grad_norm_gain = lax.dynamic_slice_in_dim(grad_norm, place * norm_rows, norm_rows, 0)
     gate_rows = gate_gain.shape[0]
     if gate_rows == LANES:
         grad_gate_gain = lax.dynamic_slice_in_dim(
             grad_gate, lax.axis_index("dp") * gate_rows, gate_rows, 0
         )
     else:
-        start = CONV * OWN + CONV * OWN_BC + 3 * LANES + D
+        start = CONV * OWN + CONV * OWN_BC + 3 * LANES
         whole_gate = from_owner(take(OWN)[:, None, :]).reshape(INNER)
         grad_gate_gain = lax.dynamic_slice_in_dim(whole_gate, place * gate_rows, gate_rows, 0)
 
@@ -742,6 +1146,10 @@
         axis=1,
     )
     grad_w_dt = heads_from_owner(grad_conv_in[:, :, OWN : OWN + OWN_HEADS])
+    grad_norm_gain = (
+        jnp.sum(w_in.astype(f32) * grad_w_in, axis=1)
+        + jnp.sum(w_dt.astype(f32) * grad_w_dt, axis=1)
+    ) / norm_gain.astype(f32)
     return (
         hidden_out,
         grad_in,

time: 1190 us -> 692 us (0.58)
  local copies, waits for them, and re-layouts: 438 us -> 82.6 us
  waiting for transfers between devices: 344 us -> 240 us
  Pallas kernels: 91 us -> 176 us
  matrix products: 153 us -> 75.8 us
  other arithmetic: 88 us -> 45.7 us
  starting transfers between devices: 59.5 us -> 42.4 us
  between operations: 2.99 us -> 16.1 us
    dynamic_update_slice x52 -> x0, local copies, waits for them, and re-layouts: 309 us -> none  [the longest x12 144 us: dp_gather(): lax.dynamic_update_index_in_dim(out, dp_swap_x(piece), source * 2 + 1 - x...]
    ppermute x21 -> x9, waiting for transfers between devices: 196 us -> 78.2 us  [dp_shift_z(): return lax.ppermute(value, 'dp', pairs)]
    pallas_call x2 -> x22, Pallas kernels: 91 us -> 176 us  [the longest x1 60.6 us: recurrence_backward(): pl.pallas_call(backward_kernel, grid_spec=pltpu.PrefetchScalarGridSpec(nu...]
    dot_general x3 -> x0, matrix products: 60.8 us -> none  [dot_nt(): lax.dot_general(a, b, (((1,), (1,)), ((), ())), preferred_element_type=f32)]
    broadcast_in_dim x22 -> x5, local copies, waits for them, and re-layouts: 45.4 us -> 0.1 us  [the longest x2 0.09 us: per_device(): every = lambda a: jnp.broadcast_to(a[None], (PART,) + a.shape)]
    convert_element_type x11 -> x6, other arithmetic: 38.6 us -> 12.5 us  [the longest x2 9.05 us: halves_sum(): return (of(row), of(1 - row).astype(bf16))]
    ppermute x32 -> x30, waiting for transfers between devices: 99.4 us -> 121 us  [xor_seq(): return lax.ppermute(value, 'seq', [(s, s ^ bits) for s in range(PART)])]
    unnamed x121 -> x125, local copies, waits for them, and re-layouts: 23.3 us -> 43.1 us
  transfers between devices with their start and end apart: 69 -> 49, of which waited for: 27 -> 23; matrix products, arithmetic and copies ran while one was open for 51% -> 17% of each run, Pallas kernels for 5% -> 20%
where the time goes in v2:
time: 692 us; the launch traced here: 679 us
  waiting for transfers between devices  240 us (35%)
  Pallas kernels  176 us (25%)
  local copies, waits for them, and re-layouts  82.6 us (12%)
  matrix products  75.8 us (11%)
  other arithmetic  45.7 us (7%)
  starting transfers between devices  42.4 us (6%)
  between operations  16.1 us (2%)
    ppermute x30, waiting for transfers between devices, xor_seq(): return lax.ppermute(value, 'seq', [(s, s ^ bits) for s in range(PART)])  121 us
    ppermute x9, waiting for transfers between devices, dp_shift_z(): return lax.ppermute(value, 'dp', pairs)  78.2 us
    pallas_call x1, Pallas kernels, recurrence_backward(): pl.pallas_call(backward_kernel, grid_spec=pltpu.PrefetchScalarGridSpec(nu...  60.6 us
    dot_general x3, matrix products, dot_tn(): lax.dot_general(a, b, (((0,), (0,)), ((), ())), preferred_element_type=f32)  45.4 us
    unnamed x125, local copies, waits for them, and re-layouts  43.1 us
    ppermute x6, waiting for transfers between devices, dp_swap_x(): return lax.ppermute(value, 'dp', [(d, d ^ 1) for d in range(8)])  34.5 us
    pallas_call x1, Pallas kernels, recurrence_forward(): pl.pallas_call(forward_kernel, grid_spec=pltpu.PrefetchScalarGridSpec(num...  31 us
    dot_general x3, matrix products, dot_nn(): lax.dot_general(a, b, (((1,), (0,)), ((), ())), preferred_element_type=f32)  30.4 us
  transfers between devices with their start and end apart: 49, of which 23 were waited for; matrix products, arithmetic and copies ran while one was open for 17% of the time, Pallas kernels for 20%

profile of v2, /device:TPU:8, one launch (start us, length us, event | category | flops | bytes accessed | tf_op | source)
XLA Modules:
  0.0 679.0 jit_solution(13416529069081330774)
XLA Ops:
  17.8 7.3 %collective-permute-done.1 = bf16[2,64,1152]{2,1,0:T(8,128)(2,1)} collective-permute-done((bf16[2,64,1152]{2,1,0:T(8,128)(2,1)S(1)}, bf16[2,64,1152]{2,1,0:T(8,128)(2,1)}, u32[]{:S(2)}, u32[]{:S(2)}) %collective-permute-start.1) | collective-permute-done | bytes 294944 | tf_op jit(solution)/shard_map/ppermute | solution.py:40
  38.1 42.1 %collective-permute-done.3.refs_0_ = bf16[512,2048]{1,0:T(8,128)(2,1)} collective-permute-done((bf16[512,2048]{1,0:T(8,128)(2,1)}, bf16[512,2048]{1,0:T(8,128)(2,1)}, u32[]{:S(2)}, u32[]{:S(2)}) %collective-permute-start.3) | collective-permute-done | bytes 2097184 | tf_op jit(solution)/shard_map/ppermute | solution.py:40
  92.6 14.0 %collective-permute-done.refs_0_ = bf16[128,2048]{1,0:T(8,128)(2,1)S(1)} collective-permute-done((bf16[128,2048]{1,0:T(8,128)(2,1)S(1)}, bf16[128,2048]{1,0:T(8,128)(2,1)S(1)}, u32[]{:S(2)}, u32[]{:S(2)}) %collective-permute-start) | collective-permute-done | bytes 524320 | tf_op jit(solution)/shard_map/ppermute | solution.py:102
  117.7 8.3 %all_positions.2.n_ref = bf16[2048,2048]{1,0:T(8,128)(2,1)S(1)} custom-call(s32[4]{0:T(128)S(1)} %pad_add_fusion.order_ref, bf16[512,2048]{1,0:T(8,128)(2,1)S(1)} %bitcast.275, bf16[512,2048]{1,0:T(8,128)(2,1)} %collective-permute-done.7.refs_1_, bf16[512,2048]{1,0:T(8,128)(2,1)} %get-tuple-element.62.refs_2_, ...), custom_call_target="tpu_custom_call" | custom-call | flops 16777216 | bytes 16777216 | tf_op jit(solution)/shard_map/all_positions/pallas_call | solution.py:239
  139.5 14.2 %select_convert_fusion.refs_1_ = bf16[2048,1024]{1,0:T(8,128)(2,1)} fusion(pred[1024]{0:T(1024)(128)(4,1)S(1)} %fusion.41, bf16[2048,2048]{1,0:T(8,128)(2,1)} %copy-done.5, bf16[2048,1152]{1,0:T(8,128)(2,1)} %all-gather.3.cloned.1.call-done.refs_4_.wc_ref), kind=kOutput, calls=%fused_computation | convolution fusion | flops 8594128896 | bytes 16778240 | tf_op jit(solution)/shard_map/dot_general | solution.py:358
  153.7 26.4 %collective-permute-done.6.refs_0_ = bf16[128,2048]{1,0:T(8,128)(2,1)S(1)} collective-permute-done((bf16[128,2048]{1,0:T(8,128)(2,1)S(1)}, bf16[128,2048]{1,0:T(8,128)(2,1)S(1)}, u32[]{:S(2)}, u32[]{:S(2)}) %collective-permute-start.6) | collective-permute-done | bytes 524320 | tf_op jit(solution)/shard_map/ppermute | solution.py:98
  186.2 31.0 %recurrence_forward.1 = (f32[2048,1024]{1,0:T(8,128)}, bf16[2048,1024]{1,0:T(8,128)(2,1)S(1)}, bf16[8,128,1024]{2,1,0:T(8,128)(2,1)S(1)}) custom-call(s32[1]{0:T(128)} %bitcast.1.me_ref, bf16[2048,1024]{1,0:T(8,128)(2,1)S(1)} %copy-done.17, bf16[1024,128]{1,0:T(8,128)(2,1)S(1)} %bc_forward.1.b0, bf16[1024,128]{1,0:T(8,128)(2,1)} %collective-permute-done.9.b1, ...), custom_call_target="tpu_custom_call" | custom-call | flops 30000001024 | bytes 16777216 | tf_op jit(solution)/shard_map/recurrence_forward/pallas_call | solution.py:583
  227.2 9.4 %collective-permute-done.18.refs_6_ = bf16[128,2048]{1,0:T(8,128)(2,1)S(1)} collective-permute-done((bf16[128,2048]{1,0:T(8,128)(2,1)}, bf16[128,2048]{1,0:T(8,128)(2,1)S(1)}, u32[]{:S(2)}, u32[]{:S(2)}) %collective-permute-start.18) | collective-permute-done | bytes 524320 | tf_op jit(solution)/shard_map/ppermute | solution.py:102
  236.5 11.1 %collective-permute-done.19.refs_7_ = bf16[128,2048]{1,0:T(8,128)(2,1)} collective-permute-done((bf16[128,2048]{1,0:T(8,128)(2,1)}, bf16[128,2048]{1,0:T(8,128)(2,1)}, u32[]{:S(2)}, u32[]{:S(2)}) %collective-permute-start.19) | collective-permute-done | bytes 524320 | tf_op jit(solution)/shard_map/ppermute | solution.py:102
  256.1 6.6 all_positions.3.t_ref
  268.2 25.4 %gate_forward.1 = (f32[2048,1024]{1,0:T(8,128)}, f32[2048,1024]{1,0:T(8,128)}, f32[8,2048]{1,0:T(8,128)S(1)}) custom-call(bf16[2048,2048]{1,0:T(8,128)(2,1)} %copy-done.5, bf16[2048,2048]{1,0:T(8,128)(2,1)} %copy-done.6, f32[2048,1024]{1,0:T(8,128)} %get-tuple-element.65.y_ref, bf16[2048,1024]{1,0:T(8,128)(2,1)S(1)} %copy-done.30, ...), custom_call_target="tpu_custom_call" | custom-call | flops 17179869184 | bytes 33554432 | tf_op jit(solution)/shard_map/gate_forward/pallas_call | solution.py:853
  302.8 12.1 %gate_backward.1 = (bf16[2048,1024]{1,0:T(8,128)(2,1)S(1)}, bf16[2048,1024]{1,0:T(8,128)(2,1)S(1)}, bf16[2048,1024]{1,0:T(8,128)(2,1)S(1)}, f32[8,1024]{1,0:T(8,128)S(1)}) custom-call(f32[2048,1024]{1,0:T(8,128)S(1)} %copy-done.7, f32[2048,1024]{1,0:T(8,128)} %get-tuple-element.76.z_ref, f32[2048,1024]{1,0:T(8,128)} %get-tuple-element.77.d_ref, ...), custom_call_target="tpu_custom_call" | custom-call | flops 62914560 | bytes 37748736 | tf_op jit(solution)/shard_map/gate_backward/pallas_call | solution.py:913
  314.9 18.0 %convolution_convert_fusion.2.refs_1_ = bf16[1024,2048]{1,0:T(8,128)(2,1)} fusion(bf16[2048,1024]{1,0:T(8,128)(2,1)S(1)} %get-tuple-element.80.refs_3_, bf16[2048,2048]{1,0:T(8,128)(2,1)} %copy-done.6), kind=kOutput, calls=%fused_computation.27 | convolution fusion | flops 8592031744 | bytes 16777216 | tf_op jit(solution)/shard_map/dot_general | solution.py:366
  333.0 10.9 %convolution_convert_fusion.3.refs_2_ = bf16[2048,1024]{1,0:T(8,128)(2,1)} fusion(bf16[2048,2048]{1,0:T(8,128)(2,1)S(1)} %bitcast.280, bf16[2048,1024]{1,0:T(8,128)(2,1)S(1)} %get-tuple-element.81.z_ref), kind=kOutput, calls=%fused_computation.28 | convolution fusion | flops 8592031744 | bytes 16777216 | tf_op jit(solution)/shard_map/dot_general | solution.py:366
  349.0 60.6 %recurrence_backward.1 = (bf16[2048,1152]{1,0:T(8,128)(2,1)}, bf16[4,1024,128]{2,1,0:T(8,128)(2,1)S(1)}, f32[2048,128]{1,0:T(8,128)S(1)}, f32[8,1024]{1,0:T(8,128)S(1)}, f32[8,128]{1,0:T(8,128)S(1)}) custom-call(s32[1]{0:T(128)} %bitcast.1.me_ref, bf16[2048,1024]{1,0:T(8,128)(2,1)} %get-tuple-element.63.ci_ref.prev_ref, ...), custom_call_target="tpu_custom_call" | custom-call | flops 70000001024 | bytes 16777216 | tf_op jit(solution)/shard_map/recurrence_backward/pallas_call | solution.py:777
  411.6 12.2 %convolution_convert_fusion.1 = bf16[2048,2048]{1,0:T(8,128)(2,1)S(1)} fusion(bf16[2048,1024]{1,0:T(8,128)(2,1)} %get-tuple-element.86, bf16[1024,2048]{1,0:T(8,128)(2,1)} %copy-done.20), kind=kOutput, calls=%fused_computation.2 | convolution fusion | flops 8594128896 | bytes 16777216 | tf_op jit(solution)/shard_map/dot_general | solution.py:358
  429.0 6.9 %collective-permute-done.24 = bf16[2,1024,128]{2,1,0:T(8,128)(2,1)S(1)} collective-permute-done((bf16[2,1024,128]{2,1,0:T(8,128)(2,1)S(1)}, bf16[2,1024,128]{2,1,0:T(8,128)(2,1)S(1)}, u32[]{:S(2)}, u32[]{:S(2)}) %collective-permute-start.24) | collective-permute-done | bytes 524320 | tf_op jit(solution)/shard_map/ppermute | solution.py:40
  439.6 7.1 %collective-permute-done.25 = bf16[1024,128]{1,0:T(8,128)(2,1)} collective-permute-done((bf16[1024,128]{1,0:T(8,128)(2,1)}, bf16[1024,128]{1,0:T(8,128)(2,1)}, u32[]{:S(2)}, u32[]{:S(2)}) %collective-permute-start.25) | collective-permute-done | bytes 262176 | tf_op jit(solution)/shard_map/ppermute | solution.py:40
  455.5 16.5 %convolution_convert_fusion.refs_1_ = bf16[2048,1152]{1,0:T(8,128)(2,1)} fusion(bf16[2048,2048]{1,0:T(8,128)(2,1)} %copy-done.5, bf16[2048,1152]{1,0:T(8,128)(2,1)} %copy-done.1), kind=kOutput, calls=%fused_computation.1 | convolution fusion | flops 9666035712 | bytes 17825792 | tf_op jit(solution)/shard_map/dot_general | solution.py:366
  490.8 26.6 %input_gradient.1.refs_4_ = bf16[2048,2048]{1,0:T(8,128)(2,1)} custom-call(bf16[2048,1024]{1,0:T(8,128)(2,1)S(1)} %copy-done.32, bf16[2048,1152]{1,0:T(8,128)(2,1)} %get-tuple-element.93.p_ref, bf16[2048,1024]{1,0:T(8,128)(2,1)} %all-gather.5.cloned.1.call-done.wg_ref, bf16[2048,1152]{1,0:T(8,128)(2,1)} %all-gather.3.cloned.1.call-done.refs_4_.wc_ref), custom_call_target="tpu_custom_call" | custom-call | flops 199999995904 | bytes 33554432 | tf_op jit(solution)/shard_map/input_gradient/pallas_call | solution.py:937
  517.4 13.7 %collective-permute-done.26.refs_0_ = bf16[128,2048]{1,0:T(8,128)(2,1)} collective-permute-done((bf16[128,2048]{1,0:T(8,128)(2,1)}, bf16[128,2048]{1,0:T(8,128)(2,1)}, u32[]{:S(2)}, u32[]{:S(2)}) %collective-permute-start.26) | collective-permute-done | bytes 524320 | tf_op jit(solution)/shard_map/ppermute | solution.py:98
  531.1 30.5 %collective-permute-done.27.refs_1_ = bf16[128,2048]{1,0:T(8,128)(2,1)} collective-permute-done((bf16[128,2048]{1,0:T(8,128)(2,1)}, bf16[128,2048]{1,0:T(8,128)(2,1)}, u32[]{:S(2)}, u32[]{:S(2)}) %collective-permute-start.27) | collective-permute-done | bytes 524320 | tf_op jit(solution)/shard_map/ppermute | solution.py:98
  605.2 40.1 %collective-permute-done.31.refs_1_ = bf16[512,2048]{1,0:T(8,128)(2,1)} collective-permute-done((bf16[512,2048]{1,0:T(8,128)(2,1)}, bf16[512,2048]{1,0:T(8,128)(2,1)}, u32[]{:S(2)}, u32[]{:S(2)}) %collective-permute-start.31) | collective-permute-done | bytes 2097184 | tf_op jit(solution)/shard_map/ppermute | solution.py:40
  653.0 9.4 %fusion.16 = (bf16[1,512,2048]{2,1,0:T(8,128)(2,1)}, bf16[1,512,2048]{2,1,0:T(8,128)(2,1)}) fusion(bf16[512,2048]{1,0:T(8,128)(2,1)} %collective-permute-done.31.refs_1_, f32[512]{0:T(512)S(1)} %broadcast_multiply_fusion, f32[512]{0:T(512)S(1)} %get-tuple-element.174, f32[2048]{0:T(1024)S(1)} %copy-done.40, f32[512]{0:T(512)S(1)} %get-tuple-element.173, ...), kind=kLoop, calls=%fused_computation.30 | loop fusion | flops 22020096 | bytes 20985868 | tf_op jit(solution)/shard_map/broadcast_in_dim | solution.py:1112
  (369 shorter events, 202.2 us)
Async XLA Ops:
  7.2 105.8 %all-gather.3.cloned.1.call-start = ((), (), s32[]{:S(2)}) async-start(), calls=%async_computation.2 | async-start | bytes 5308416 | tf_op jit(solution)/shard_map/all_gather | solution.py:185
  30.9 235.2 %all-gather.5.cloned.1.call-start = ((), (), s32[]{:S(2)}) async-start(), calls=%async_computation.3 | async-start | bytes 4718592 | tf_op jit(solution)/shard_map/all_gather | solution.py:190
  32.3 48.0 %collective-permute-start.3 = (bf16[512,2048]{1,0:T(8,128)(2,1)}, bf16[512,2048]{1,0:T(8,128)(2,1)}, u32[]{:S(2)}, u32[]{:S(2)}) collective-permute-start(bf16[512,2048]{1,0:T(8,128)(2,1)} %after.5), channel_id=1, source_target_pairs={{0,2},{1,3},{2,0},{3,1},{4,6},{5,7},{6,4},{7,5},{8,10},{9,11},{10,... | collective-permute-start | bytes 6291464 | tf_op jit(solution)/shard_map/ppermute | solution.py:40
  90.0 16.6 %collective-permute-start = (bf16[128,2048]{1,0:T(8,128)(2,1)S(1)}, bf16[128,2048]{1,0:T(8,128)(2,1)S(1)}, u32[]{:S(2)}, u32[]{:S(2)}) collective-permute-start(bf16[128,2048]{1,0:T(8,128)(2,1)S(1)} %copy.204.refs_3_), channel_id=1, source_target_pairs={{0,4},{4,0},{8,12},{12,8},{16,20},{20,16},{24,28},{28,24},{1,5},{5... | collective-permute-start | bytes 1572872 | tf_op jit(solution)/shard_map/ppermute | solution.py:102
  91.5 25.1 %collective-permute-start.7 = (bf16[512,2048]{1,0:T(8,128)(2,1)S(1)}, bf16[512,2048]{1,0:T(8,128)(2,1)}, u32[]{:S(2)}, u32[]{:S(2)}) collective-permute-start(bf16[512,2048]{1,0:T(8,128)(2,1)S(1)} %bitcast.274), channel_id=1, source_target_pairs={{0,1},{1,0},{2,3},{3,2},{4,5},{5,4},{6,7},{7,6},{8,9},{9,8},{10,11... | collective-permute-start | bytes 6291464 | tf_op jit(solution)/shard_map/ppermute | solution.py:40
  113.2 142.9 %collective-permute-start.12 = (bf16[512,2048]{1,0:T(8,128)(2,1)}, bf16[512,2048]{1,0:T(8,128)(2,1)}, u32[]{:S(2)}, u32[]{:S(2)}) collective-permute-start(bf16[512,2048]{1,0:T(8,128)(2,1)} %bitcast.276), channel_id=1, source_target_pairs={{0,1},{1,0},{2,3},{3,2},{4,5},{5,4},{6,7},{7,6},{8,9},{9,8},{10,11... | collective-permute-start | bytes 6291464 | tf_op jit(solution)/shard_map/ppermute | solution.py:40
  134.2 438.1 %reduce-scatter.3.cloned.1.call-start = ((), (), s32[]{:S(2)}) async-start(), calls=%async_computation.4 | async-start | bytes 4718592 | tf_op jit(solution)/shard_map/reduce_scatter | solution.py:320
  134.3 45.8 %collective-permute-start.6 = (bf16[128,2048]{1,0:T(8,128)(2,1)S(1)}, bf16[128,2048]{1,0:T(8,128)(2,1)S(1)}, u32[]{:S(2)}, u32[]{:S(2)}) collective-permute-start(bf16[128,2048]{1,0:T(8,128)(2,1)S(1)} %copy-done.11), channel_id=1, source_target_pairs={{0,8},{4,12},{8,16},{12,20},{16,24},{20,28},{24,0},{28,4},{1,9},{5... | collective-permute-start | bytes 1572872 | tf_op jit(solution)/shard_map/ppermute | solution.py:98
  135.9 84.6 %collective-permute-start.14 = (bf16[128,2048]{1,0:T(8,128)(2,1)S(1)}, bf16[128,2048]{1,0:T(8,128)(2,1)S(1)}, u32[]{:S(2)}, u32[]{:S(2)}) collective-permute-start(bf16[128,2048]{1,0:T(8,128)(2,1)S(1)} %copy-done.11), channel_id=1, source_target_pairs={{0,16},{4,20},{8,24},{12,28},{16,0},{20,4},{24,8},{28,12},{1,17},{... | collective-permute-start | bytes 1572872 | tf_op jit(solution)/shard_map/ppermute | solution.py:98
  138.0 44.7 %collective-permute-start.9 = (bf16[1024,128]{1,0:T(8,128)(2,1)S(1)}, bf16[1024,128]{1,0:T(8,128)(2,1)}, u32[]{:S(2)}, u32[]{:S(2)}) collective-permute-start(bf16[1024,128]{1,0:T(8,128)(2,1)S(1)} %bc_forward.1.b0), channel_id=1, source_target_pairs={{0,1},{1,0},{2,3},{3,2},{4,5},{5,4},{6,7},{7,6},{8,9},{9,8},{10,11... | collective-permute-start | bytes 786440 | tf_op jit(solution)/shard_map/ppermute | solution.py:40
  139.5 43.2 %collective-permute-start.11 = (bf16[1024,128]{1,0:T(8,128)(2,1)}, bf16[1024,128]{1,0:T(8,128)(2,1)}, u32[]{:S(2)}, u32[]{:S(2)}) collective-permute-start(bf16[1024,128]{1,0:T(8,128)(2,1)} %collective-permute-done.10.b2), channel_id=1, source_target_pairs={{0,1},{1,0},{2,3},{3,2},{4,5},{5,4},{6,7},{7,6},{8,9},{9,8},{10,11... | collective-permute-start | bytes 786440 | tf_op jit(solution)/shard_map/ppermute | solution.py:40
  181.0 39.5 %collective-permute-start.15 = (bf16[128,2048]{1,0:T(8,128)(2,1)S(1)}, bf16[128,2048]{1,0:T(8,128)(2,1)}, u32[]{:S(2)}, u32[]{:S(2)}) collective-permute-start(bf16[128,2048]{1,0:T(8,128)(2,1)S(1)} %copy-done.11), channel_id=1, source_target_pairs={{0,24},{4,28},{8,0},{12,4},{16,8},{20,12},{24,16},{28,20},{1,25},{... | collective-permute-start | bytes 1572872 | tf_op jit(solution)/shard_map/ppermute | solution.py:98
  182.7 37.8 %collective-permute-start.16 = (bf16[128,2048]{1,0:T(8,128)(2,1)}, bf16[128,2048]{1,0:T(8,128)(2,1)}, u32[]{:S(2)}, u32[]{:S(2)}) collective-permute-start(bf16[128,2048]{1,0:T(8,128)(2,1)} %get-tuple-element.68.refs_1_), channel_id=1, source_target_pairs={{0,4},{4,0},{8,12},{12,8},{16,20},{20,16},{24,28},{28,24},{1,5},{5... | collective-permute-start | bytes 1572872 | tf_op jit(solution)/shard_map/ppermute | solution.py:102
  182.7 37.8 %collective-permute-start.13 = (bf16[512,2048]{1,0:T(8,128)(2,1)}, bf16[512,2048]{1,0:T(8,128)(2,1)}, u32[]{:S(2)}, u32[]{:S(2)}) collective-permute-start(bf16[512,2048]{1,0:T(8,128)(2,1)} %get-tuple-element.66), channel_id=1, source_target_pairs={{0,2},{1,3},{2,0},{3,1},{4,6},{5,7},{6,4},{7,5},{8,10},{9,11},{10,... | collective-permute-start | bytes 6291464 | tf_op jit(solution)/shard_map/ppermute | solution.py:40
  221.4 34.7 %collective-permute-start.17 = (bf16[512,2048]{1,0:T(8,128)(2,1)}, bf16[512,2048]{1,0:T(8,128)(2,1)}, u32[]{:S(2)}, u32[]{:S(2)}) collective-permute-start(bf16[512,2048]{1,0:T(8,128)(2,1)} %get-tuple-element.70.refs_2_), channel_id=1, source_target_pairs={{0,1},{1,0},{2,3},{3,2},{4,5},{5,4},{6,7},{7,6},{8,9},{9,8},{10,11... | collective-permute-start | bytes 6291464 | tf_op jit(solution)/shard_map/ppermute | solution.py:40
  223.5 24.1 %collective-permute-start.19 = (bf16[128,2048]{1,0:T(8,128)(2,1)}, bf16[128,2048]{1,0:T(8,128)(2,1)}, u32[]{:S(2)}, u32[]{:S(2)}) collective-permute-start(bf16[128,2048]{1,0:T(8,128)(2,1)} %get-tuple-element.73.refs_3_), channel_id=1, source_target_pairs={{0,4},{4,0},{8,12},{12,8},{16,20},{20,16},{24,28},{28,24},{1,5},{5... | collective-permute-start | bytes 1572872 | tf_op jit(solution)/shard_map/ppermute | solution.py:102
  347.2 64.4 %collective-permute-start.22 = (bf16[4,128,2048]{2,1,0:T(8,128)(2,1)}, bf16[4,128,2048]{2,1,0:T(8,128)(2,1)}, u32[]{:S(2)}, u32[]{:S(2)}) collective-permute-start(bf16[4,128,2048]{2,1,0:T(8,128)(2,1)} %dynamic-slice_bitcast_fusion.2), channel_id=1, source_target_pairs={{0,4},{4,0},{8,12},{12,8},{16,20},{20,16},{24,28},{28,24},{1,5},{5... | collective-permute-start | bytes 6291464 | tf_op jit(solution)/shard_map/ppermute | solution.py:102
  349.0 300.9 %reduce-scatter.5.cloned.1.call-start = ((), (), s32[]{:S(2)}) async-start(), calls=%async_computation.5 | async-start | bytes 5308416 | tf_op jit(solution)/shard_map/reduce_scatter | solution.py:320
  428.4 56.7 %collective-permute-start.23 = (bf16[2,512,2048]{2,1,0:T(8,128)(2,1)}, bf16[2,512,2048]{2,1,0:T(8,128)(2,1)}, u32[]{:S(2)}, u32[]{:S(2)}) collective-permute-start(bf16[2,512,2048]{2,1,0:T(8,128)(2,1)} %dynamic-slice_bitcast_fusion.1), channel_id=1, source_target_pairs={{0,1},{1,0},{2,3},{3,2},{4,5},{5,4},{6,7},{7,6},{8,9},{9,8},{10,11... | collective-permute-start | bytes 12582920 | tf_op jit(solution)/shard_map/ppermute | solution.py:40
  475.2 55.8 %collective-permute-start.26 = (bf16[128,2048]{1,0:T(8,128)(2,1)}, bf16[128,2048]{1,0:T(8,128)(2,1)}, u32[]{:S(2)}, u32[]{:S(2)}) collective-permute-start(bf16[128,2048]{1,0:T(8,128)(2,1)} %get-tuple-element.139), channel_id=1, source_target_pairs={{0,8},{4,12},{8,16},{12,20},{16,24},{20,28},{24,0},{28,4},{1,9},{5... | collective-permute-start | bytes 1572872 | tf_op jit(solution)/shard_map/ppermute | solution.py:98
  481.0 80.5 %collective-permute-start.27 = (bf16[128,2048]{1,0:T(8,128)(2,1)}, bf16[128,2048]{1,0:T(8,128)(2,1)}, u32[]{:S(2)}, u32[]{:S(2)}) collective-permute-start(bf16[128,2048]{1,0:T(8,128)(2,1)} %get-tuple-element.138), channel_id=1, source_target_pairs={{0,16},{4,20},{8,24},{12,28},{16,0},{20,4},{24,8},{28,12},{1,17},{... | collective-permute-start | bytes 1572872 | tf_op jit(solution)/shard_map/ppermute | solution.py:98
  483.0 83.3 %collective-permute-start.28 = (bf16[128,2048]{1,0:T(8,128)(2,1)}, bf16[128,2048]{1,0:T(8,128)(2,1)}, u32[]{:S(2)}, u32[]{:S(2)}) collective-permute-start(bf16[128,2048]{1,0:T(8,128)(2,1)} %get-tuple-element.137), channel_id=1, source_target_pairs={{0,24},{4,28},{8,0},{12,4},{16,8},{20,12},{24,16},{28,20},{1,25},{... | collective-permute-start | bytes 1572872 | tf_op jit(solution)/shard_map/ppermute | solution.py:98
  489.7 76.7 %collective-permute-start.29 = (bf16[512,2048]{1,0:T(8,128)(2,1)}, bf16[512,2048]{1,0:T(8,128)(2,1)}, u32[]{:S(2)}, u32[]{:S(2)}) collective-permute-start(bf16[512,2048]{1,0:T(8,128)(2,1)} %fusion.13), channel_id=1, source_target_pairs={{0,2},{1,3},{2,0},{3,1},{4,6},{5,7},{6,4},{7,5},{8,10},{9,11},{10,... | collective-permute-start | bytes 6291464 | tf_op jit(solution)/shard_map/ppermute | solution.py:40
  599.3 46.1 %collective-permute-start.31 = (bf16[512,2048]{1,0:T(8,128)(2,1)}, bf16[512,2048]{1,0:T(8,128)(2,1)}, u32[]{:S(2)}, u32[]{:S(2)}) collective-permute-start(bf16[512,2048]{1,0:T(8,128)(2,1)} %get-tuple-element.100), channel_id=1, source_target_pairs={{0,2},{1,3},{2,0},{3,1},{4,6},{5,7},{6,4},{7,5},{8,10},{9,11},{10,... | collective-permute-start | bytes 6291464 | tf_op jit(solution)/shard_map/ppermute | solution.py:40
  (78 other events, 603.6 us)
Sparse Core Ops, SparseCore 0:
  31.0 81.9 all-gather.2
  134.4 111.9 all-gather.4
  349.1 103.6 reduce-scatter.2
  485.2 130.4 reduce-scatter.4

commit v3 on v2

--- a/solution.py
+++ b/solution.py
@@ -61,7 +61,7 @@
 def seq_scatter_relative(blocks):
     view = blocks.reshape((2, 2) + blocks.shape[1:])
     half = view[:, 0].astype(f32) + xor_seq(view[:, 1], 1).astype(f32)
-    return half[0] + xor_seq(half[1].astype(bf16), 2).astype(f32)
+    return half[0], xor_seq(half[1].astype(bf16), 2)
 
 
 def by_partner(pieces):
@@ -78,10 +78,9 @@
     )
 
 
-def seq_transpose(pieces):
+def seq_exchange(pieces):
     turned = by_partner([pieces[k] for k in range(PART)])
-    moved = [turned[0]] + [xor_seq(turned[k], k) for k in range(1, PART)]
-    return jnp.stack(by_partner(moved))
+    return [turned[0]] + [xor_seq(turned[k], k) for k in range(1, PART)]
 
 
 def seq_total(value):
@@ -157,13 +156,64 @@
     )(places, *pieces)
 
 
-def seq_pass(pieces):
+def pieces_kernel(w_ref, dt_ref, norm_ref, gate_ref, conv_ref, gates_ref):
+    rows = w_ref.shape[0]
+    lane = lax.broadcasted_iota(jnp.int32, (1, LANES), 1)
+    square = lax.broadcasted_iota(jnp.int32, (rows, rows), 0) == lax.broadcasted_iota(
+        jnp.int32, (rows, rows), 1
+    )
+
+    def column(values):
+        return jnp.sum(jnp.where(square, values, 0.0), axis=1, keepdims=True)
+
+    gain = column(norm_ref[0:1, :].astype(f32))
+    gates = [column(gate_ref[k : k + 1, :].astype(f32)) for k in range(2)]
+    head = lax.broadcasted_iota(jnp.int32, (HEADS, LANES), 0)
+    slot = lax.broadcasted_iota(jnp.int32, (HEADS, LANES), 1)
+    for owner in range(PART):
+        for strip in range(STRIPS):
+            source = (strip * PART + owner) * LANES
+            at = slice(strip * LANES, (strip + 1) * LANES)
+            gates_ref[owner, :, at] = w_ref[:, source : source + LANES]
+            conv_ref[owner, :, at] = w_ref[:, INNER + source : INNER + source + LANES]
+        chosen = (slot < OWN_HEADS) & (head == slot // 2 * 2 * PART + 2 * owner + slot % 2)
+        steps = dot_nn(dt_ref[...], jnp.where(chosen, 1.0, 0.0).astype(bf16))
+        first = 2 * INNER + owner // 2 * LANES
+        tile = w_ref[:, first : first + LANES].astype(f32)
+        if owner % 2 == 0:
+            tile = pltpu.roll(tile, OWN_BC, 1)
+        tail = jnp.where(lane < OWN_HEADS, steps, jnp.where(lane == OWN_HEADS, gain, 0.0))
+        for k in range(2):
+            tail = jnp.where(lane == OWN_HEADS + 1 + k, gates[k], tail)
+        tail = jnp.where(lane >= LANES - OWN_BC, tile, tail)
+        conv_ref[owner, :, OWN:] = tail.astype(bf16)
+
+
+def owners_pieces(w_in, w_dt, norm_gain, gate_gain):
+    rows = w_in.shape[0]
+    whole = lambda *block: pl.BlockSpec(block, lambda i: (0,) * len(block))
+
+    return pl.pallas_call(
+        pieces_kernel,
+        grid=(1,),
+        in_specs=[whole(rows, 2 * INNER + 2 * STATE), whole(rows, HEADS), whole(1, rows), whole(2, rows)],
+        out_specs=[whole(PART, rows, CONV_COLS), whole(PART, rows, OWN)],
+        out_shape=[
+            jax.ShapeDtypeStruct((PART, rows, CONV_COLS), bf16),
+            jax.ShapeDtypeStruct((PART, rows, OWN), bf16),
+        ],
+        compiler_params=pltpu.CompilerParams(vmem_limit_bytes=32 * 2**20),
+        name="owners_pieces",
+    )(w_in, w_dt, norm_gain[None, :], gate_gain.reshape(2, rows))
+
+
+def seq_pass(pieces, *beside):
     me = lax.axis_index("seq")
     core, row = me % 2, me // 2
     view = pieces.reshape((2, 2) + pieces.shape[1:])
     give = lax.dynamic_index_in_dim(view, 1 - row, 0, False)
     keep = lax.dynamic_index_in_dim(view, row, 0, False)
-    got = xor_seq(give, 2)
+    got, *beside = tie(xor_seq(give, 2), *beside)
     lower = jnp.where(row == 0, keep, got)
     upper = jnp.where(row == 0, got, keep)
     both = jnp.stack([lower, upper])
@@ -171,7 +221,7 @@
     other = xor_seq(lax.dynamic_index_in_dim(both, 1 - core, 1, False), 1)
     first = jnp.where(core == 0, mine, other)
     second = jnp.where(core == 0, other, mine)
-    return jnp.stack([first, second], axis=1).reshape(pieces.shape)
+    return jnp.stack([first, second], axis=1).reshape((-1,) + pieces.shape[2:]), beside
 
 
 def seq_pieces(block, after=None):
@@ -180,16 +230,20 @@
     return block, xor_seq(block, 1), across, xor_seq(across, 1)
 
 
-def gather_everything(conv_pieces, gate_pieces, o, x_block):
-    c = seq_pass(conv_pieces).reshape(-1, CONV_COLS)
+def gather_everything(conv_pieces, gate_pieces, o, x_block, cot_block):
+    c, (o1,) = seq_pass(conv_pieces, dp_shift_z(o, 1))
     w_conv = lax.all_gather(c, "dp", axis=0, tiled=True)
-    x_across, gate_pieces = after([xor_seq(after([x_block], [c])[0], 2), gate_pieces], [])
-    g = seq_pass(gate_pieces).reshape(-1, OWN)
-    o_x, g, x_across, o = after([dp_swap_x(o), g, x_across, o], [w_conv])
+    x_across, gate_pieces = tie(xor_seq(after([x_block], [c])[0], 2), gate_pieces)
+    g, _ = seq_pass(gate_pieces)
+    half = cot_block.shape[0] // 2
+    cot_a, cot_b = after([cot_block[:half], cot_block[half:]], [g])
+    cot_a = xor_seq(cot_a, 2)
+    o2, o3, o_x, g, x_across = after(
+        [dp_shift_z(o, 2), dp_shift_z(o, 3), dp_swap_x(o), g, x_across], [w_conv]
+    )
     x_pieces = (x_block, xor_seq(x_block, 1), x_across, xor_seq(x_across, 1))
     w_gate = lax.all_gather(g, "dp", axis=0, tiled=True)
-    out_rows = [o] + [dp_shift_z(o, steps) for steps in range(1, 4)] + [o_x]
-    return w_conv, w_gate, out_rows, x_pieces
+    return w_conv, w_gate, [o, o1, o2, o3, o_x], x_pieces, (cot_a, cot_b)
 
 
 def out_places():
@@ -253,29 +307,6 @@
     )(order, *pieces, *extra)
 
 
-def x_parts(blocks):
-    x = lax.axis_index("dp") % 2
-    view = blocks.reshape((4, 2) + blocks.shape[1:])
-    mine = lax.dynamic_index_in_dim(view, x, 1, False)
-    return mine, lax.dynamic_index_in_dim(view, 1 - x, 1, False)
-
-
-def x_halves(blocks):
-    mine, other = x_parts(blocks)
-    return mine, dp_swap_x(other)
-
-
-def z_gives(mine, received):
-    z = lax.axis_index("dp") // 2
-
-    def of(steps):
-        which = (z + steps) % 4
-        a = lax.dynamic_index_in_dim(mine, which, 0, False)
-        return a.astype(f32) + lax.dynamic_index_in_dim(received, which, 0, False).astype(f32)
-
-    return of(0), [of(steps).astype(bf16) for steps in range(1, 4)]
-
-
 def dp_total(value):
     if not fast_mesh():
         return lax.psum(value, "dp")
@@ -321,7 +352,7 @@
 
 
 def owners_rows(total):
-    return seq_transpose(total.astype(bf16).reshape(PART, -1, total.shape[1])).astype(f32)
+    return seq_exchange(total.reshape(PART, -1, total.shape[1]))
 
 
 def scatter_in(grads):
@@ -336,12 +367,13 @@
     return lax.dynamic_index_in_dim(full, lax.axis_index("seq"), 1, False).reshape(OWN, -1)
 
 
-def gather_plainly(conv_pieces, gate_pieces, out_rows, x_block):
+def gather_plainly(conv_pieces, gate_pieces, out_rows, x_block, cot_block):
     return (
         gather_in(conv_pieces),
         gather_in(gate_pieces),
         gather_out(out_rows),
         seq_pieces(x_block),
+        jnp.split(cot_block, 2),
     )
 
 
@@ -458,7 +490,7 @@
         ],
         input_output_aliases={4: 0},
         scratch_shapes=[pltpu.VMEM((8 + length, LANES), f32), pltpu.VMEM((8 + length, LANES), f32)],
-        compiler_params=pltpu.CompilerParams(vmem_limit_bytes=24 * 2**20),
+        compiler_params=pltpu.CompilerParams(vmem_limit_bytes=60 * 2**20),
         cost_estimate=pl.CostEstimate(
             flops=40 * length * LANES, bytes_accessed=14 * length * LANES, transcendentals=0
         ),
@@ -606,10 +638,10 @@
             jax.ShapeDtypeStruct((blocks, STATE, OWN), bf16),
         ],
         compiler_params=pltpu.CompilerParams(
-            dimension_semantics=("arbitrary",), vmem_limit_bytes=40 * 2**20
+            dimension_semantics=("arbitrary",), vmem_limit_bytes=60 * 2**20
         ),
         cost_estimate=pl.CostEstimate(
-            flops=30 * 10**9, bytes_accessed=2**24, transcendentals=10**7
+            flops=60 * 10**9, bytes_accessed=2**24, transcendentals=10**7
         ),
         name="recurrence_forward",
     )(me, conv_in, *bc, dt_tile, taps, rows, skip_row)
@@ -824,7 +856,7 @@
             jax.ShapeDtypeStruct((8, LANES), f32),
         ],
         compiler_params=pltpu.CompilerParams(
-            dimension_semantics=("arbitrary",), vmem_limit_bytes=48 * 2**20
+            dimension_semantics=("arbitrary",), vmem_limit_bytes=60 * 2**20
         ),
         cost_estimate=pl.CostEstimate(
             flops=70 * 10**9, bytes_accessed=2**24, transcendentals=10**7
@@ -945,12 +977,114 @@
         ],
         out_specs=pl.BlockSpec((Q, D), along),
         out_shape=jax.ShapeDtypeStruct((length, D), bf16),
+        compiler_params=pltpu.CompilerParams(vmem_limit_bytes=60 * 2**20),
+        cost_estimate=pl.CostEstimate(
+            flops=10**10, bytes_accessed=2**22, transcendentals=0
+        ),
+        name="input_gradient",
+    )(d_z, d_project, w_gate, w_conv)
+
+
+def products_kernel(n_ref, z_ref, r_ref, t_ref, out_ref):
+    rows = n_ref.shape[1]
+    half = r_ref.shape[1]
+    out_ref[0, :rows, :] = dot_nn(n_ref[...].T, z_ref[...]).astype(bf16)
+    product = dot_nn(r_ref[...].T, t_ref[...]).astype(bf16)
+    out_ref[0, rows : rows + half, :] = product[:, :OWN]
+    out_ref[0, rows + half :, :] = product[:, OWN:]
+
+
+def products(normed, d_z, rounded_out, cot):
+    length = normed.shape[0]
+    count = STRIPS
+    whole = lambda i: (0, 0)
+    across = lambda i: (0, i)
+    return pl.pallas_call(
+        products_kernel,
+        grid=(count,),
+        in_specs=[
+            pl.BlockSpec((length, D // count), across),
+            pl.BlockSpec((length, OWN), whole),
+            pl.BlockSpec((length, LANES), across),
+            pl.BlockSpec((length, D), whole),
+        ],
+        out_specs=pl.BlockSpec((1, D // count + 2 * LANES, OWN), lambda i: (i, 0, 0)),
+        out_shape=jax.ShapeDtypeStruct((count, D // count + 2 * LANES, OWN), bf16),
         compiler_params=pltpu.CompilerParams(vmem_limit_bytes=48 * 2**20),
         cost_estimate=pl.CostEstimate(
-            flops=200 * 10**9, bytes_accessed=2**25, transcendentals=0
-        ),
-        name="input_gradient",
-    )(d_z, d_project, w_gate, w_conv)
+            flops=4 * length * D * OWN, bytes_accessed=2**25, transcendentals=0
+        ),
+        name="products",
+    )(normed, d_z, rounded_out, cot)
+
+
+def rows_kernel(me_ref, *refs):
+    gates, convs = refs[:PART], refs[PART : 2 * PART]
+    w_ref, wdt_ref, gain_ref, grad_ref, gdt_ref, gnorm_ref = refs[2 * PART :]
+    me = me_ref[0]
+    rows = w_ref.shape[0]
+    for k in range(PART):
+        owner = jnp.bitwise_xor(me, k)
+        for strip in range(STRIPS):
+            at = slice(strip * LANES, (strip + 1) * LANES)
+            first = pl.multiple_of((strip * PART + owner) * LANES, LANES)
+            grad_ref[:, pl.ds(first, LANES)] = gates[k][:, at].astype(f32)
+            grad_ref[:, pl.ds(INNER + first, LANES)] = convs[k][:, at].astype(f32)
+    odd, lower = me % 2 == 1, me >= 2
+    p = [convs[k][:, OWN:].astype(f32) for k in range(PART)]
+    r0, r1 = jnp.where(odd, p[1], p[0]), jnp.where(odd, p[0], p[1])
+    r2, r3 = jnp.where(odd, p[3], p[2]), jnp.where(odd, p[2], p[3])
+    tails = (
+        jnp.where(lower, r2, r0),
+        jnp.where(lower, r3, r1),
+        jnp.where(lower, r0, r2),
+        jnp.where(lower, r1, r3),
+    )
+    left = lax.broadcasted_iota(jnp.int32, (1, LANES), 1) < OWN_BC
+    for pair in range(2):
+        low, high = tails[2 * pair], tails[2 * pair + 1]
+        first = 2 * INNER + pair * LANES
+        grad_ref[:, first : first + LANES] = jnp.where(left, pltpu.roll(low, OWN_BC, 1), high)
+    slot = lax.broadcasted_iota(jnp.int32, (LANES, HEADS), 0)
+    head = lax.broadcasted_iota(jnp.int32, (LANES, HEADS), 1)
+    d_dt = jnp.zeros((rows, HEADS), f32)
+    for owner in range(PART):
+        chosen = (slot < OWN_HEADS) & (head == slot // 2 * 2 * PART + 2 * owner + slot % 2)
+        d_dt = d_dt + dot_nn(tails[owner].astype(bf16), jnp.where(chosen, 1.0, 0.0).astype(bf16))
+    gdt_ref[...] = d_dt
+    total = jnp.sum(wdt_ref[...].astype(f32) * d_dt, axis=1, keepdims=True)
+    for strip in range(2 * STRIPS * PART + 2):
+        at = slice(strip * LANES, (strip + 1) * LANES)
+        total = total + jnp.sum(w_ref[:, at].astype(f32) * grad_ref[:, at], axis=1, keepdims=True)
+    square = lax.broadcasted_iota(jnp.int32, (rows, rows), 0) == lax.broadcasted_iota(
+        jnp.int32, (rows, rows), 1
+    )
+    flat = jnp.sum(jnp.where(square, total, 0.0), axis=0, keepdims=True)
+    gnorm_ref[...] = flat / gain_ref[...].astype(f32)
+
+
+def projection_rows(me, gates, convs, w_in, w_dt, norm_gain):
+    rows = w_in.shape[0]
+    whole = lambda *block: pl.BlockSpec(block, lambda i, me: (0,) * len(block))
+    columns = w_in.shape[1]
+    return pl.pallas_call(
+        rows_kernel,
+        grid_spec=pltpu.PrefetchScalarGridSpec(
+            num_scalar_prefetch=1,
+            grid=(1,),
+            in_specs=[whole(rows, OWN)] * PART
+            + [whole(rows, CONV_COLS)] * PART
+            + [whole(rows, columns), whole(rows, HEADS), whole(1, rows)],
+            out_specs=[whole(rows, columns), whole(rows, HEADS), whole(1, rows)],
+        ),
+        out_shape=[
+            jax.ShapeDtypeStruct((rows, columns), f32),
+            jax.ShapeDtypeStruct((rows, HEADS), f32),
+            jax.ShapeDtypeStruct((1, rows), f32),
+        ],
+        compiler_params=pltpu.CompilerParams(vmem_limit_bytes=32 * 2**20),
+        name="projection_rows",
+    )(me, *gates, *convs, w_in, w_dt, norm_gain[None, :])
 
 
 def per_device(
@@ -977,21 +1111,27 @@
     unit_used = block * LANES < used_units
     head_used = ((jnp.arange(OWN_HEADS) // 2 * PART + me) * LANES < used_units).astype(f32)
 
-    every = lambda a: jnp.broadcast_to(a[None], (PART,) + a.shape)
-    tail = jnp.concatenate(
-        [
-            heads_by_owner(w_dt),
-            every(norm_gain[:, None]),
-            every(gate_gain.reshape(2, rows_in).T),
-            jnp.zeros((PART, rows_in, LANES - OWN_HEADS - 3 - OWN_BC), bf16),
-            w_in[:, 2 * INNER :].reshape(rows_in, PART, OWN_BC).transpose(1, 0, 2),
-        ],
-        axis=2,
-    )
-    conv_pieces = jnp.concatenate([by_owner(w_in[:, INNER : 2 * INNER]), tail], axis=2)
-    gate_pieces = by_owner(w_in[:, :INNER])
+    if fast_mesh():
+        conv_pieces, gate_pieces = owners_pieces(w_in, w_dt, norm_gain, gate_gain)
+    else:
+        every = lambda a: jnp.broadcast_to(a[None], (PART,) + a.shape)
+        tail = jnp.concatenate(
+            [
+                heads_by_owner(w_dt),
+                every(norm_gain[:, None]),
+                every(gate_gain.reshape(2, rows_in).T),
+                jnp.zeros((PART, rows_in, LANES - OWN_HEADS - 3 - OWN_BC), bf16),
+                w_in[:, 2 * INNER :].reshape(rows_in, PART, OWN_BC).transpose(1, 0, 2),
+            ],
+            axis=2,
+        )
+        conv_pieces = jnp.concatenate([by_owner(w_in[:, INNER : 2 * INNER]), tail], axis=2)
+        gate_pieces = by_owner(w_in[:, :INNER])
+
     gather = gather_everything if fast_mesh() else gather_plainly
-    w_conv, w_gate, w_o, x_pieces = gather(conv_pieces, gate_pieces, w_out, hidden_in[0])
+    w_conv, w_gate, w_o, x_pieces, (cot_a, cot_b) = gather(
+        conv_pieces, gate_pieces, w_out, hidden_in[0], grad_out[0]
+    )
     order = jnp.stack([me, me ^ 1, me ^ 2, me ^ 3]).astype(jnp.int32)
     gate_all = w_conv[:, OWN + OWN_HEADS + 1 : OWN + OWN_HEADS + 3]
     gate_all = gate_all.reshape(D // rows_in, rows_in, 2).transpose(0, 2, 1)
@@ -1021,18 +1161,22 @@
     normed = all_positions(x_pieces, order, jnp.broadcast_to(gain_row, (8, D)))
     dt_tile = dot_nn(normed, w_conv[:, OWN:])
     bc = seq_pieces(bc_forward(dt_tile, taps_tile))
-    cot_across = xor_seq(tie(grad_out[0], bc[2])[0], 2)
     conv_in = jnp.where(unit_used, dot_nn(normed, w_conv[:, :OWN]), 0.0).astype(bf16)
     if fast_mesh():
-        w_o[1], conv_in = tie(w_o[1], conv_in)
-        w_o.append(dp_swap_x(w_o[1]))
+        w_o += [dp_swap_x(piece) for piece in w_o[1:4]]
+    if not fast_mesh():
+        cot_a = xor_seq(cot_a, 2)
+    cot_a, cot_b, conv_in = tie(cot_a, cot_b, conv_in)
+    cot_b = xor_seq(cot_b, 2)
     y, act, entry = recurrence_forward(place_me, conv_in, bc, dt_tile, taps, rows, skip_row)
     if fast_mesh():
-        cot_across, *w_o[2:] = after([cot_across, *w_o[2:]], [entry])
-        w_o += [dp_swap_x(w_o[2]), dp_swap_x(w_o[3])]
+        cot_b, *w_o[5:] = after([cot_b, *w_o[5:]], [entry])
+    cot_pieces = (
+        grad_out[0], xor_seq(grad_out[0], 1), cot_a, cot_b, xor_seq(cot_a, 1), xor_seq(cot_b, 1)
+    )
+    cot_all = all_positions(cot_pieces, order)
+    if fast_mesh():
         w_o = assemble(w_o, out_places(), 512)
-    cot_pieces = (grad_out[0], xor_seq(grad_out[0], 1), cot_across, xor_seq(cot_across, 1))
-    cot_all = all_positions(cot_pieces, order)
     row = jnp.concatenate(
         [
             gate_row,
@@ -1045,22 +1189,23 @@
     rounded_out, d_y, d_z, grad_gate_rows = gate_backward(y, z, d_rounded, seq_total(sums), row)
     grad_gate_local = grad_gate_rows[0]
 
-    out_product = dot_tn(rounded_out, cot_all).astype(bf16)
-    gate_product = dot_tn(normed, d_z).astype(bf16)
-    d_y, out_product, gate_product = tie(d_y, out_product, gate_product)
     if fast_mesh():
-        out_mine, out_got = x_halves(out_product.reshape(8, LANES, D))
-        gate_total = dp_sum(gate_product)
+        both = products(normed, d_z, rounded_out, cot_all)
+        d_y, both = tie(d_y, both)
+        both_total = dp_sum(both.reshape(-1, OWN))
 
     d_values, d_bc, d_dt, g_conv, g_rows = recurrence_backward(
         place_me, conv_in, act, d_y, y, bc, dt_tile, entry, taps, rows, skip_row
     )
     if fast_mesh():
-        d_values, d_bc, out_got, rounded_out = tie(d_values, d_bc, out_got, rounded_out)
+        d_values, d_bc, rounded_out = tie(d_values, d_bc, rounded_out)
     branch = dot_nn(rounded_out, w_o).astype(bf16).reshape(PART, tokens, D)
     branch_mine, branch_got = core_halves(branch)
+    d_bc_mine, d_bc_got = seq_scatter_relative(d_bc)
+    branch_keep, branch_give = halves_sum(branch_mine, branch_got)
+    d_bc_got, branch_give = tie(d_bc_got, branch_give)
     d_project, g_tail = tail_backward(
-        dt_tile, seq_scatter_relative(d_bc), d_dt, taps_tile, d_values
+        dt_tile, d_bc_mine + d_bc_got.astype(f32), d_dt, taps_tile, d_values
     )
     g_skip = jnp.sum(g_conv[4].reshape(OWN_HEADS, HEAD_DIM), axis=1)
     small = jnp.concatenate(
@@ -1078,30 +1223,48 @@
     small = jnp.pad(small, (0, padded - count)).reshape(-1, LANES)
     if fast_mesh():
         conv_product = dot_tn(normed, d_project).astype(bf16)
-        d_project, conv_product, out_got = tie(d_project, conv_product, out_got)
+        d_project, conv_product = tie(d_project, conv_product)
+        (conv_product,) = after([conv_product], [both_total])
         conv_total = dp_sum(conv_product)
-        out_keep, out_gives = z_gives(out_mine, out_got)
-        out_parts = [dp_shift_z(give, steps + 1) for steps, give in enumerate(out_gives)]
-    branch_keep, branch_give = halves_sum(branch_mine, branch_got)
     branch_across = xor_seq(branch_give, 2)
     d_normed = input_gradient(d_z, d_project, w_gate, w_conv)
     if fast_mesh():
-        *out_parts, branch_across, d_normed = tie(*out_parts, branch_across, d_normed)
-        grad_w_out = out_keep + sum(part.astype(f32) for part in out_parts)
-    else:
-        grad_w_out = scatter_out(out_product)
+        branch_across, d_normed = tie(branch_across, d_normed)
     mine, got = core_halves(d_normed.reshape(PART, tokens, D))
     keep, give = halves_sum(mine, got)
     small, give = tie(small, give)
     across = xor_seq(give, 2)
+    small, across = tie(dp_total(small), across)
     d_own = keep + across.astype(f32)
     if fast_mesh():
-        (conv_total,) = after([conv_total], [across])
-        grad_gate_in = owners_rows(gate_total)
-        grad_conv_in = owners_rows(conv_total)
+        both_total = after([both_total], [across])[0]
+        small_pieces = seq_pieces(small)
+        gate_rows, out_left, out_right = jnp.split(both_total, [rows_in * PART, rows_in * PART + LANES])
+        grad_w_out = jnp.concatenate([out_left, out_right], axis=1).astype(f32)
+        gate_rows = owners_rows(gate_rows)
+        (conv_total,) = after([conv_total], [small_pieces[3], *gate_rows[1:]])
+        grad_w_in, grad_w_dt, grad_norm_gain = projection_rows(
+            place_me, gate_rows, owners_rows(conv_total), w_in, w_dt, norm_gain
+        )
+        grad_norm_gain = grad_norm_gain[0]
     else:
-        grad_gate_in = scatter_in(gate_product)
+        small_pieces = seq_pieces(small)
+        grad_w_out = scatter_out(dot_tn(rounded_out, cot_all).astype(bf16))
+        grad_gate_in = scatter_in(dot_tn(normed, d_z).astype(bf16))
         grad_conv_in = scatter_in(dot_tn(normed, d_project).astype(bf16))
+        grad_w_in = jnp.concatenate(
+            [
+                from_owner(grad_gate_in),
+                from_owner(grad_conv_in[:, :, :OWN]),
+                grad_conv_in[:, :, CONV_COLS - OWN_BC :].transpose(1, 0, 2).reshape(rows_in, 2 * STATE),
+            ],
+            axis=1,
+        )
+        grad_w_dt = heads_from_owner(grad_conv_in[:, :, OWN : OWN + OWN_HEADS])
+        grad_norm_gain = (
+            jnp.sum(w_in.astype(f32) * grad_w_in, axis=1)
+            + jnp.sum(w_dt.astype(f32) * grad_w_dt, axis=1)
+        ) / norm_gain.astype(f32)
     x_own = hidden_in[0].astype(f32)
     hidden_out = (x_own + branch_keep + branch_across.astype(f32)).astype(bf16)[None]
     own_rms = lax.rsqrt(jnp.mean(x_own * x_own, axis=1, keepdims=True) + epsilon)
@@ -1111,7 +1274,7 @@
     )
     grad_in = (grad_out[0].astype(f32) + d_input).astype(bf16)[None]
 
-    every = jnp.stack(by_partner(seq_pieces(dp_total(small)))).reshape(PART, padded)
+    every = jnp.stack(by_partner(small_pieces)).reshape(PART, padded)
     start = 0
 
     def take(size):
@@ -1127,29 +1290,16 @@
         [from_owner(all_conv), all_conv_bc.transpose(1, 0, 2).reshape(CONV, 2 * STATE)], axis=1
     )
     place = lax.axis_index(("dp", "seq"))
-    gate_rows = gate_gain.shape[0]
-    if gate_rows == LANES:
+    gain_rows = gate_gain.shape[0]
+    if gain_rows == LANES:
         grad_gate_gain = lax.dynamic_slice_in_dim(
-            grad_gate, lax.axis_index("dp") * gate_rows, gate_rows, 0
+            grad_gate, lax.axis_index("dp") * gain_rows, gain_rows, 0
         )
     else:
         start = CONV * OWN + CONV * OWN_BC + 3 * LANES
         whole_gate = from_owner(take(OWN)[:, None, :]).reshape(INNER)
-        grad_gate_gain = lax.dynamic_slice_in_dim(whole_gate, place * gate_rows, gate_rows, 0)
-
-    grad_w_in = jnp.concatenate(
-        [
-            from_owner(grad_gate_in),
-            from_owner(grad_conv_in[:, :, :OWN]),
-            grad_conv_in[:, :, CONV_COLS - OWN_BC :].transpose(1, 0, 2).reshape(rows_in, 2 * STATE),
-        ],
-        axis=1,
-    )
-    grad_w_dt = heads_from_owner(grad_conv_in[:, :, OWN : OWN + OWN_HEADS])
-    grad_norm_gain = (
-        jnp.sum(w_in.astype(f32) * grad_w_in, axis=1)
-        + jnp.sum(w_dt.astype(f32) * grad_w_dt, axis=1)
-    ) / norm_gain.astype(f32)
+        grad_gate_gain = lax.dynamic_slice_in_dim(whole_gate, place * gain_rows, gain_rows, 0)
+
     return (
         hidden_out,
         grad_in,

time: 692 us -> 610 us (0.88)
  waiting for transfers between devices: 240 us -> 200 us
  Pallas kernels: 176 us -> 206 us
  matrix products: 75.8 us -> 46.7 us
  local copies, waits for them, and re-layouts: 82.6 us -> 57.6 us
    dot_general x3 -> x1, matrix products: 45.4 us -> 16.4 us  [dot_tn(): lax.dot_general(a, b, (((0,), (0,)), ((), ())), preferred_element_type=f32)]
    ppermute x9 -> x6, waiting for transfers between devices: 78.2 us -> 49.4 us  [dp_shift_z(): return lax.ppermute(value, 'dp', pairs)]
    pallas_call x0 -> x3, Pallas kernels: none -> 27.6 us  [the longest x1 25.8 us: products(): pl.pallas_call(products_kernel, grid=(count,), in_specs=[pl.BlockSpec((le...]
    ppermute x6 -> x5, waiting for transfers between devices: 34.5 us -> 8.05 us  [dp_swap_x(): return lax.ppermute(value, 'dp', [(d, d ^ 1) for d in range(8)])]
    ppermute x30 -> x32, waiting for transfers between devices: 121 us -> 133 us  [xor_seq(): return lax.ppermute(value, 'seq', [(s, s ^ bits) for s in range(PART)])]
    unnamed x125 -> x121, local copies, waits for them, and re-layouts: 43.1 us -> 33 us
    reduce_scatter x2, waiting for transfers between devices: 0.02 us -> 9.28 us  [dp_sum(): return lax.psum_scatter(product, 'dp', scatter_dimension=0, tiled=True)]
    ppermute x9 -> x6, starting transfers between devices: 16.1 us -> 8.57 us  [dp_shift_z(): return lax.ppermute(value, 'dp', pairs)]
  transfers between devices with their start and end apart: 49 -> 47, of which waited for: 23 -> 23; matrix products, arithmetic and copies ran while one was open for 17% -> 18% of each run, Pallas kernels for 20% -> 23%
where the time goes in v3:
time: 610 us; the launch traced here: 601 us
  Pallas kernels  206 us (34%)
  waiting for transfers between devices  200 us (33%)
  local copies, waits for them, and re-layouts  57.6 us (9%)
  matrix products  46.7 us (8%)
  other arithmetic  39 us (6%)
  starting transfers between devices  36.3 us (6%)
  between operations  15.5 us (3%)
    ppermute x32, waiting for transfers between devices, xor_seq(): return lax.ppermute(value, 'seq', [(s, s ^ bits) for s in range(PART)])  133 us
    pallas_call x1, Pallas kernels, recurrence_backward(): pl.pallas_call(backward_kernel, grid_spec=pltpu.PrefetchScalarGridSpec(nu...  61.6 us
    ppermute x6, waiting for transfers between devices, dp_shift_z(): return lax.ppermute(value, 'dp', pairs)  49.4 us
    unnamed x121, local copies, waits for them, and re-layouts  33 us
    pallas_call x1, Pallas kernels, recurrence_forward(): pl.pallas_call(forward_kernel, grid_spec=pltpu.PrefetchScalarGridSpec(num...  31.4 us
    dot_general x3, matrix products, dot_nn(): lax.dot_general(a, b, (((1,), (0,)), ((), ())), preferred_element_type=f32)  30.3 us
    pallas_call x1, Pallas kernels, input_gradient(): pl.pallas_call(input_gradient_kernel, grid=(length // Q,), in_specs=[pl.B...  26.4 us
    pallas_call x1, Pallas kernels, products(): pl.pallas_call(products_kernel, grid=(count,), in_specs=[pl.BlockSpec((le...  25.8 us
  transfers between devices with their start and end apart: 47, of which 23 were waited for; matrix products, arithmetic and copies ran while one was open for 18% of the time, Pallas kernels for 23%

profile of v3, /device:TPU:8, one launch (start us, length us, event | category | flops | bytes accessed | tf_op | source)
XLA Modules:
  0.0 601.1 jit_solution(12035213710130073795)
XLA Ops:
  15.6 7.2 %collective-permute-done.refs_0_ = bf16[2,64,1152]{2,1,0:T(8,128)(2,1)S(1)} collective-permute-done((bf16[2,64,1152]{2,1,0:T(8,128)(2,1)}, bf16[2,64,1152]{2,1,0:T(8,128)(2,1)S(1)}, u32[]{:S(2)}, u32[]{:S(2)}) %collective-permute-start) | collective-permute-done | bytes 294944 | tf_op jit(solution)/shard_map/ppermute | solution.py:40
  31.9 46.5 %collective-permute-done.3.refs_0_ = bf16[512,2048]{1,0:T(8,128)(2,1)} collective-permute-done((bf16[512,2048]{1,0:T(8,128)(2,1)}, bf16[512,2048]{1,0:T(8,128)(2,1)}, u32[]{:S(2)}, u32[]{:S(2)}) %collective-permute-start.3) | collective-permute-done | bytes 2097184 | tf_op jit(solution)/shard_map/ppermute | solution.py:40
  92.8 44.1 %collective-permute-done.8.refs_0_ = bf16[128,2048]{1,0:T(8,128)(2,1)} collective-permute-done((bf16[128,2048]{1,0:T(8,128)(2,1)S(1)}, bf16[128,2048]{1,0:T(8,128)(2,1)}, u32[]{:S(2)}, u32[]{:S(2)}) %collective-permute-start.8) | collective-permute-done | bytes 524320 | tf_op jit(solution)/shard_map/ppermute | solution.py:97
  144.6 8.3 %all_positions.2.n_ref = bf16[2048,2048]{1,0:T(8,128)(2,1)S(1)} custom-call(s32[4]{0:T(128)S(1)} %pad_add_fusion.order_ref, bf16[512,2048]{1,0:T(8,128)(2,1)S(1)} %bitcast.192, bf16[512,2048]{1,0:T(8,128)(2,1)} %collective-permute-done.7.refs_1_, bf16[512,2048]{1,0:T(8,128)(2,1)} %get-tuple-element.73.refs_2_, ...), custom_call_target="tpu_custom_call" | custom-call | flops 16777216 | bytes 16777216 | tf_op jit(solution)/shard_map/all_positions/pallas_call | solution.py:293
  166.8 14.3 %select_convert_fusion.refs_2_ = bf16[2048,1024]{1,0:T(8,128)(2,1)} fusion(pred[1024]{0:T(1024)(128)(4,1)S(1)} %fusion.37, bf16[2048,2048]{1,0:T(8,128)(2,1)} %copy-done.3, bf16[2048,1152]{1,0:T(8,128)(2,1)} %all-gather.3.cloned.1.call-done.refs_5_.wc_ref), kind=kOutput, calls=%fused_computation | convolution fusion | flops 8594128896 | bytes 16778240 | tf_op jit(solution)/shard_map/dot_general | solution.py:390
  181.1 7.4 %collective-permute-done.6.refs_0_ = bf16[256,2048]{1,0:T(8,128)(2,1)} collective-permute-done((bf16[256,2048]{1,0:T(8,128)(2,1)}, bf16[256,2048]{1,0:T(8,128)(2,1)}, u32[]{:S(2)}, u32[]{:S(2)}) %collective-permute-start.6) | collective-permute-done | bytes 1048608 | tf_op jit(solution)/shard_map/ppermute | solution.py:40
  192.6 31.4 %recurrence_forward.1 = (f32[2048,1024]{1,0:T(8,128)}, bf16[2048,1024]{1,0:T(8,128)(2,1)}, bf16[8,128,1024]{2,1,0:T(8,128)(2,1)}) custom-call(s32[1]{0:T(128)} %bitcast.1.me_ref, bf16[2048,1024]{1,0:T(8,128)(2,1)} %get-tuple-element.74.ci_ref.prev_ref, bf16[1024,128]{1,0:T(8,128)(2,1)} %copy-done.28, bf16[1024,128]{1,0:T(8,128)(2,1)} %collective-permute-done.12.b1, ...), custom_call_target="tpu_custom_call" | custom-call | flops 60000002048 | bytes 16777216 | tf_op jit(solution)/shard_map/recurrence_forward/pallas_call | solution.py:615
  224.2 6.0 %collective-permute-done.19.refs_3_ = bf16[128,2048]{1,0:T(8,128)(2,1)S(1)} collective-permute-done((bf16[128,2048]{1,0:T(8,128)(2,1)}, bf16[128,2048]{1,0:T(8,128)(2,1)S(1)}, u32[]{:S(2)}, u32[]{:S(2)}) %collective-permute-start.19) | collective-permute-done | bytes 524320 | tf_op jit(solution)/shard_map/ppermute | solution.py:101
  245.8 4.5 all_positions.3.t_ref
  256.0 25.6 %gate_forward.1 = (f32[2048,1024]{1,0:T(8,128)}, f32[2048,1024]{1,0:T(8,128)}, f32[8,2048]{1,0:T(8,128)S(1)}) custom-call(bf16[2048,2048]{1,0:T(8,128)(2,1)} %copy-done.3, bf16[2048,2048]{1,0:T(8,128)(2,1)} %copy-done.4, f32[2048,1024]{1,0:T(8,128)} %get-tuple-element.76.y_ref, bf16[2048,1024]{1,0:T(8,128)(2,1)S(1)} %copy-done.34, ...), custom_call_target="tpu_custom_call" | custom-call | flops 17179869184 | bytes 33554432 | tf_op jit(solution)/shard_map/gate_forward/pallas_call | solution.py:885
  287.5 11.7 %gate_backward.1 = (bf16[2048,1024]{1,0:T(8,128)(2,1)S(1)}, bf16[2048,1024]{1,0:T(8,128)(2,1)S(1)}, bf16[2048,1024]{1,0:T(8,128)(2,1)S(1)}, f32[8,1024]{1,0:T(8,128)S(1)}) custom-call(f32[2048,1024]{1,0:T(8,128)S(1)} %bitcast.196, f32[2048,1024]{1,0:T(8,128)} %get-tuple-element.89.z_ref, f32[2048,1024]{1,0:T(8,128)} %get-tuple-element.90.d_ref, ...), custom_call_target="tpu_custom_call" | custom-call | flops 62914560 | bytes 37748736 | tf_op jit(solution)/shard_map/gate_backward/pallas_call | solution.py:945
  303.2 25.8 %products.1.refs_1_ = bf16[8,512,1024]{2,1,0:T(8,128)(2,1)} custom-call(bf16[2048,2048]{1,0:T(8,128)(2,1)} %copy-done.3, bf16[2048,1024]{1,0:T(8,128)(2,1)S(1)} %get-tuple-element.93.z_ref, bf16[2048,1024]{1,0:T(8,128)(2,1)} %copy-done.10, bf16[2048,2048]{1,0:T(8,128)(2,1)} %copy-done.4), custom_call_target="tpu_custom_call" | custom-call | flops 17179869184 | bytes 33554432 | tf_op jit(solution)/shard_map/products/pallas_call | solution.py:1002
  329.0 61.6 %recurrence_backward.1 = (bf16[2048,1152]{1,0:T(8,128)(2,1)}, bf16[4,1024,128]{2,1,0:T(8,128)(2,1)}, f32[2048,128]{1,0:T(8,128)}, f32[8,1024]{1,0:T(8,128)}, f32[8,128]{1,0:T(8,128)}) custom-call(s32[1]{0:T(128)} %bitcast.1.me_ref, bf16[2048,1024]{1,0:T(8,128)(2,1)} %get-tuple-element.74.ci_ref.prev_ref, ...), custom_call_target="tpu_custom_call" | custom-call | flops 70000001024 | bytes 16777216 | tf_op jit(solution)/shard_map/recurrence_backward/pallas_call | solution.py:809
  390.6 12.2 %convolution_convert_fusion.1 = bf16[2048,2048]{1,0:T(8,128)(2,1)S(1)} fusion(bf16[2048,1024]{1,0:T(8,128)(2,1)} %get-tuple-element.98, bf16[1024,2048]{1,0:T(8,128)(2,1)} %copy-done.9), kind=kOutput, calls=%fused_computation.2 | convolution fusion | flops 8594128896 | bytes 16777216 | tf_op jit(solution)/shard_map/dot_general | solution.py:390
  408.7 6.9 %collective-permute-done.25 = bf16[2,1024,128]{2,1,0:T(8,128)(2,1)} collective-permute-done((bf16[2,1024,128]{2,1,0:T(8,128)(2,1)}, bf16[2,1024,128]{2,1,0:T(8,128)(2,1)}, u32[]{:S(2)}, u32[]{:S(2)}) %collective-permute-start.25) | collective-permute-done | bytes 524320 | tf_op jit(solution)/shard_map/ppermute | solution.py:40
  419.4 4.4 fusion.13.refs_1_
  434.5 16.4 %convolution_convert_fusion.refs_1_ = bf16[2048,1152]{1,0:T(8,128)(2,1)} fusion(bf16[2048,2048]{1,0:T(8,128)(2,1)} %copy-done.3, bf16[2048,1152]{1,0:T(8,128)(2,1)} %get-tuple-element.104.refs_0_), kind=kOutput, calls=%fused_computation.1 | convolution fusion | flops 9666035712 | bytes 17825792 | tf_op jit(solution)/shard_map/dot_general | solution.py:398
  450.9 26.4 %input_gradient.1.refs_1_ = bf16[2048,2048]{1,0:T(8,128)(2,1)} custom-call(bf16[2048,1024]{1,0:T(8,128)(2,1)} %copy-done.35, bf16[2048,1152]{1,0:T(8,128)(2,1)} %get-tuple-element.105.p_ref, bf16[2048,1024]{1,0:T(8,128)(2,1)} %all-gather.5.cloned.1.call-done.wg_ref, bf16[2048,1152]{1,0:T(8,128)(2,1)} %all-gather.3.cloned.1.call-done.refs_5_.wc_ref), custom_call_target="tpu_custom_call" | custom-call | flops 10000000000 | bytes 4194304 | tf_op jit(solution)/shard_map/input_gradient/pallas_call | solution.py:969
  477.3 4.8 dynamic-slice_bitcast_fusion
  484.7 4.9 collective-permute-done.28
  507.2 34.9 %collective-permute-done.33.refs_1_ = bf16[512,2048]{1,0:T(8,128)(2,1)} collective-permute-done((bf16[512,2048]{1,0:T(8,128)(2,1)}, bf16[512,2048]{1,0:T(8,128)(2,1)}, u32[]{:S(2)}, u32[]{:S(2)}) %collective-permute-start.33) | collective-permute-done | bytes 2097184 | tf_op jit(solution)/shard_map/ppermute | solution.py:40
  542.7 4.6 fusion.2
  547.9 8.7 %fusion.16 = (bf16[1,512,2048]{2,1,0:T(8,128)(2,1)}, bf16[1,512,2048]{2,1,0:T(8,128)(2,1)}) fusion(bf16[512,2048]{1,0:T(8,128)(2,1)} %get-tuple-element.114.refs_1_, f32[512]{0:T(512)S(1)} %broadcast_multiply_fusion, f32[512]{0:T(512)S(1)} %get-tuple-element.155, f32[2048]{0:T(1024)S(1)} %copy-done.45, f32[512]{0:T(512)S(1)} %get-tuple-element.154, ...), kind=kLoop, calls=%fused_computation.27 | loop fusion | flops 22020096 | bytes 20985868 | tf_op jit(solution)/shard_map/broadcast_in_dim | solution.py:1275
  570.5 9.3 %reduce-scatter.5.cloned.1.call-done.refs_0_ = bf16[256,1152]{1,0:T(8,128)(2,1)} async-done(((bf16[2048,1152]{1,0:T(8,128)(2,1)}), bf16[256,1152]{1,0:T(8,128)(2,1)}) %reduce-scatter.5.cloned.1.call-update) | async-done | bytes 589840 | tf_op jit(solution)/shard_map/reduce_scatter | solution.py:351
  (330 shorter events, 157.8 us)
Async XLA Ops:
  7.2 132.0 %all-gather.3.cloned.1.call-start = ((), (), s32[]{:S(2)}) async-start(), calls=%async_computation.2 | async-start | bytes 5308416 | tf_op jit(solution)/shard_map/all_gather | solution.py:235
  7.2 15.5 %collective-permute-start.1 = (bf16[128,2048]{1,0:T(8,128)(2,1)}, bf16[128,2048]{1,0:T(8,128)(2,1)S(1)}, u32[]{:S(2)}, u32[]{:S(2)}) collective-permute-start(bf16[128,2048]{1,0:T(8,128)(2,1)} %refs_0_.1), channel_id=1, source_target_pairs={{0,8},{4,12},{8,16},{12,20},{16,24},{20,28},{24,0},{28,4},{1,9},{5... | collective-permute-start | bytes 1572872 | tf_op jit(solution)/shard_map/ppermute | solution.py:97
  30.4 48.0 %collective-permute-start.3 = (bf16[512,2048]{1,0:T(8,128)(2,1)}, bf16[512,2048]{1,0:T(8,128)(2,1)}, u32[]{:S(2)}, u32[]{:S(2)}) collective-permute-start(bf16[512,2048]{1,0:T(8,128)(2,1)} %after.7), channel_id=1, source_target_pairs={{0,2},{1,3},{2,0},{3,1},{4,6},{5,7},{6,4},{7,5},{8,10},{9,11},{10,... | collective-permute-start | bytes 6291464 | tf_op jit(solution)/shard_map/ppermute | solution.py:40
  80.9 62.7 %collective-permute-start.7 = (bf16[512,2048]{1,0:T(8,128)(2,1)S(1)}, bf16[512,2048]{1,0:T(8,128)(2,1)}, u32[]{:S(2)}, u32[]{:S(2)}) collective-permute-start(bf16[512,2048]{1,0:T(8,128)(2,1)S(1)} %bitcast.191), channel_id=1, source_target_pairs={{0,1},{1,0},{2,3},{3,2},{4,5},{5,4},{6,7},{7,6},{8,9},{9,8},{10,11... | collective-permute-start | bytes 6291464 | tf_op jit(solution)/shard_map/ppermute | solution.py:40
  80.9 56.0 %collective-permute-start.8 = (bf16[128,2048]{1,0:T(8,128)(2,1)S(1)}, bf16[128,2048]{1,0:T(8,128)(2,1)}, u32[]{:S(2)}, u32[]{:S(2)}) collective-permute-start(bf16[128,2048]{1,0:T(8,128)(2,1)S(1)} %copy-done.20), channel_id=1, source_target_pairs={{0,16},{4,20},{8,24},{12,28},{16,0},{20,4},{24,8},{28,12},{1,17},{... | collective-permute-start | bytes 1572872 | tf_op jit(solution)/shard_map/ppermute | solution.py:97
  82.4 56.8 %collective-permute-start.9 = (bf16[128,2048]{1,0:T(8,128)(2,1)S(1)}, bf16[128,2048]{1,0:T(8,128)(2,1)}, u32[]{:S(2)}, u32[]{:S(2)}) collective-permute-start(bf16[128,2048]{1,0:T(8,128)(2,1)S(1)} %copy-done.20), channel_id=1, source_target_pairs={{0,24},{4,28},{8,0},{12,4},{16,8},{20,12},{24,16},{28,20},{1,25},{... | collective-permute-start | bytes 1572872 | tf_op jit(solution)/shard_map/ppermute | solution.py:97
  84.0 55.2 %collective-permute-start.10 = (bf16[128,2048]{1,0:T(8,128)(2,1)S(1)}, bf16[128,2048]{1,0:T(8,128)(2,1)S(1)}, u32[]{:S(2)}, u32[]{:S(2)}) collective-permute-start(bf16[128,2048]{1,0:T(8,128)(2,1)S(1)} %copy-done.20), channel_id=1, source_target_pairs={{0,4},{4,0},{8,12},{12,8},{16,20},{20,16},{24,28},{28,24},{1,5},{5... | collective-permute-start | bytes 1572872 | tf_op jit(solution)/shard_map/ppermute | solution.py:101
  92.8 160.8 %all-gather.5.cloned.1.call-start = ((), (), s32[]{:S(2)}) async-start(), calls=%async_computation.3 | async-start | bytes 4718592 | tf_op jit(solution)/shard_map/all_gather | solution.py:245
  140.1 105.7 %collective-permute-start.15 = (bf16[512,2048]{1,0:T(8,128)(2,1)}, bf16[512,2048]{1,0:T(8,128)(2,1)}, u32[]{:S(2)}, u32[]{:S(2)}) collective-permute-start(bf16[512,2048]{1,0:T(8,128)(2,1)} %bitcast.193), channel_id=1, source_target_pairs={{0,1},{1,0},{2,3},{3,2},{4,5},{5,4},{6,7},{7,6},{8,9},{9,8},{10,11... | collective-permute-start | bytes 6291464 | tf_op jit(solution)/shard_map/ppermute | solution.py:40
  160.6 63.4 %collective-permute-start.17 = (bf16[128,2048]{1,0:T(8,128)(2,1)}, bf16[128,2048]{1,0:T(8,128)(2,1)}, u32[]{:S(2)}, u32[]{:S(2)}) collective-permute-start(bf16[128,2048]{1,0:T(8,128)(2,1)} %get-tuple-element.79.refs_1_), channel_id=1, source_target_pairs={{0,4},{4,0},{8,12},{12,8},{16,20},{20,16},{24,28},{28,24},{1,5},{5... | collective-permute-start | bytes 1572872 | tf_op jit(solution)/shard_map/ppermute | solution.py:101
  162.1 26.3 %collective-permute-start.6 = (bf16[256,2048]{1,0:T(8,128)(2,1)}, bf16[256,2048]{1,0:T(8,128)(2,1)}, u32[]{:S(2)}, u32[]{:S(2)}) collective-permute-start(bf16[256,2048]{1,0:T(8,128)(2,1)} %get-tuple-element.70), channel_id=1, source_target_pairs={{0,2},{1,3},{2,0},{3,1},{4,6},{5,7},{6,4},{7,5},{8,10},{9,11},{10,... | collective-permute-start | bytes 3145736 | tf_op jit(solution)/shard_map/ppermute | solution.py:40
  162.7 319.5 %reduce-scatter.3.cloned.1.call-start = ((), (), s32[]{:S(2)}) async-start(), calls=%async_computation.4 | async-start | bytes 9437184 | tf_op jit(solution)/shard_map/reduce_scatter | solution.py:351
  162.7 27.2 %collective-permute-start.12 = (bf16[1024,128]{1,0:T(8,128)(2,1)S(1)}, bf16[1024,128]{1,0:T(8,128)(2,1)}, u32[]{:S(2)}, u32[]{:S(2)}) collective-permute-start(bf16[1024,128]{1,0:T(8,128)(2,1)S(1)} %bc_forward.1.b0), channel_id=1, source_target_pairs={{0,1},{1,0},{2,3},{3,2},{4,5},{5,4},{6,7},{7,6},{8,9},{9,8},{10,11... | collective-permute-start | bytes 786440 | tf_op jit(solution)/shard_map/ppermute | solution.py:40
  166.8 23.7 %collective-permute-start.14 = (bf16[1024,128]{1,0:T(8,128)(2,1)}, bf16[1024,128]{1,0:T(8,128)(2,1)}, u32[]{:S(2)}, u32[]{:S(2)}) collective-permute-start(bf16[1024,128]{1,0:T(8,128)(2,1)} %collective-permute-done.13.b2), channel_id=1, source_target_pairs={{0,1},{1,0},{2,3},{3,2},{4,5},{5,4},{6,7},{7,6},{8,9},{9,8},{10,11... | collective-permute-start | bytes 786440 | tf_op jit(solution)/shard_map/ppermute | solution.py:40
  188.5 35.7 %collective-permute-start.18 = (bf16[128,2048]{1,0:T(8,128)(2,1)}, bf16[128,2048]{1,0:T(8,128)(2,1)}, u32[]{:S(2)}, u32[]{:S(2)}) collective-permute-start(bf16[128,2048]{1,0:T(8,128)(2,1)} %get-tuple-element.80.refs_2_), channel_id=1, source_target_pairs={{0,4},{4,0},{8,12},{12,8},{16,20},{20,16},{24,28},{28,24},{1,5},{5... | collective-permute-start | bytes 1572872 | tf_op jit(solution)/shard_map/ppermute | solution.py:101
  190.0 40.2 %collective-permute-start.19 = (bf16[128,2048]{1,0:T(8,128)(2,1)}, bf16[128,2048]{1,0:T(8,128)(2,1)S(1)}, u32[]{:S(2)}, u32[]{:S(2)}) collective-permute-start(bf16[128,2048]{1,0:T(8,128)(2,1)} %get-tuple-element.81.refs_3_), channel_id=1, source_target_pairs={{0,4},{4,0},{8,12},{12,8},{16,20},{20,16},{24,28},{28,24},{1,5},{5... | collective-permute-start | bytes 1572872 | tf_op jit(solution)/shard_map/ppermute | solution.py:101
  190.5 39.7 %collective-permute-start.16 = (bf16[256,2048]{1,0:T(8,128)(2,1)}, bf16[256,2048]{1,0:T(8,128)(2,1)S(1)}, u32[]{:S(2)}, u32[]{:S(2)}) collective-permute-start(bf16[256,2048]{1,0:T(8,128)(2,1)} %get-tuple-element.78), channel_id=1, source_target_pairs={{0,2},{1,3},{2,0},{3,1},{4,6},{5,7},{6,4},{7,5},{8,10},{9,11},{10,... | collective-permute-start | bytes 3145736 | tf_op jit(solution)/shard_map/ppermute | solution.py:40
  224.1 21.7 %collective-permute-start.20 = (bf16[256,2048]{1,0:T(8,128)(2,1)}, bf16[256,2048]{1,0:T(8,128)(2,1)}, u32[]{:S(2)}, u32[]{:S(2)}) collective-permute-start(bf16[256,2048]{1,0:T(8,128)(2,1)} %get-tuple-element.77.refs_2_), channel_id=1, source_target_pairs={{0,1},{1,0},{2,3},{3,2},{4,5},{5,4},{6,7},{7,6},{8,9},{9,8},{10,11... | collective-permute-start | bytes 3145736 | tf_op jit(solution)/shard_map/ppermute | solution.py:40
  232.0 13.8 %collective-permute-start.21 = (bf16[256,2048]{1,0:T(8,128)(2,1)}, bf16[256,2048]{1,0:T(8,128)(2,1)S(1)}, u32[]{:S(2)}, u32[]{:S(2)}) collective-permute-start(bf16[256,2048]{1,0:T(8,128)(2,1)} %get-tuple-element.83.refs_3_), channel_id=1, source_target_pairs={{0,1},{1,0},{2,3},{3,2},{4,5},{5,4},{6,7},{7,6},{8,9},{9,8},{10,11... | collective-permute-start | bytes 3145736 | tf_op jit(solution)/shard_map/ppermute | solution.py:40
  328.9 250.8 %reduce-scatter.5.cloned.1.call-start = ((), (), s32[]{:S(2)}) async-start(), calls=%async_computation.5 | async-start | bytes 5308416 | tf_op jit(solution)/shard_map/reduce_scatter | solution.py:351
  407.4 12.0 %collective-permute-start.24 = (bf16[2,512,2048]{2,1,0:T(8,128)(2,1)}, bf16[2,512,2048]{2,1,0:T(8,128)(2,1)}, u32[]{:S(2)}, u32[]{:S(2)}) collective-permute-start(bf16[2,512,2048]{2,1,0:T(8,128)(2,1)} %dynamic-slice_bitcast_fusion.1), channel_id=1, source_target_pairs={{0,1},{1,0},{2,3},{3,2},{4,5},{5,4},{6,7},{7,6},{8,9},{9,8},{10,11... | collective-permute-start | bytes 12582920 | tf_op jit(solution)/shard_map/ppermute | solution.py:40
  426.9 50.4 %collective-permute-start.27 = (bf16[512,2048]{1,0:T(8,128)(2,1)}, bf16[512,2048]{1,0:T(8,128)(2,1)}, u32[]{:S(2)}, u32[]{:S(2)}) collective-permute-start(bf16[512,2048]{1,0:T(8,128)(2,1)} %get-tuple-element.100), channel_id=1, source_target_pairs={{0,2},{1,3},{2,0},{3,1},{4,6},{5,7},{6,4},{7,5},{8,10},{9,11},{10,... | collective-permute-start | bytes 6291464 | tf_op jit(solution)/shard_map/ppermute | solution.py:40
  494.1 48.0 %collective-permute-start.33 = (bf16[512,2048]{1,0:T(8,128)(2,1)}, bf16[512,2048]{1,0:T(8,128)(2,1)}, u32[]{:S(2)}, u32[]{:S(2)}) collective-permute-start(bf16[512,2048]{1,0:T(8,128)(2,1)} %get-tuple-element.113), channel_id=1, source_target_pairs={{0,2},{1,3},{2,0},{3,1},{4,6},{5,7},{6,4},{7,5},{8,10},{9,11},{10,... | collective-permute-start | bytes 6291464 | tf_op jit(solution)/shard_map/ppermute | solution.py:40
  542.7 13.9 %collective-permute-start.42 = (f32[48,128]{1,0:T(8,128)}, f32[48,128]{1,0:T(8,128)S(1)}, u32[]{:S(2)}, u32[]{:S(2)}) collective-permute-start(f32[48,128]{1,0:T(8,128)} %get-tuple-element.117), channel_id=1, source_target_pairs={{0,1},{1,0},{2,3},{3,2},{4,5},{5,4},{6,7},{7,6},{8,9},{9,8},{10,11... | collective-permute-start | bytes 73736 | tf_op jit(solution)/shard_map/ppermute | solution.py:40
  (79 other events, 667.8 us)
Sparse Core Ops, SparseCore 0:
  29.1 107.2 all-gather.2
  162.8 86.0 all-gather.4
  329.1 147.4 reduce-scatter.2
  482.3 97.4 reduce-scatter.4

commit v4 on v3

--- a/solution.py
+++ b/solution.py
@@ -24,6 +24,7 @@
 CONV_COLS = OWN + LANES
 Q = 256
 HALF = Q // 2
+WIDE = 512
 
 epsilon = 1e-05
 highest = lax.Precision.HIGHEST
@@ -84,8 +85,7 @@
 
 
 def seq_total(value):
-    value = value + xor_seq(value, 1)
-    return value + xor_seq(value, 2)
+    return value + xor_seq(value, 1) + xor_seq(value, 2) + xor_seq(value, 3)
 
 
 def fast_mesh():
@@ -233,14 +233,17 @@
 def gather_everything(conv_pieces, gate_pieces, o, x_block, cot_block):
     c, (o1,) = seq_pass(conv_pieces, dp_shift_z(o, 1))
     w_conv = lax.all_gather(c, "dp", axis=0, tiled=True)
-    x_across, gate_pieces = tie(xor_seq(after([x_block], [c])[0], 2), gate_pieces)
+    x_across, gate_pieces, o2, o3, o_x = tie(
+        xor_seq(after([x_block], [c])[0], 2),
+        gate_pieces,
+        dp_shift_z(o, 2),
+        dp_shift_z(o, 3),
+        dp_swap_x(o),
+    )
     g, _ = seq_pass(gate_pieces)
     half = cot_block.shape[0] // 2
     cot_a, cot_b = after([cot_block[:half], cot_block[half:]], [g])
-    cot_a = xor_seq(cot_a, 2)
-    o2, o3, o_x, g, x_across = after(
-        [dp_shift_z(o, 2), dp_shift_z(o, 3), dp_swap_x(o), g, x_across], [w_conv]
-    )
+    g, x_across, cot_a = after([g, x_across, xor_seq(cot_a, 2)], [w_conv])
     x_pieces = (x_block, xor_seq(x_block, 1), x_across, xor_seq(x_across, 1))
     w_gate = lax.all_gather(g, "dp", axis=0, tiled=True)
     return w_conv, w_gate, [o, o1, o2, o3, o_x], x_pieces, (cot_a, cot_b)
@@ -542,8 +545,15 @@
     return v, steps, running, shifted, end
 
 
+def spread_heads(values, spread):
+    high = values.astype(bf16)
+    low = (values - high.astype(f32)).astype(bf16)
+    return dot_nn(high, spread) + dot_nn(low, spread)
+
+
 def forward_kernel(
-    me_ref, ci_ref, b0, b1, b2, b3, dt_ref, cw_ref, rows_ref, skip_ref, y_ref, act_ref, s_ref, state, xf
+    me_ref, ci_ref, b0, b1, b2, b3, dt_ref, cw_ref, rows_ref, skip_ref, y_ref, act_ref, s_ref, state, xf,
+    e_wide, w_wide
 ):
     @pl.when(pl.program_id(0) == 0)
     def _():
@@ -567,6 +577,12 @@
         jnp.int32, (HALF, HALF), 1
     )
     left = lax.broadcasted_iota(jnp.int32, (1, LANES), 1) < HEAD_DIM
+    spread = lax.broadcasted_iota(jnp.int32, (LANES, OWN), 0) == (
+        lax.broadcasted_iota(jnp.int32, (LANES, OWN), 1) // HEAD_DIM
+    )
+    spread = jnp.where(spread, 1.0, 0.0).astype(bf16)
+    e_wide[...] = spread_heads(e_run, spread)
+    w_wide[...] = spread_heads(w_end, spread)
     s_ref[0] = state[...].astype(bf16)
     for strip in range(STRIPS):
         at = slice(strip * LANES, (strip + 1) * LANES)
@@ -577,13 +593,11 @@
         act = (pre * sigmoid(pre)).astype(bf16)
         act_ref[:, at] = act
         actf = act.astype(f32)
-        inter = dot_nn(reads, s_ref[0, :, at]) * jnp.where(
-            left, e_run[:, h0 : h0 + 1], e_run[:, h1 : h1 + 1]
-        )
+        inter = dot_nn(reads, s_ref[0, :, at]) * e_wide[:, at]
         inter = inter + skip_ref[0:1, at] * actf
         top, bottom = inter[:HALF], inter[HALF:]
         for h, side in ((h0, left), (h1, jnp.logical_not(left))):
-            x_h = jnp.where(side, actf, 0.0).astype(bf16)
+            x_h = jnp.where(side, act, jnp.zeros_like(act))
             m00 = jnp.where(
                 causal,
                 jnp.exp2(running[:HALF, h : h + 1] - shifted_t[h : h + 1, :HALF]) * cb[:HALF, :HALF],
@@ -601,7 +615,7 @@
             )
         y_ref[:HALF, at] = top
         y_ref[HALF:, at] = bottom
-        weighted = (actf * jnp.where(left, w_end[:, h0 : h0 + 1], w_end[:, h1 : h1 + 1])).astype(bf16)
+        weighted = (actf * w_wide[:, at]).astype(bf16)
         state[:, at] = state[:, at] * jnp.where(
             left, e_end[:, h0 : h0 + 1], e_end[:, h1 : h1 + 1]
         ) + dot_nn(keys_t, weighted)
@@ -630,7 +644,12 @@
                 pl.BlockSpec((Q, OWN), along),
                 pl.BlockSpec((1, STATE, OWN), lambda i, me: (i, 0, 0)),
             ],
-            scratch_shapes=[pltpu.VMEM((STATE, OWN), f32), pltpu.VMEM((Q + 8, OWN), f32)],
+            scratch_shapes=[
+                pltpu.VMEM((STATE, OWN), f32),
+                pltpu.VMEM((Q + 8, OWN), f32),
+                pltpu.VMEM((Q, OWN), f32),
+                pltpu.VMEM((Q, OWN), f32),
+            ],
         ),
         out_shape=[
             jax.ShapeDtypeStruct((length, OWN), f32),
@@ -641,7 +660,7 @@
             dimension_semantics=("arbitrary",), vmem_limit_bytes=60 * 2**20
         ),
         cost_estimate=pl.CostEstimate(
-            flops=60 * 10**9, bytes_accessed=2**24, transcendentals=10**7
+            flops=40 * 10**9, bytes_accessed=2**24, transcendentals=10**7
         ),
         name="recurrence_forward",
     )(me, conv_in, *bc, dt_tile, taps, rows, skip_row)
@@ -865,50 +884,91 @@
     )(me, conv_in, conv_in, act, dy, y, *bc, dt_tile, entry, taps, rows, skip_row)
 
 
-def gate_forward_kernel(n_ref, t_ref, y_ref, wg_ref, wo_ref, row_ref, z_ref, d_ref, sums_ref):
+def pull_out_kernel(order_ref, own, sibling, across_a, across_b, corner_a, corner_b, wo_ref, cot_ref, d_ref):
+    del order_ref
+    step = pl.program_id(0)
+    half = across_a.shape[0]
+    for k, ref in enumerate((own, sibling)):
+
+        @pl.when(step == k)
+        def _():
+            cot_ref[...] = ref[...]
+
+    for k, (first, second) in enumerate(((across_a, across_b), (corner_a, corner_b))):
+
+        @pl.when(step == 2 + k)
+        def _():
+            cot_ref[:half, :] = first[...]
+            cot_ref[half:, :] = second[...]
+
+    d_ref[...] = dot_nt(cot_ref[...], wo_ref[...])
+
+
+def pull_out(pieces, order, w_o):
+    tile = pieces[0].shape[0]
+    whole = lambda i, order: (0, 0)
+    there = lambda i, order: (order[i], 0)
+    length = tile * PART
+    return pl.pallas_call(
+        pull_out_kernel,
+        grid_spec=pltpu.PrefetchScalarGridSpec(
+            num_scalar_prefetch=1,
+            grid=(PART,),
+            in_specs=[pl.BlockSpec(piece.shape, whole) for piece in pieces]
+            + [pl.BlockSpec((OWN, D), whole)],
+            out_specs=[pl.BlockSpec((tile, D), there), pl.BlockSpec((tile, OWN), there)],
+        ),
+        out_shape=[
+            jax.ShapeDtypeStruct((length, D), bf16),
+            jax.ShapeDtypeStruct((length, OWN), f32),
+        ],
+        compiler_params=pltpu.CompilerParams(vmem_limit_bytes=52 * 2**20),
+        cost_estimate=pl.CostEstimate(
+            flops=2 * length * D * OWN, bytes_accessed=2**25, transcendentals=0
+        ),
+        name="pull_out",
+    )(order, *pieces, w_o)
+
+
+def gate_forward_kernel(n_ref, y_ref, d_ref, wg_ref, row_ref, z_ref, sums_ref):
     z = dot_nn(n_ref[...], wg_ref[...]) * row_ref[1:2, :]
-    d = dot_nt(t_ref[...], wo_ref[...])
     z_ref[...] = z
-    d_ref[...] = d
     gated = y_ref[...] * (z * sigmoid(z))
     squares = jnp.sum(gated * gated, axis=1, keepdims=True)
-    cross = jnp.sum(d * row_ref[0:1, :] * gated, axis=1, keepdims=True)
+    cross = jnp.sum(d_ref[...] * row_ref[0:1, :] * gated, axis=1, keepdims=True)
     lane = lax.broadcasted_iota(jnp.int32, (1, LANES), 1)
     both = jnp.where(lane == 0, squares, jnp.where(lane == 1, cross, 0.0))
     sums_ref[...] = both.T[0:8, :]
 
 
-def gate_forward(normed, cot, y, w_gate, w_o, row):
+def gate_forward(normed, y, d, w_gate, row):
     length = normed.shape[0]
     whole = lambda i: (0, 0)
     along = lambda i: (i, 0)
     return pl.pallas_call(
         gate_forward_kernel,
-        grid=(length // Q,),
+        grid=(length // WIDE,),
         in_specs=[
-            pl.BlockSpec((Q, D), along),
-            pl.BlockSpec((Q, D), along),
-            pl.BlockSpec((Q, OWN), along),
+            pl.BlockSpec((WIDE, D), along),
+            pl.BlockSpec((WIDE, OWN), along),
+            pl.BlockSpec((WIDE, OWN), along),
             pl.BlockSpec((D, OWN), whole),
-            pl.BlockSpec((OWN, D), whole),
             pl.BlockSpec((8, OWN), whole),
         ],
         out_specs=[
-            pl.BlockSpec((Q, OWN), along),
-            pl.BlockSpec((Q, OWN), along),
-            pl.BlockSpec((8, Q), lambda i: (0, i)),
+            pl.BlockSpec((WIDE, OWN), along),
+            pl.BlockSpec((8, WIDE), lambda i: (0, i)),
         ],
         out_shape=[
             jax.ShapeDtypeStruct((length, OWN), f32),
-            jax.ShapeDtypeStruct((length, OWN), f32),
             jax.ShapeDtypeStruct((8, length), f32),
         ],
-        compiler_params=pltpu.CompilerParams(vmem_limit_bytes=48 * 2**20),
+        compiler_params=pltpu.CompilerParams(vmem_limit_bytes=52 * 2**20),
         cost_estimate=pl.CostEstimate(
-            flops=4 * length * D * OWN, bytes_accessed=2**25, transcendentals=length * OWN
+            flops=2 * length * D * OWN, bytes_accessed=2**25, transcendentals=length * OWN
         ),
         name="gate_forward",
-    )(normed, cot, y, w_gate, w_o, row)
+    )(normed, y, d, w_gate, row)
 
 
 def gate_backward_kernel(y_ref, z_ref, d_ref, sums_ref, row_ref, out_ref, dy_ref, dz_ref, gain_ref):
@@ -968,14 +1028,14 @@
     along = lambda i: (i, 0)
     return pl.pallas_call(
         input_gradient_kernel,
-        grid=(length // Q,),
+        grid=(length // WIDE,),
         in_specs=[
-            pl.BlockSpec((Q, OWN), along),
-            pl.BlockSpec((Q, CONV_COLS), along),
+            pl.BlockSpec((WIDE, OWN), along),
+            pl.BlockSpec((WIDE, CONV_COLS), along),
             pl.BlockSpec((D, OWN), whole),
             pl.BlockSpec((D, CONV_COLS), whole),
         ],
-        out_specs=pl.BlockSpec((Q, D), along),
+        out_specs=pl.BlockSpec((WIDE, D), along),
         out_shape=jax.ShapeDtypeStruct((length, D), bf16),
         compiler_params=pltpu.CompilerParams(vmem_limit_bytes=60 * 2**20),
         cost_estimate=pl.CostEstimate(
@@ -986,31 +1046,34 @@
 
 
 def products_kernel(n_ref, z_ref, r_ref, t_ref, out_ref):
-    rows = n_ref.shape[1]
-    half = r_ref.shape[1]
-    out_ref[0, :rows, :] = dot_nn(n_ref[...].T, z_ref[...]).astype(bf16)
-    product = dot_nn(r_ref[...].T, t_ref[...]).astype(bf16)
-    out_ref[0, rows : rows + half, :] = product[:, :OWN]
-    out_ref[0, rows + half :, :] = product[:, OWN:]
+    rows = D // STRIPS
+    gate = dot_nn(n_ref[...].T, z_ref[...]).astype(bf16)
+    rest = dot_nn(r_ref[...].T, t_ref[...]).astype(bf16)
+    for k in range(out_ref.shape[0]):
+        out_ref[k, :rows, :] = gate[k * rows : (k + 1) * rows]
+        product = rest[k * LANES : (k + 1) * LANES]
+        out_ref[k, rows : rows + LANES, :] = product[:, :OWN]
+        out_ref[k, rows + LANES :, :] = product[:, OWN:]
 
 
 def products(normed, d_z, rounded_out, cot):
     length = normed.shape[0]
-    count = STRIPS
+    rows = D // STRIPS
+    each = 2
     whole = lambda i: (0, 0)
     across = lambda i: (0, i)
     return pl.pallas_call(
         products_kernel,
-        grid=(count,),
+        grid=(STRIPS // each,),
         in_specs=[
-            pl.BlockSpec((length, D // count), across),
+            pl.BlockSpec((length, each * rows), across),
             pl.BlockSpec((length, OWN), whole),
-            pl.BlockSpec((length, LANES), across),
+            pl.BlockSpec((length, each * LANES), across),
             pl.BlockSpec((length, D), whole),
         ],
-        out_specs=pl.BlockSpec((1, D // count + 2 * LANES, OWN), lambda i: (i, 0, 0)),
-        out_shape=jax.ShapeDtypeStruct((count, D // count + 2 * LANES, OWN), bf16),
-        compiler_params=pltpu.CompilerParams(vmem_limit_bytes=48 * 2**20),
+        out_specs=pl.BlockSpec((each, rows + 2 * LANES, OWN), lambda i: (i, 0, 0)),
+        out_shape=jax.ShapeDtypeStruct((STRIPS, rows + 2 * LANES, OWN), bf16),
+        compiler_params=pltpu.CompilerParams(vmem_limit_bytes=56 * 2**20),
         cost_estimate=pl.CostEstimate(
             flops=4 * length * D * OWN, bytes_accessed=2**25, transcendentals=0
         ),
@@ -1160,23 +1223,25 @@
 
     normed = all_positions(x_pieces, order, jnp.broadcast_to(gain_row, (8, D)))
     dt_tile = dot_nn(normed, w_conv[:, OWN:])
-    bc = seq_pieces(bc_forward(dt_tile, taps_tile))
+    bc = bc_forward(dt_tile, taps_tile)
+    bc = [bc] + [xor_seq(bc, bits) for bits in range(1, PART)]
     conv_in = jnp.where(unit_used, dot_nn(normed, w_conv[:, :OWN]), 0.0).astype(bf16)
     if fast_mesh():
         w_o += [dp_swap_x(piece) for piece in w_o[1:4]]
-    if not fast_mesh():
+    else:
         cot_a = xor_seq(cot_a, 2)
-    cot_a, cot_b, conv_in = tie(cot_a, cot_b, conv_in)
+    cot_b, conv_in, *bc[1:] = tie(cot_b, conv_in, *bc[1:])
     cot_b = xor_seq(cot_b, 2)
     y, act, entry = recurrence_forward(place_me, conv_in, bc, dt_tile, taps, rows, skip_row)
     if fast_mesh():
         cot_b, *w_o[5:] = after([cot_b, *w_o[5:]], [entry])
+        w_o = assemble(w_o, out_places(), 512)
+    else:
+        (cot_b,) = after([cot_b], [entry])
     cot_pieces = (
         grad_out[0], xor_seq(grad_out[0], 1), cot_a, cot_b, xor_seq(cot_a, 1), xor_seq(cot_b, 1)
     )
-    cot_all = all_positions(cot_pieces, order)
-    if fast_mesh():
-        w_o = assemble(w_o, out_places(), 512)
+    cot_all, d_rounded = pull_out(cot_pieces, order, w_o)
     row = jnp.concatenate(
         [
             gate_row,
@@ -1185,7 +1250,7 @@
         ],
         axis=0,
     )
-    z, d_rounded, sums = gate_forward(normed, cot_all, y, w_gate, w_o, row)
+    z, sums = gate_forward(normed, y, d_rounded, w_gate, row)
     rounded_out, d_y, d_z, grad_gate_rows = gate_backward(y, z, d_rounded, seq_total(sums), row)
     grad_gate_local = grad_gate_rows[0]
 

time: 610 us -> 582 us (0.954)
  waiting for transfers between devices: 200 us -> 184 us
  local copies, waits for them, and re-layouts: 57.6 us -> 50.4 us
    ppermute x32 -> x33, waiting for transfers between devices: 133 us -> 104 us  [xor_seq(): return lax.ppermute(value, 'seq', [(s, s ^ bits) for s in range(PART)])]
    pallas_call x3 -> x4, Pallas kernels: 77.8 us -> 87 us  [the longest x1 26.2 us: input_gradient(): pl.pallas_call(input_gradient_kernel, grid=(length // WIDE,), in_specs=[p...]
    all_gather x1, waiting for transfers between devices: 0.01 us -> 6.15 us  [gather_everything(): w_conv = lax.all_gather(c, 'dp', axis=0, tiled=True)]
    unnamed x121 -> x125, local copies, waits for them, and re-layouts: 33 us -> 28.3 us
    pallas_call x2 -> x1, Pallas kernels: 12.9 us -> 8.54 us  [all_positions(): pl.pallas_call(functools.partial(positions_kernel, shares, gain_rows is n...]
    ppermute x32 -> x33, starting transfers between devices: 20.4 us -> 20.6 us  [xor_seq(): return lax.ppermute(value, 'seq', [(s, s ^ bits) for s in range(PART)])]
  transfers between devices with their start and end apart: 47 -> 48, of which waited for: 23 -> 22; matrix products, arithmetic and copies ran while one was open for 18% -> 17% of each run, Pallas kernels for 23% -> 26%
where the time goes in v4:
time: 582 us; the launch traced here: 577 us
  Pallas kernels  210 us (36%)
  waiting for transfers between devices  184 us (32%)
  local copies, waits for them, and re-layouts  50.4 us (9%)
  matrix products  42.1 us (7%)
  other arithmetic  38.3 us (7%)
  starting transfers between devices  35.8 us (6%)
  between operations  15.6 us (3%)
    ppermute x33, waiting for transfers between devices, xor_seq(): return lax.ppermute(value, 'seq', [(s, s ^ bits) for s in range(PART)])  104 us
    pallas_call x1, Pallas kernels, recurrence_backward(): pl.pallas_call(backward_kernel, grid_spec=pltpu.PrefetchScalarGridSpec(nu...  61.8 us
    ppermute x6, waiting for transfers between devices, dp_shift_z(): return lax.ppermute(value, 'dp', pairs)  55.1 us
    pallas_call x1, Pallas kernels, recurrence_forward(): pl.pallas_call(forward_kernel, grid_spec=pltpu.PrefetchScalarGridSpec(num...  31 us
    unnamed x125, local copies, waits for them, and re-layouts  28.3 us
    pallas_call x1, Pallas kernels, input_gradient(): pl.pallas_call(input_gradient_kernel, grid=(length // WIDE,), in_specs=[p...  26.2 us
    dot_general x3, matrix products, dot_nn(): lax.dot_general(a, b, (((1,), (0,)), ((), ())), preferred_element_type=f32)  25.7 us
    pallas_call x1, Pallas kernels, products(): pl.pallas_call(products_kernel, grid=(STRIPS // each,), in_specs=[pl.Bloc...  25 us
  transfers between devices with their start and end apart: 48, of which 22 were waited for; matrix products, arithmetic and copies ran while one was open for 17% of the time, Pallas kernels for 26%

profile of v4, /device:TPU:8, one launch (start us, length us, event | category | flops | bytes accessed | tf_op | source)
XLA Modules:
  0.0 576.7 jit_solution(15446304781469777272)
XLA Ops:
  14.9 6.9 %collective-permute-done.refs_0_ = bf16[2,64,1152]{2,1,0:T(8,128)(2,1)S(1)} collective-permute-done((bf16[2,64,1152]{2,1,0:T(8,128)(2,1)S(1)}, bf16[2,64,1152]{2,1,0:T(8,128)(2,1)S(1)}, u32[]{:S(2)}, u32[]{:S(2)}) %collective-permute-start) | collective-permute-done | bytes 294944 | tf_op jit(solution)/shard_map/ppermute | solution.py:41
  33.7 49.5 %collective-permute-done.4.refs_2_ = bf16[128,2048]{1,0:T(8,128)(2,1)} collective-permute-done((bf16[128,2048]{1,0:T(8,128)(2,1)S(1)}, bf16[128,2048]{1,0:T(8,128)(2,1)}, u32[]{:S(2)}, u32[]{:S(2)}) %collective-permute-start.4) | collective-permute-done | bytes 524320 | tf_op jit(solution)/shard_map/ppermute | solution.py:97
  87.2 7.2 %collective-permute-done.7.refs_0_ = bf16[2,64,1024]{2,1,0:T(8,128)(2,1)S(1)} collective-permute-done((bf16[2,64,1024]{2,1,0:T(8,128)(2,1)S(1)}, bf16[2,64,1024]{2,1,0:T(8,128)(2,1)S(1)}, u32[]{:S(2)}, u32[]{:S(2)}) %collective-permute-start.7) | collective-permute-done | bytes 262176 | tf_op jit(solution)/shard_map/ppermute | solution.py:41
  101.0 25.0 %collective-permute-done.10.refs_2_ = bf16[256,2048]{1,0:T(8,128)(2,1)S(1)} collective-permute-done((bf16[256,2048]{1,0:T(8,128)(2,1)}, bf16[256,2048]{1,0:T(8,128)(2,1)S(1)}, u32[]{:S(2)}, u32[]{:S(2)}) %collective-permute-start.10) | collective-permute-done | bytes 1048608 | tf_op jit(solution)/shard_map/ppermute | solution.py:41
  126.1 6.2 %all-gather.3.cloned.1.call-done.refs_3_.wc_ref = bf16[2048,1152]{1,0:T(8,128)(2,1)} async-done(((bf16[256,1152]{1,0:T(8,128)(2,1)}), bf16[2048,1152]{1,0:T(8,128)(2,1)}) %all-gather.3.cloned.1.call-update) | async-done | bytes 4718608 | tf_op jit(solution)/shard_map/all_gather | solution.py:235
  138.8 8.5 %all_positions.1.n_ref = bf16[2048,2048]{1,0:T(8,128)(2,1)S(1)} custom-call(s32[4]{0:T(128)S(1)} %pad_add_fusion.order_ref, bf16[512,2048]{1,0:T(8,128)(2,1)S(1)} %bitcast.192, bf16[512,2048]{1,0:T(8,128)(2,1)} %collective-permute-done.9.refs_1_, bf16[512,2048]{1,0:T(8,128)(2,1)} %get-tuple-element.77.refs_2_, ...), custom_call_target="tpu_custom_call" | custom-call | flops 16777216 | bytes 16777216 | tf_op jit(solution)/shard_map/all_positions/pallas_call | solution.py:296
  152.4 10.9 %select_convert_fusion.refs_1_ = bf16[2048,1024]{1,0:T(8,128)(2,1)} fusion(pred[1024]{0:T(1024)(128)(4,1)S(1)} %fusion.37, bf16[2048,2048]{1,0:T(8,128)(2,1)S(1)} %all_positions.1.n_ref, bf16[2048,1152]{1,0:T(8,128)(2,1)S(1)} %bitcast.214), kind=kOutput, calls=%fused_computation | convolution fusion | flops 8594128896 | bytes 16778240 | tf_op jit(solution)/shard_map/dot_general | solution.py:393
  169.0 31.0 %recurrence_forward.1 = (f32[2048,1024]{1,0:T(8,128)}, bf16[2048,1024]{1,0:T(8,128)(2,1)}, bf16[8,128,1024]{2,1,0:T(8,128)(2,1)}) custom-call(s32[1]{0:T(128)} %bitcast.1.me_ref, bf16[2048,1024]{1,0:T(8,128)(2,1)} %get-tuple-element.78.ci_ref.prev_ref, bf16[1024,128]{1,0:T(8,128)(2,1)} %copy-done.25, bf16[1024,128]{1,0:T(8,128)(2,1)} %get-tuple-element.79.b1, ...), custom_call_target="tpu_custom_call" | custom-call | flops 40000000000 | bytes 16777216 | tf_op jit(solution)/shard_map/recurrence_forward/pallas_call | solution.py:629
  200.2 7.1 %collective-permute-done.19.refs_3_ = bf16[128,2048]{1,0:T(8,128)(2,1)} collective-permute-done((bf16[128,2048]{1,0:T(8,128)(2,1)}, bf16[128,2048]{1,0:T(8,128)(2,1)}, u32[]{:S(2)}, u32[]{:S(2)}) %collective-permute-start.19) | collective-permute-done | bytes 524320 | tf_op jit(solution)/shard_map/ppermute | solution.py:101
  218.9 16.4 %pull_out.1 = (bf16[2048,2048]{1,0:T(8,128)(2,1)}, f32[2048,1024]{1,0:T(8,128)}) custom-call(s32[4]{0:T(128)S(1)} %pad_add_fusion.order_ref, bf16[512,2048]{1,0:T(8,128)(2,1)} %bitcast.207, bf16[512,2048]{1,0:T(8,128)(2,1)} %collective-permute-done.15.sibling, bf16[256,2048]{1,0:T(8,128)(2,1)S(1)} %copy-done.16, ...), custom_call_target="tpu_custom_call" | custom-call | flops 8589934592 | bytes 33554432 | tf_op jit(solution)/shard_map/pull_out/pallas_call | solution.py:912
  235.4 19.3 %gate_forward.1 = (f32[2048,1024]{1,0:T(8,128)}, f32[8,2048]{1,0:T(8,128)S(1)}) custom-call(bf16[2048,2048]{1,0:T(8,128)(2,1)} %copy-done.1, f32[2048,1024]{1,0:T(8,128)} %get-tuple-element.83.y_ref, f32[2048,1024]{1,0:T(8,128)} %get-tuple-element.95.d_ref, bf16[2048,1024]{1,0:T(8,128)(2,1)} %all-gather.5.cloned.1.call-done.wg_ref, ...), custom_call_target="tpu_custom_call" | custom-call | flops 8589934592 | bytes 33554432 | tf_op jit(solution)/shard_map/gate_forward/pallas_call | solution.py:948
  260.6 11.7 %gate_backward.1 = (bf16[2048,1024]{1,0:T(8,128)(2,1)S(1)}, bf16[2048,1024]{1,0:T(8,128)(2,1)S(1)}, bf16[2048,1024]{1,0:T(8,128)(2,1)S(1)}, f32[8,1024]{1,0:T(8,128)S(1)}) custom-call(f32[2048,1024]{1,0:T(8,128)S(1)} %bitcast.194, f32[2048,1024]{1,0:T(8,128)} %get-tuple-element.97.z_ref, f32[2048,1024]{1,0:T(8,128)} %get-tuple-element.95.d_ref, ...), custom_call_target="tpu_custom_call" | custom-call | flops 62914560 | bytes 37748736 | tf_op jit(solution)/shard_map/gate_backward/pallas_call | solution.py:1005
  278.2 25.0 %products.1.refs_1_ = bf16[8,512,1024]{2,1,0:T(8,128)(2,1)} custom-call(bf16[2048,2048]{1,0:T(8,128)(2,1)} %copy-done.1, bf16[2048,1024]{1,0:T(8,128)(2,1)} %copy-done.31, bf16[2048,1024]{1,0:T(8,128)(2,1)} %copy-done.7, bf16[2048,2048]{1,0:T(8,128)(2,1)} %get-tuple-element.102.t_ref), custom_call_target="tpu_custom_call" | custom-call | flops 17179869184 | bytes 33554432 | tf_op jit(solution)/shard_map/products/pallas_call | solution.py:1065
  303.4 61.8 %recurrence_backward.1 = (bf16[2048,1152]{1,0:T(8,128)(2,1)}, bf16[4,1024,128]{2,1,0:T(8,128)(2,1)}, f32[2048,128]{1,0:T(8,128)}, f32[8,1024]{1,0:T(8,128)}, f32[8,128]{1,0:T(8,128)}) custom-call(s32[1]{0:T(128)} %bitcast.1.me_ref, bf16[2048,1024]{1,0:T(8,128)(2,1)} %get-tuple-element.78.ci_ref.prev_ref, ...), custom_call_target="tpu_custom_call" | custom-call | flops 70000001024 | bytes 16777216 | tf_op jit(solution)/shard_map/recurrence_backward/pallas_call | solution.py:828
  365.1 12.4 %convolution_convert_fusion.1 = bf16[2048,2048]{1,0:T(8,128)(2,1)S(1)} fusion(bf16[2048,1024]{1,0:T(8,128)(2,1)} %get-tuple-element.106, bf16[1024,2048]{1,0:T(8,128)(2,1)} %copy-done.6), kind=kOutput, calls=%fused_computation.2 | convolution fusion | flops 8594128896 | bytes 16777216 | tf_op jit(solution)/shard_map/dot_general | solution.py:393
  383.5 6.9 %collective-permute-done.26 = bf16[2,1024,128]{2,1,0:T(8,128)(2,1)} collective-permute-done((bf16[2,1024,128]{2,1,0:T(8,128)(2,1)}, bf16[2,1024,128]{2,1,0:T(8,128)(2,1)}, u32[]{:S(2)}, u32[]{:S(2)}) %collective-permute-start.26) | collective-permute-done | bytes 524320 | tf_op jit(solution)/shard_map/ppermute | solution.py:41
  409.2 16.4 %convolution_convert_fusion.refs_1_ = bf16[2048,1152]{1,0:T(8,128)(2,1)} fusion(bf16[2048,2048]{1,0:T(8,128)(2,1)} %copy-done.1, bf16[2048,1152]{1,0:T(8,128)(2,1)} %get-tuple-element.112.refs_0_), kind=kOutput, calls=%fused_computation.1 | convolution fusion | flops 9666035712 | bytes 17825792 | tf_op jit(solution)/shard_map/dot_general | solution.py:401
  425.7 26.2 %input_gradient.1.refs_1_ = bf16[2048,2048]{1,0:T(8,128)(2,1)} custom-call(bf16[2048,1024]{1,0:T(8,128)(2,1)} %copy-done.31, bf16[2048,1152]{1,0:T(8,128)(2,1)} %get-tuple-element.113.p_ref, bf16[2048,1024]{1,0:T(8,128)(2,1)} %all-gather.5.cloned.1.call-done.wg_ref, bf16[2048,1152]{1,0:T(8,128)(2,1)} %all-gather.3.cloned.1.call-done.refs_3_.wc_ref), custom_call_target="tpu_custom_call" | custom-call | flops 10000000000 | bytes 4194304 | tf_op jit(solution)/shard_map/input_gradient/pallas_call | solution.py:1029
  451.9 4.8 dynamic-slice_bitcast_fusion
  459.3 4.9 collective-permute-done.29
  482.9 33.9 %collective-permute-done.34.refs_1_ = bf16[512,2048]{1,0:T(8,128)(2,1)} collective-permute-done((bf16[512,2048]{1,0:T(8,128)(2,1)}, bf16[512,2048]{1,0:T(8,128)(2,1)}, u32[]{:S(2)}, u32[]{:S(2)}) %collective-permute-start.34) | collective-permute-done | bytes 2097184 | tf_op jit(solution)/shard_map/ppermute | solution.py:41
  517.7 4.6 fusion.2
  522.9 8.7 %fusion.16 = (bf16[1,512,2048]{2,1,0:T(8,128)(2,1)}, bf16[1,512,2048]{2,1,0:T(8,128)(2,1)}) fusion(bf16[512,2048]{1,0:T(8,128)(2,1)} %get-tuple-element.122.refs_1_, f32[512]{0:T(512)S(1)} %broadcast_multiply_fusion, f32[512]{0:T(512)S(1)} %get-tuple-element.163, f32[2048]{0:T(1024)S(1)} %copy-done.45, f32[512]{0:T(512)S(1)} %get-tuple-element.162, ...), kind=kLoop, calls=%fused_computation.27 | loop fusion | flops 22020096 | bytes 20985868 | tf_op jit(solution)/shard_map/broadcast_in_dim | solution.py:1340
  545.5 9.9 %reduce-scatter.5.cloned.1.call-done.refs_0_ = bf16[256,1152]{1,0:T(8,128)(2,1)} async-done(((bf16[2048,1152]{1,0:T(8,128)(2,1)}), bf16[256,1152]{1,0:T(8,128)(2,1)}) %reduce-scatter.5.cloned.1.call-update) | async-done | bytes 589840 | tf_op jit(solution)/shard_map/reduce_scatter | solution.py:354
  (336 shorter events, 145.5 us)
Async XLA Ops:
  7.2 125.1 %all-gather.3.cloned.1.call-start = ((), (), s32[]{:S(2)}) async-start(), calls=%async_computation.2 | async-start | bytes 5308416 | tf_op jit(solution)/shard_map/all_gather | solution.py:235
  7.2 14.7 %collective-permute-start.1 = (bf16[128,2048]{1,0:T(8,128)(2,1)}, bf16[128,2048]{1,0:T(8,128)(2,1)}, u32[]{:S(2)}, u32[]{:S(2)}) collective-permute-start(bf16[128,2048]{1,0:T(8,128)(2,1)} %refs_0_.1), channel_id=1, source_target_pairs={{0,8},{4,12},{8,16},{12,20},{16,24},{20,28},{24,0},{28,4},{1,9},{5... | collective-permute-start | bytes 1572872 | tf_op jit(solution)/shard_map/ppermute | solution.py:97
  26.3 209.1 %all-gather.5.cloned.1.call-start = ((), (), s32[]{:S(2)}) async-start(), calls=%async_computation.3 | async-start | bytes 4718592 | tf_op jit(solution)/shard_map/all_gather | solution.py:248
  27.7 57.2 %collective-permute-start.3 = (bf16[512,2048]{1,0:T(8,128)(2,1)}, bf16[512,2048]{1,0:T(8,128)(2,1)}, u32[]{:S(2)}, u32[]{:S(2)}) collective-permute-start(bf16[512,2048]{1,0:T(8,128)(2,1)} %after.7), channel_id=1, source_target_pairs={{0,2},{1,3},{2,0},{3,1},{4,6},{5,7},{6,4},{7,5},{8,10},{9,11},{10,... | collective-permute-start | bytes 6291464 | tf_op jit(solution)/shard_map/ppermute | solution.py:41
  29.2 54.1 %collective-permute-start.4 = (bf16[128,2048]{1,0:T(8,128)(2,1)S(1)}, bf16[128,2048]{1,0:T(8,128)(2,1)}, u32[]{:S(2)}, u32[]{:S(2)}) collective-permute-start(bf16[128,2048]{1,0:T(8,128)(2,1)S(1)} %copy-done.17), channel_id=1, source_target_pairs={{0,16},{4,20},{8,24},{12,28},{16,0},{20,4},{24,8},{28,12},{1,17},{... | collective-permute-start | bytes 1572872 | tf_op jit(solution)/shard_map/ppermute | solution.py:97
  30.6 54.2 %collective-permute-start.5 = (bf16[128,2048]{1,0:T(8,128)(2,1)S(1)}, bf16[128,2048]{1,0:T(8,128)(2,1)}, u32[]{:S(2)}, u32[]{:S(2)}) collective-permute-start(bf16[128,2048]{1,0:T(8,128)(2,1)S(1)} %copy-done.17), channel_id=1, source_target_pairs={{0,24},{4,28},{8,0},{12,4},{16,8},{20,12},{24,16},{28,20},{1,25},{... | collective-permute-start | bytes 1572872 | tf_op jit(solution)/shard_map/ppermute | solution.py:97
  32.2 52.6 %collective-permute-start.6 = (bf16[128,2048]{1,0:T(8,128)(2,1)S(1)}, bf16[128,2048]{1,0:T(8,128)(2,1)S(1)}, u32[]{:S(2)}, u32[]{:S(2)}) collective-permute-start(bf16[128,2048]{1,0:T(8,128)(2,1)S(1)} %copy-done.17), channel_id=1, source_target_pairs={{0,4},{4,0},{8,12},{12,8},{16,20},{20,16},{24,28},{28,24},{1,5},{5... | collective-permute-start | bytes 1572872 | tf_op jit(solution)/shard_map/ppermute | solution.py:101
  100.3 25.8 %collective-permute-start.10 = (bf16[256,2048]{1,0:T(8,128)(2,1)}, bf16[256,2048]{1,0:T(8,128)(2,1)S(1)}, u32[]{:S(2)}, u32[]{:S(2)}) collective-permute-start(bf16[256,2048]{1,0:T(8,128)(2,1)} %get-tuple-element.76), channel_id=1, source_target_pairs={{0,2},{1,3},{2,0},{3,1},{4,6},{5,7},{6,4},{7,5},{8,10},{9,11},{10,... | collective-permute-start | bytes 3145736 | tf_op jit(solution)/shard_map/ppermute | solution.py:41
  100.8 38.0 %collective-permute-start.9 = (bf16[512,2048]{1,0:T(8,128)(2,1)S(1)}, bf16[512,2048]{1,0:T(8,128)(2,1)}, u32[]{:S(2)}, u32[]{:S(2)}) collective-permute-start(bf16[512,2048]{1,0:T(8,128)(2,1)S(1)} %bitcast.191), channel_id=1, source_target_pairs={{0,1},{1,0},{2,3},{3,2},{4,5},{5,4},{6,7},{7,6},{8,9},{9,8},{10,11... | collective-permute-start | bytes 6291464 | tf_op jit(solution)/shard_map/ppermute | solution.py:41
  132.4 86.6 %collective-permute-start.15 = (bf16[512,2048]{1,0:T(8,128)(2,1)}, bf16[512,2048]{1,0:T(8,128)(2,1)}, u32[]{:S(2)}, u32[]{:S(2)}) collective-permute-start(bf16[512,2048]{1,0:T(8,128)(2,1)} %bitcast.206), channel_id=1, source_target_pairs={{0,1},{1,0},{2,3},{3,2},{4,5},{5,4},{6,7},{7,6},{8,9},{9,8},{10,11... | collective-permute-start | bytes 6291464 | tf_op jit(solution)/shard_map/ppermute | solution.py:41
  136.0 64.0 %collective-permute-start.17 = (bf16[128,2048]{1,0:T(8,128)(2,1)}, bf16[128,2048]{1,0:T(8,128)(2,1)S(1)}, u32[]{:S(2)}, u32[]{:S(2)}) collective-permute-start(bf16[128,2048]{1,0:T(8,128)(2,1)} %get-tuple-element.86.refs_1_), channel_id=1, source_target_pairs={{0,4},{4,0},{8,12},{12,8},{16,20},{20,16},{24,28},{28,24},{1,5},{5... | collective-permute-start | bytes 1572872 | tf_op jit(solution)/shard_map/ppermute | solution.py:101
  136.6 320.1 %reduce-scatter.3.cloned.1.call-start = ((), (), s32[]{:S(2)}) async-start(), calls=%async_computation.4 | async-start | bytes 9437184 | tf_op jit(solution)/shard_map/reduce_scatter | solution.py:354
  150.5 12.9 %collective-permute-start.12 = (bf16[1024,128]{1,0:T(8,128)(2,1)S(1)}, bf16[1024,128]{1,0:T(8,128)(2,1)S(1)}, u32[]{:S(2)}, u32[]{:S(2)}) collective-permute-start(bf16[1024,128]{1,0:T(8,128)(2,1)S(1)} %bc_forward.1.b0), channel_id=1, source_target_pairs={{0,1},{1,0},{2,3},{3,2},{4,5},{5,4},{6,7},{7,6},{8,9},{9,8},{10,11... | collective-permute-start | bytes 786440 | tf_op jit(solution)/shard_map/ppermute | solution.py:41
  150.6 15.0 %collective-permute-start.13 = (bf16[1024,128]{1,0:T(8,128)(2,1)S(1)}, bf16[1024,128]{1,0:T(8,128)(2,1)S(1)}, u32[]{:S(2)}, u32[]{:S(2)}) collective-permute-start(bf16[1024,128]{1,0:T(8,128)(2,1)S(1)} %bc_forward.1.b0), channel_id=1, source_target_pairs={{0,2},{1,3},{2,0},{3,1},{4,6},{5,7},{6,4},{7,5},{8,10},{9,11},{10,... | collective-permute-start | bytes 786440 | tf_op jit(solution)/shard_map/ppermute | solution.py:41
  152.1 14.0 %collective-permute-start.14 = (bf16[1024,128]{1,0:T(8,128)(2,1)S(1)}, bf16[1024,128]{1,0:T(8,128)(2,1)S(1)}, u32[]{:S(2)}, u32[]{:S(2)}) collective-permute-start(bf16[1024,128]{1,0:T(8,128)(2,1)S(1)} %bc_forward.1.b0), channel_id=1, source_target_pairs={{0,3},{1,2},{2,1},{3,0},{4,7},{5,6},{6,5},{7,4},{8,11},{9,10},{10,... | collective-permute-start | bytes 786440 | tf_op jit(solution)/shard_map/ppermute | solution.py:41
  164.1 36.1 %collective-permute-start.18 = (bf16[128,2048]{1,0:T(8,128)(2,1)}, bf16[128,2048]{1,0:T(8,128)(2,1)S(1)}, u32[]{:S(2)}, u32[]{:S(2)}) collective-permute-start(bf16[128,2048]{1,0:T(8,128)(2,1)} %get-tuple-element.87.refs_2_), channel_id=1, source_target_pairs={{0,4},{4,0},{8,12},{12,8},{16,20},{20,16},{24,28},{28,24},{1,5},{5... | collective-permute-start | bytes 1572872 | tf_op jit(solution)/shard_map/ppermute | solution.py:101
  165.5 41.7 %collective-permute-start.19 = (bf16[128,2048]{1,0:T(8,128)(2,1)}, bf16[128,2048]{1,0:T(8,128)(2,1)}, u32[]{:S(2)}, u32[]{:S(2)}) collective-permute-start(bf16[128,2048]{1,0:T(8,128)(2,1)} %get-tuple-element.88.refs_3_), channel_id=1, source_target_pairs={{0,4},{4,0},{8,12},{12,8},{16,20},{20,16},{24,28},{28,24},{1,5},{5... | collective-permute-start | bytes 1572872 | tf_op jit(solution)/shard_map/ppermute | solution.py:101
  166.9 40.4 %collective-permute-start.16 = (bf16[256,2048]{1,0:T(8,128)(2,1)}, bf16[256,2048]{1,0:T(8,128)(2,1)}, u32[]{:S(2)}, u32[]{:S(2)}) collective-permute-start(bf16[256,2048]{1,0:T(8,128)(2,1)} %get-tuple-element.85), channel_id=1, source_target_pairs={{0,2},{1,3},{2,0},{3,1},{4,6},{5,7},{6,4},{7,5},{8,10},{9,11},{10,... | collective-permute-start | bytes 3145736 | tf_op jit(solution)/shard_map/ppermute | solution.py:41
  200.1 18.9 %collective-permute-start.20 = (bf16[256,2048]{1,0:T(8,128)(2,1)}, bf16[256,2048]{1,0:T(8,128)(2,1)}, u32[]{:S(2)}, u32[]{:S(2)}) collective-permute-start(bf16[256,2048]{1,0:T(8,128)(2,1)} %get-tuple-element.84.across_a), channel_id=1, source_target_pairs={{0,1},{1,0},{2,3},{3,2},{4,5},{5,4},{6,7},{7,6},{8,9},{9,8},{10,11... | collective-permute-start | bytes 3145736 | tf_op jit(solution)/shard_map/ppermute | solution.py:41
  303.3 252.1 %reduce-scatter.5.cloned.1.call-start = ((), (), s32[]{:S(2)}) async-start(), calls=%async_computation.5 | async-start | bytes 5308416 | tf_op jit(solution)/shard_map/reduce_scatter | solution.py:354
  382.2 12.0 %collective-permute-start.25 = (bf16[2,512,2048]{2,1,0:T(8,128)(2,1)}, bf16[2,512,2048]{2,1,0:T(8,128)(2,1)}, u32[]{:S(2)}, u32[]{:S(2)}) collective-permute-start(bf16[2,512,2048]{2,1,0:T(8,128)(2,1)} %dynamic-slice_bitcast_fusion.1), channel_id=1, source_target_pairs={{0,1},{1,0},{2,3},{3,2},{4,5},{5,4},{6,7},{7,6},{8,9},{9,8},{10,11... | collective-permute-start | bytes 12582920 | tf_op jit(solution)/shard_map/ppermute | solution.py:41
  401.8 50.1 %collective-permute-start.28 = (bf16[512,2048]{1,0:T(8,128)(2,1)}, bf16[512,2048]{1,0:T(8,128)(2,1)}, u32[]{:S(2)}, u32[]{:S(2)}) collective-permute-start(bf16[512,2048]{1,0:T(8,128)(2,1)} %get-tuple-element.108), channel_id=1, source_target_pairs={{0,2},{1,3},{2,0},{3,1},{4,6},{5,7},{6,4},{7,5},{8,10},{9,11},{10,... | collective-permute-start | bytes 6291464 | tf_op jit(solution)/shard_map/ppermute | solution.py:41
  468.8 48.0 %collective-permute-start.34 = (bf16[512,2048]{1,0:T(8,128)(2,1)}, bf16[512,2048]{1,0:T(8,128)(2,1)}, u32[]{:S(2)}, u32[]{:S(2)}) collective-permute-start(bf16[512,2048]{1,0:T(8,128)(2,1)} %get-tuple-element.121), channel_id=1, source_target_pairs={{0,2},{1,3},{2,0},{3,1},{4,6},{5,7},{6,4},{7,5},{8,10},{9,11},{10,... | collective-permute-start | bytes 6291464 | tf_op jit(solution)/shard_map/ppermute | solution.py:41
  517.7 13.9 %collective-permute-start.43 = (f32[48,128]{1,0:T(8,128)}, f32[48,128]{1,0:T(8,128)S(1)}, u32[]{:S(2)}, u32[]{:S(2)}) collective-permute-start(f32[48,128]{1,0:T(8,128)} %get-tuple-element.125), channel_id=1, source_target_pairs={{0,1},{1,0},{2,3},{3,2},{4,5},{5,4},{6,7},{7,6},{8,9},{9,8},{10,11... | collective-permute-start | bytes 73736 | tf_op jit(solution)/shard_map/ppermute | solution.py:41
  (82 other events, 592.5 us)
Sparse Core Ops, SparseCore 0:
  26.4 105.7 all-gather.2
  136.7 89.9 all-gather.4
  303.4 148.6 reduce-scatter.2
  456.9 98.5 reduce-scatter.4

commit v5 on v4

--- a/solution.py
+++ b/solution.py
@@ -148,7 +148,7 @@
             out_specs=pl.BlockSpec((rows * count, tile), along),
         ),
         out_shape=jax.ShapeDtypeStruct((rows * count, columns), pieces[0].dtype),
-        compiler_params=pltpu.CompilerParams(vmem_limit_bytes=24 * 2**20),
+        compiler_params=pltpu.CompilerParams(vmem_limit_bytes=60 * 2**20),
         cost_estimate=pl.CostEstimate(
             flops=0, bytes_accessed=4 * rows * count * columns, transcendentals=0
         ),
@@ -1018,31 +1018,46 @@
     )(y, z, d, sums, row)
 
 
-def input_gradient_kernel(z_ref, p_ref, wg_ref, wc_ref, out_ref):
-    out_ref[...] = (dot_nt(z_ref[...], wg_ref[...]) + dot_nt(p_ref[...], wc_ref[...])).astype(bf16)
-
-
-def input_gradient(d_z, d_project, w_gate, w_conv):
-    length = d_z.shape[0]
-    whole = lambda i: (0, 0)
-    along = lambda i: (i, 0)
+def input_gradient_kernel(core_ref, z_ref, p_ref, wg_ref, wc_ref, other_ref, mine_ref):
+    del core_ref
+    out = (dot_nt(z_ref[...], wg_ref[...]) + dot_nt(p_ref[...], wc_ref[...])).astype(bf16)
+
+    @pl.when(pl.program_id(0) < 2)
+    def _():
+        other_ref[...] = out
+
+    @pl.when(pl.program_id(0) >= 2)
+    def _():
+        mine_ref[...] = out
+
+
+def input_gradient(core, d_z, d_project, w_gate, w_conv):
+    tokens = d_z.shape[0] // PART
+    whole = lambda i, core: (0, 0)
+    along = lambda i, core: (i % 2 * 2 + jnp.where(i < 2, 1 - core[0], core[0]), 0)
     return pl.pallas_call(
         input_gradient_kernel,
-        grid=(length // WIDE,),
-        in_specs=[
-            pl.BlockSpec((WIDE, OWN), along),
-            pl.BlockSpec((WIDE, CONV_COLS), along),
-            pl.BlockSpec((D, OWN), whole),
-            pl.BlockSpec((D, CONV_COLS), whole),
-        ],
-        out_specs=pl.BlockSpec((WIDE, D), along),
-        out_shape=jax.ShapeDtypeStruct((length, D), bf16),
+        grid_spec=pltpu.PrefetchScalarGridSpec(
+            num_scalar_prefetch=1,
+            grid=(PART,),
+            in_specs=[
+                pl.BlockSpec((tokens, OWN), along),
+                pl.BlockSpec((tokens, CONV_COLS), along),
+                pl.BlockSpec((D, OWN), whole),
+                pl.BlockSpec((D, CONV_COLS), whole),
+            ],
+            out_specs=[
+                pl.BlockSpec((tokens, D), lambda i, core: (jnp.minimum(i, 1), 0)),
+                pl.BlockSpec((tokens, D), lambda i, core: (jnp.maximum(i - 2, 0), 0)),
+            ],
+        ),
+        out_shape=[jax.ShapeDtypeStruct((2 * tokens, D), bf16)] * 2,
         compiler_params=pltpu.CompilerParams(vmem_limit_bytes=60 * 2**20),
         cost_estimate=pl.CostEstimate(
             flops=10**10, bytes_accessed=2**22, transcendentals=0
         ),
         name="input_gradient",
-    )(d_z, d_project, w_gate, w_conv)
+    )(core, d_z, d_project, w_gate, w_conv)
 
 
 def products_kernel(n_ref, z_ref, r_ref, t_ref, out_ref):
@@ -1145,7 +1160,7 @@
             jax.ShapeDtypeStruct((rows, HEADS), f32),
             jax.ShapeDtypeStruct((1, rows), f32),
         ],
-        compiler_params=pltpu.CompilerParams(vmem_limit_bytes=32 * 2**20),
+        compiler_params=pltpu.CompilerParams(vmem_limit_bytes=60 * 2**20),
         name="projection_rows",
     )(me, *gates, *convs, w_in, w_dt, norm_gain[None, :])
 
@@ -1292,10 +1307,11 @@
         (conv_product,) = after([conv_product], [both_total])
         conv_total = dp_sum(conv_product)
     branch_across = xor_seq(branch_give, 2)
-    d_normed = input_gradient(d_z, d_project, w_gate, w_conv)
+    other, mine = input_gradient(place_me % 2, d_z, d_project, w_gate, w_conv)
     if fast_mesh():
-        branch_across, d_normed = tie(branch_across, d_normed)
-    mine, got = core_halves(d_normed.reshape(PART, tokens, D))
+        branch_across, other, mine = tie(branch_across, other, mine)
+    mine = mine.reshape(2, tokens, D)
+    got = xor_seq(other, 1).reshape(2, tokens, D)
     keep, give = halves_sum(mine, got)
     small, give = tie(small, give)
     across = xor_seq(give, 2)

time: 582 us -> 581 us (level)
  local copies, waits for them, and re-layouts: 50.4 us -> 40.3 us
  Pallas kernels: 210 us -> 216 us
    unnamed x125 -> x109, local copies, waits for them, and re-layouts: 28.3 us -> 20.5 us
  transfers between devices with their start and end apart: 48 -> 48, of which waited for: 22 -> 22; matrix products, arithmetic and copies ran while one was open for 17% -> 17% of each run, Pallas kernels for 26% -> 27%
where the time goes in v5:
time: 581 us; the launch traced here: 576 us
  Pallas kernels  216 us (37%)
  waiting for transfers between devices  187 us (32%)
  matrix products  42.1 us (7%)
  local copies, waits for them, and re-layouts  40.3 us (7%)
  other arithmetic  40.1 us (7%)
  starting transfers between devices  35.6 us (6%)
  between operations  15.5 us (3%)
    ppermute x33, waiting for transfers between devices, xor_seq(): return lax.ppermute(value, 'seq', [(s, s ^ bits) for s in range(PART)])  103 us
    pallas_call x1, Pallas kernels, recurrence_backward(): pl.pallas_call(backward_kernel, grid_spec=pltpu.PrefetchScalarGridSpec(nu...  61.8 us
    ppermute x6, waiting for transfers between devices, dp_shift_z(): return lax.ppermute(value, 'dp', pairs)  54.5 us
    pallas_call x1, Pallas kernels, recurrence_forward(): pl.pallas_call(forward_kernel, grid_spec=pltpu.PrefetchScalarGridSpec(num...  31.1 us
    pallas_call x1, Pallas kernels, input_gradient(): pl.pallas_call(input_gradient_kernel, grid_spec=pltpu.PrefetchScalarGridS...  27.8 us
    dot_general x3, matrix products, dot_nn(): lax.dot_general(a, b, (((1,), (0,)), ((), ())), preferred_element_type=f32)  25.7 us
    pallas_call x1, Pallas kernels, products(): pl.pallas_call(products_kernel, grid=(STRIPS // each,), in_specs=[pl.Bloc...  25.2 us
    unnamed x109, local copies, waits for them, and re-layouts  20.5 us
  transfers between devices with their start and end apart: 48, of which 22 were waited for; matrix products, arithmetic and copies ran while one was open for 17% of the time, Pallas kernels for 27%

profile of v5, /device:TPU:8, one launch (start us, length us, event | category | flops | bytes accessed | tf_op | source)
XLA Modules:
  0.0 576.1 jit_solution(2387439447656114845)
XLA Ops:
  15.6 7.2 %collective-permute-done.refs_0_ = bf16[2,64,1152]{2,1,0:T(8,128)(2,1)S(1)} collective-permute-done((bf16[2,64,1152]{2,1,0:T(8,128)(2,1)}, bf16[2,64,1152]{2,1,0:T(8,128)(2,1)S(1)}, u32[]{:S(2)}, u32[]{:S(2)}) %collective-permute-start) | collective-permute-done | bytes 294944 | tf_op jit(solution)/shard_map/ppermute | solution.py:41
  35.4 49.5 %collective-permute-done.4.refs_2_ = bf16[128,2048]{1,0:T(8,128)(2,1)} collective-permute-done((bf16[128,2048]{1,0:T(8,128)(2,1)S(1)}, bf16[128,2048]{1,0:T(8,128)(2,1)}, u32[]{:S(2)}, u32[]{:S(2)}) %collective-permute-start.4) | collective-permute-done | bytes 524320 | tf_op jit(solution)/shard_map/ppermute | solution.py:97
  88.3 6.7 %collective-permute-done.7.refs_0_ = bf16[2,64,1024]{2,1,0:T(8,128)(2,1)S(1)} collective-permute-done((bf16[2,64,1024]{2,1,0:T(8,128)(2,1)S(1)}, bf16[2,64,1024]{2,1,0:T(8,128)(2,1)S(1)}, u32[]{:S(2)}, u32[]{:S(2)}) %collective-permute-start.7) | collective-permute-done | bytes 262176 | tf_op jit(solution)/shard_map/ppermute | solution.py:41
  101.6 25.0 %collective-permute-done.10.refs_2_ = bf16[256,2048]{1,0:T(8,128)(2,1)S(1)} collective-permute-done((bf16[256,2048]{1,0:T(8,128)(2,1)}, bf16[256,2048]{1,0:T(8,128)(2,1)S(1)}, u32[]{:S(2)}, u32[]{:S(2)}) %collective-permute-start.10) | collective-permute-done | bytes 1048608 | tf_op jit(solution)/shard_map/ppermute | solution.py:41
  126.7 7.2 %all-gather.3.cloned.1.call-done.refs_3_.wc_ref = bf16[2048,1152]{1,0:T(8,128)(2,1)} async-done(((bf16[256,1152]{1,0:T(8,128)(2,1)}), bf16[2048,1152]{1,0:T(8,128)(2,1)}) %all-gather.3.cloned.1.call-update) | async-done | bytes 4718608 | tf_op jit(solution)/shard_map/all_gather | solution.py:235
  141.1 8.4 %all_positions.1.n_ref = bf16[2048,2048]{1,0:T(8,128)(2,1)S(1)} custom-call(s32[4]{0:T(128)S(1)} %pad_add_fusion.order_ref, bf16[512,2048]{1,0:T(8,128)(2,1)S(1)} %bitcast.189, bf16[512,2048]{1,0:T(8,128)(2,1)} %collective-permute-done.9.refs_1_, bf16[512,2048]{1,0:T(8,128)(2,1)} %get-tuple-element.80.refs_2_, ...), custom_call_target="tpu_custom_call" | custom-call | flops 16777216 | bytes 16777216 | tf_op jit(solution)/shard_map/all_positions/pallas_call | solution.py:296
  154.6 10.9 %select_convert_fusion.refs_1_ = bf16[2048,1024]{1,0:T(8,128)(2,1)} fusion(pred[1024]{0:T(1024)(128)(4,1)S(1)} %fusion.36, bf16[2048,2048]{1,0:T(8,128)(2,1)S(1)} %all_positions.1.n_ref, bf16[2048,1152]{1,0:T(8,128)(2,1)S(1)} %bitcast.210), kind=kOutput, calls=%fused_computation | convolution fusion | flops 8594128896 | bytes 16778240 | tf_op jit(solution)/shard_map/dot_general | solution.py:393
  170.4 31.1 %recurrence_forward.1 = (f32[2048,1024]{1,0:T(8,128)}, bf16[2048,1024]{1,0:T(8,128)(2,1)}, bf16[8,128,1024]{2,1,0:T(8,128)(2,1)}) custom-call(s32[1]{0:T(128)} %bitcast.1.me_ref, bf16[2048,1024]{1,0:T(8,128)(2,1)} %get-tuple-element.81.ci_ref.prev_ref, bf16[1024,128]{1,0:T(8,128)(2,1)} %copy-done.9, bf16[1024,128]{1,0:T(8,128)(2,1)} %get-tuple-element.82.b1, ...), custom_call_target="tpu_custom_call" | custom-call | flops 40000000000 | bytes 16777216 | tf_op jit(solution)/shard_map/recurrence_forward/pallas_call | solution.py:629
  201.7 7.0 %collective-permute-done.19.refs_3_ = bf16[128,2048]{1,0:T(8,128)(2,1)} collective-permute-done((bf16[128,2048]{1,0:T(8,128)(2,1)}, bf16[128,2048]{1,0:T(8,128)(2,1)}, u32[]{:S(2)}, u32[]{:S(2)}) %collective-permute-start.19) | collective-permute-done | bytes 524320 | tf_op jit(solution)/shard_map/ppermute | solution.py:101
  212.9 5.5 assemble.1.wo_ref
  218.5 16.4 %pull_out.1 = (bf16[2048,2048]{1,0:T(8,128)(2,1)}, f32[2048,1024]{1,0:T(8,128)}) custom-call(s32[4]{0:T(128)S(1)} %pad_add_fusion.order_ref, bf16[512,2048]{1,0:T(8,128)(2,1)} %bitcast.203, bf16[512,2048]{1,0:T(8,128)(2,1)} %collective-permute-done.15.sibling, bf16[256,2048]{1,0:T(8,128)(2,1)S(1)} %copy-done.8, ...), custom_call_target="tpu_custom_call" | custom-call | flops 8589934592 | bytes 33554432 | tf_op jit(solution)/shard_map/pull_out/pallas_call | solution.py:912
  234.9 19.3 %gate_forward.1 = (f32[2048,1024]{1,0:T(8,128)}, f32[8,2048]{1,0:T(8,128)S(1)}) custom-call(bf16[2048,2048]{1,0:T(8,128)(2,1)} %copy-done.1, f32[2048,1024]{1,0:T(8,128)} %get-tuple-element.86.y_ref, f32[2048,1024]{1,0:T(8,128)} %get-tuple-element.98.d_ref, bf16[2048,1024]{1,0:T(8,128)(2,1)} %all-gather.5.cloned.1.call-done.wg_ref, ...), custom_call_target="tpu_custom_call" | custom-call | flops 8589934592 | bytes 33554432 | tf_op jit(solution)/shard_map/gate_forward/pallas_call | solution.py:948
  260.1 11.8 %gate_backward.1 = (bf16[2048,1024]{1,0:T(8,128)(2,1)S(1)}, bf16[2048,1024]{1,0:T(8,128)(2,1)S(1)}, bf16[2048,1024]{1,0:T(8,128)(2,1)S(1)}, f32[8,1024]{1,0:T(8,128)S(1)}) custom-call(f32[2048,1024]{1,0:T(8,128)S(1)} %bitcast.191, f32[2048,1024]{1,0:T(8,128)} %get-tuple-element.100.z_ref, f32[2048,1024]{1,0:T(8,128)} %get-tuple-element.98.d_ref, ...), custom_call_target="tpu_custom_call" | custom-call | flops 62914560 | bytes 37748736 | tf_op jit(solution)/shard_map/gate_backward/pallas_call | solution.py:1005
  277.8 25.2 %products.1.refs_1_ = bf16[8,512,1024]{2,1,0:T(8,128)(2,1)} custom-call(bf16[2048,2048]{1,0:T(8,128)(2,1)} %copy-done.1, bf16[2048,1024]{1,0:T(8,128)(2,1)} %copy-done.13, bf16[2048,1024]{1,0:T(8,128)(2,1)} %copy-done.5, bf16[2048,2048]{1,0:T(8,128)(2,1)} %get-tuple-element.105.t_ref), custom_call_target="tpu_custom_call" | custom-call | flops 17179869184 | bytes 33554432 | tf_op jit(solution)/shard_map/products/pallas_call | solution.py:1080
  303.1 61.8 %recurrence_backward.1 = (bf16[2048,1152]{1,0:T(8,128)(2,1)}, bf16[4,1024,128]{2,1,0:T(8,128)(2,1)}, f32[2048,128]{1,0:T(8,128)}, f32[8,1024]{1,0:T(8,128)}, f32[8,128]{1,0:T(8,128)}) custom-call(s32[1]{0:T(128)} %bitcast.1.me_ref, bf16[2048,1024]{1,0:T(8,128)(2,1)} %get-tuple-element.81.ci_ref.prev_ref, ...), custom_call_target="tpu_custom_call" | custom-call | flops 70000001024 | bytes 16777216 | tf_op jit(solution)/shard_map/recurrence_backward/pallas_call | solution.py:828
  364.8 12.4 %convolution_convert_fusion.1 = bf16[2048,2048]{1,0:T(8,128)(2,1)S(1)} fusion(bf16[2048,1024]{1,0:T(8,128)(2,1)} %get-tuple-element.109, bf16[1024,2048]{1,0:T(8,128)(2,1)} %assemble.1.wo_ref), kind=kOutput, calls=%fused_computation.2 | convolution fusion | flops 8594128896 | bytes 16777216 | tf_op jit(solution)/shard_map/dot_general | solution.py:393
  383.2 6.9 %collective-permute-done.26 = bf16[2,1024,128]{2,1,0:T(8,128)(2,1)} collective-permute-done((bf16[2,1024,128]{2,1,0:T(8,128)(2,1)}, bf16[2,1024,128]{2,1,0:T(8,128)(2,1)}, u32[]{:S(2)}, u32[]{:S(2)}) %collective-permute-start.26) | collective-permute-done | bytes 524320 | tf_op jit(solution)/shard_map/ppermute | solution.py:41
  408.8 16.4 %convolution_convert_fusion.refs_1_ = bf16[2048,1152]{1,0:T(8,128)(2,1)} fusion(bf16[2048,2048]{1,0:T(8,128)(2,1)} %copy-done.1, bf16[2048,1152]{1,0:T(8,128)(2,1)} %get-tuple-element.115.refs_0_), kind=kOutput, calls=%fused_computation.1 | convolution fusion | flops 9666035712 | bytes 17825792 | tf_op jit(solution)/shard_map/dot_general | solution.py:401
  425.2 27.8 %input_gradient.1 = (bf16[1024,2048]{1,0:T(8,128)(2,1)}, bf16[1024,2048]{1,0:T(8,128)(2,1)}) custom-call(s32[1]{0:T(128)S(6)} %select_n.316.core_ref, bf16[2048,1024]{1,0:T(8,128)(2,1)} %copy-done.13, bf16[2048,1152]{1,0:T(8,128)(2,1)} %get-tuple-element.116.p_ref, bf16[2048,1024]{1,0:T(8,128)(2,1)} %all-gather.5.cloned.1.call-done.wg_ref, ...), custom_call_target="tpu_custom_call" | custom-call | flops 10000000000 | bytes 4194304 | tf_op jit(solution)/shard_map/input_gradient/pallas_call | solution.py:1038
  455.7 4.9 collective-permute-done.29
  479.9 33.1 %collective-permute-done.34.refs_1_ = bf16[512,2048]{1,0:T(8,128)(2,1)} collective-permute-done((bf16[512,2048]{1,0:T(8,128)(2,1)}, bf16[512,2048]{1,0:T(8,128)(2,1)}, u32[]{:S(2)}, u32[]{:S(2)}) %collective-permute-start.34) | collective-permute-done | bytes 2097184 | tf_op jit(solution)/shard_map/ppermute | solution.py:41
  513.7 4.7 fusion.2
  518.9 8.6 %fusion.15 = (bf16[1,512,2048]{2,1,0:T(8,128)(2,1)}, bf16[1,512,2048]{2,1,0:T(8,128)(2,1)}) fusion(bf16[512,2048]{1,0:T(8,128)(2,1)} %get-tuple-element.128.refs_1_, f32[512]{0:T(512)S(1)} %broadcast_multiply_fusion, f32[512]{0:T(512)S(1)} %get-tuple-element.169, f32[2048]{0:T(1024)S(1)} %copy-done.37, f32[512]{0:T(512)S(1)} %get-tuple-element.168, ...), kind=kLoop, calls=%fused_computation.25 | loop fusion | flops 22020096 | bytes 20985868 | tf_op jit(solution)/shard_map/broadcast_in_dim | solution.py:1356
  542.0 12.6 %reduce-scatter.5.cloned.1.call-done.refs_0_ = bf16[256,1152]{1,0:T(8,128)(2,1)} async-done(((bf16[2048,1152]{1,0:T(8,128)(2,1)}), bf16[256,1152]{1,0:T(8,128)(2,1)}) %reduce-scatter.5.cloned.1.call-update) | async-done | bytes 589840 | tf_op jit(solution)/shard_map/reduce_scatter | solution.py:354
  (319 shorter events, 140.1 us)
Async XLA Ops:
  7.2 126.7 %all-gather.3.cloned.1.call-start = ((), (), s32[]{:S(2)}) async-start(), calls=%async_computation.2 | async-start | bytes 5308416 | tf_op jit(solution)/shard_map/all_gather | solution.py:235
  7.2 15.5 %collective-permute-start.1 = (bf16[128,2048]{1,0:T(8,128)(2,1)}, bf16[128,2048]{1,0:T(8,128)(2,1)S(1)}, u32[]{:S(2)}, u32[]{:S(2)}) collective-permute-start(bf16[128,2048]{1,0:T(8,128)(2,1)} %refs_0_.1), channel_id=1, source_target_pairs={{0,8},{4,12},{8,16},{12,20},{16,24},{20,28},{24,0},{28,4},{1,9},{5... | collective-permute-start | bytes 1572872 | tf_op jit(solution)/shard_map/ppermute | solution.py:97
  28.0 207.0 %all-gather.5.cloned.1.call-start = ((), (), s32[]{:S(2)}) async-start(), calls=%async_computation.3 | async-start | bytes 4718592 | tf_op jit(solution)/shard_map/all_gather | solution.py:248
  29.4 56.6 %collective-permute-start.3 = (bf16[512,2048]{1,0:T(8,128)(2,1)}, bf16[512,2048]{1,0:T(8,128)(2,1)}, u32[]{:S(2)}, u32[]{:S(2)}) collective-permute-start(bf16[512,2048]{1,0:T(8,128)(2,1)} %after.7), channel_id=1, source_target_pairs={{0,2},{1,3},{2,0},{3,1},{4,6},{5,7},{6,4},{7,5},{8,10},{9,11},{10,... | collective-permute-start | bytes 6291464 | tf_op jit(solution)/shard_map/ppermute | solution.py:41
  30.9 54.1 %collective-permute-start.4 = (bf16[128,2048]{1,0:T(8,128)(2,1)S(1)}, bf16[128,2048]{1,0:T(8,128)(2,1)}, u32[]{:S(2)}, u32[]{:S(2)}) collective-permute-start(bf16[128,2048]{1,0:T(8,128)(2,1)S(1)} %copy-done.25), channel_id=1, source_target_pairs={{0,16},{4,20},{8,24},{12,28},{16,0},{20,4},{24,8},{28,12},{1,17},{... | collective-permute-start | bytes 1572872 | tf_op jit(solution)/shard_map/ppermute | solution.py:97
  32.3 53.7 %collective-permute-start.5 = (bf16[128,2048]{1,0:T(8,128)(2,1)S(1)}, bf16[128,2048]{1,0:T(8,128)(2,1)}, u32[]{:S(2)}, u32[]{:S(2)}) collective-permute-start(bf16[128,2048]{1,0:T(8,128)(2,1)S(1)} %copy-done.25), channel_id=1, source_target_pairs={{0,24},{4,28},{8,0},{12,4},{16,8},{20,12},{24,16},{28,20},{1,25},{... | collective-permute-start | bytes 1572872 | tf_op jit(solution)/shard_map/ppermute | solution.py:97
  33.9 52.1 %collective-permute-start.6 = (bf16[128,2048]{1,0:T(8,128)(2,1)S(1)}, bf16[128,2048]{1,0:T(8,128)(2,1)S(1)}, u32[]{:S(2)}, u32[]{:S(2)}) collective-permute-start(bf16[128,2048]{1,0:T(8,128)(2,1)S(1)} %copy-done.25), channel_id=1, source_target_pairs={{0,4},{4,0},{8,12},{12,8},{16,20},{20,16},{24,28},{28,24},{1,5},{5... | collective-permute-start | bytes 1572872 | tf_op jit(solution)/shard_map/ppermute | solution.py:101
  100.9 25.8 %collective-permute-start.10 = (bf16[256,2048]{1,0:T(8,128)(2,1)}, bf16[256,2048]{1,0:T(8,128)(2,1)S(1)}, u32[]{:S(2)}, u32[]{:S(2)}) collective-permute-start(bf16[256,2048]{1,0:T(8,128)(2,1)} %get-tuple-element.79), channel_id=1, source_target_pairs={{0,2},{1,3},{2,0},{3,1},{4,6},{5,7},{6,4},{7,5},{8,10},{9,11},{10,... | collective-permute-start | bytes 3145736 | tf_op jit(solution)/shard_map/ppermute | solution.py:41
  101.5 39.1 %collective-permute-start.9 = (bf16[512,2048]{1,0:T(8,128)(2,1)S(1)}, bf16[512,2048]{1,0:T(8,128)(2,1)}, u32[]{:S(2)}, u32[]{:S(2)}) collective-permute-start(bf16[512,2048]{1,0:T(8,128)(2,1)S(1)} %bitcast.188), channel_id=1, source_target_pairs={{0,1},{1,0},{2,3},{3,2},{4,5},{5,4},{6,7},{7,6},{8,9},{9,8},{10,11... | collective-permute-start | bytes 6291464 | tf_op jit(solution)/shard_map/ppermute | solution.py:41
  134.0 84.4 %collective-permute-start.15 = (bf16[512,2048]{1,0:T(8,128)(2,1)}, bf16[512,2048]{1,0:T(8,128)(2,1)}, u32[]{:S(2)}, u32[]{:S(2)}) collective-permute-start(bf16[512,2048]{1,0:T(8,128)(2,1)} %bitcast.202), channel_id=1, source_target_pairs={{0,1},{1,0},{2,3},{3,2},{4,5},{5,4},{6,7},{7,6},{8,9},{9,8},{10,11... | collective-permute-start | bytes 6291464 | tf_op jit(solution)/shard_map/ppermute | solution.py:41
  137.7 63.8 %collective-permute-start.17 = (bf16[128,2048]{1,0:T(8,128)(2,1)}, bf16[128,2048]{1,0:T(8,128)(2,1)}, u32[]{:S(2)}, u32[]{:S(2)}) collective-permute-start(bf16[128,2048]{1,0:T(8,128)(2,1)} %get-tuple-element.89.refs_1_), channel_id=1, source_target_pairs={{0,4},{4,0},{8,12},{12,8},{16,20},{20,16},{24,28},{28,24},{1,5},{5... | collective-permute-start | bytes 1572872 | tf_op jit(solution)/shard_map/ppermute | solution.py:101
  138.3 314.9 %reduce-scatter.3.cloned.1.call-start = ((), (), s32[]{:S(2)}) async-start(), calls=%async_computation.4 | async-start | bytes 9437184 | tf_op jit(solution)/shard_map/reduce_scatter | solution.py:354
  152.6 12.9 %collective-permute-start.12 = (bf16[1024,128]{1,0:T(8,128)(2,1)S(1)}, bf16[1024,128]{1,0:T(8,128)(2,1)S(1)}, u32[]{:S(2)}, u32[]{:S(2)}) collective-permute-start(bf16[1024,128]{1,0:T(8,128)(2,1)S(1)} %bc_forward.1.b0), channel_id=1, source_target_pairs={{0,1},{1,0},{2,3},{3,2},{4,5},{5,4},{6,7},{7,6},{8,9},{9,8},{10,11... | collective-permute-start | bytes 786440 | tf_op jit(solution)/shard_map/ppermute | solution.py:41
  152.7 14.4 %collective-permute-start.13 = (bf16[1024,128]{1,0:T(8,128)(2,1)S(1)}, bf16[1024,128]{1,0:T(8,128)(2,1)S(1)}, u32[]{:S(2)}, u32[]{:S(2)}) collective-permute-start(bf16[1024,128]{1,0:T(8,128)(2,1)S(1)} %bc_forward.1.b0), channel_id=1, source_target_pairs={{0,2},{1,3},{2,0},{3,1},{4,6},{5,7},{6,4},{7,5},{8,10},{9,11},{10,... | collective-permute-start | bytes 786440 | tf_op jit(solution)/shard_map/ppermute | solution.py:41
  154.3 13.4 %collective-permute-start.14 = (bf16[1024,128]{1,0:T(8,128)(2,1)S(1)}, bf16[1024,128]{1,0:T(8,128)(2,1)S(1)}, u32[]{:S(2)}, u32[]{:S(2)}) collective-permute-start(bf16[1024,128]{1,0:T(8,128)(2,1)S(1)} %bc_forward.1.b0), channel_id=1, source_target_pairs={{0,3},{1,2},{2,1},{3,0},{4,7},{5,6},{6,5},{7,4},{8,11},{9,10},{10,... | collective-permute-start | bytes 786440 | tf_op jit(solution)/shard_map/ppermute | solution.py:41
  165.5 36.1 %collective-permute-start.18 = (bf16[128,2048]{1,0:T(8,128)(2,1)}, bf16[128,2048]{1,0:T(8,128)(2,1)}, u32[]{:S(2)}, u32[]{:S(2)}) collective-permute-start(bf16[128,2048]{1,0:T(8,128)(2,1)} %get-tuple-element.90.refs_2_), channel_id=1, source_target_pairs={{0,4},{4,0},{8,12},{12,8},{16,20},{20,16},{24,28},{28,24},{1,5},{5... | collective-permute-start | bytes 1572872 | tf_op jit(solution)/shard_map/ppermute | solution.py:101
  167.1 41.6 %collective-permute-start.19 = (bf16[128,2048]{1,0:T(8,128)(2,1)}, bf16[128,2048]{1,0:T(8,128)(2,1)}, u32[]{:S(2)}, u32[]{:S(2)}) collective-permute-start(bf16[128,2048]{1,0:T(8,128)(2,1)} %get-tuple-element.91.refs_3_), channel_id=1, source_target_pairs={{0,4},{4,0},{8,12},{12,8},{16,20},{20,16},{24,28},{28,24},{1,5},{5... | collective-permute-start | bytes 1572872 | tf_op jit(solution)/shard_map/ppermute | solution.py:101
  168.3 40.4 %collective-permute-start.16 = (bf16[256,2048]{1,0:T(8,128)(2,1)}, bf16[256,2048]{1,0:T(8,128)(2,1)}, u32[]{:S(2)}, u32[]{:S(2)}) collective-permute-start(bf16[256,2048]{1,0:T(8,128)(2,1)} %get-tuple-element.88), channel_id=1, source_target_pairs={{0,2},{1,3},{2,0},{3,1},{4,6},{5,7},{6,4},{7,5},{8,10},{9,11},{10,... | collective-permute-start | bytes 3145736 | tf_op jit(solution)/shard_map/ppermute | solution.py:41
  201.6 16.9 %collective-permute-start.20 = (bf16[256,2048]{1,0:T(8,128)(2,1)S(1)}, bf16[256,2048]{1,0:T(8,128)(2,1)}, u32[]{:S(2)}, u32[]{:S(2)}) collective-permute-start(bf16[256,2048]{1,0:T(8,128)(2,1)S(1)} %copy-done.8), channel_id=1, source_target_pairs={{0,1},{1,0},{2,3},{3,2},{4,5},{5,4},{6,7},{7,6},{8,9},{9,8},{10,11... | collective-permute-start | bytes 3145736 | tf_op jit(solution)/shard_map/ppermute | solution.py:41
  303.0 251.5 %reduce-scatter.5.cloned.1.call-start = ((), (), s32[]{:S(2)}) async-start(), calls=%async_computation.5 | async-start | bytes 5308416 | tf_op jit(solution)/shard_map/reduce_scatter | solution.py:354
  381.9 11.9 %collective-permute-start.25 = (bf16[2,512,2048]{2,1,0:T(8,128)(2,1)}, bf16[2,512,2048]{2,1,0:T(8,128)(2,1)}, u32[]{:S(2)}, u32[]{:S(2)}) collective-permute-start(bf16[2,512,2048]{2,1,0:T(8,128)(2,1)} %dynamic-slice_bitcast_fusion), channel_id=1, source_target_pairs={{0,1},{1,0},{2,3},{3,2},{4,5},{5,4},{6,7},{7,6},{8,9},{9,8},{10,11... | collective-permute-start | bytes 12582920 | tf_op jit(solution)/shard_map/ppermute | solution.py:41
  401.5 51.6 %collective-permute-start.28 = (bf16[512,2048]{1,0:T(8,128)(2,1)}, bf16[512,2048]{1,0:T(8,128)(2,1)}, u32[]{:S(2)}, u32[]{:S(2)}) collective-permute-start(bf16[512,2048]{1,0:T(8,128)(2,1)} %get-tuple-element.111), channel_id=1, source_target_pairs={{0,2},{1,3},{2,0},{3,1},{4,6},{5,7},{6,4},{7,5},{8,10},{9,11},{10,... | collective-permute-start | bytes 6291464 | tf_op jit(solution)/shard_map/ppermute | solution.py:41
  465.1 48.0 %collective-permute-start.34 = (bf16[512,2048]{1,0:T(8,128)(2,1)}, bf16[512,2048]{1,0:T(8,128)(2,1)}, u32[]{:S(2)}, u32[]{:S(2)}) collective-permute-start(bf16[512,2048]{1,0:T(8,128)(2,1)} %get-tuple-element.127), channel_id=1, source_target_pairs={{0,2},{1,3},{2,0},{3,1},{4,6},{5,7},{6,4},{7,5},{8,10},{9,11},{10,... | collective-permute-start | bytes 6291464 | tf_op jit(solution)/shard_map/ppermute | solution.py:41
  513.7 13.8 %collective-permute-start.43 = (f32[48,128]{1,0:T(8,128)}, f32[48,128]{1,0:T(8,128)S(1)}, u32[]{:S(2)}, u32[]{:S(2)}) collective-permute-start(f32[48,128]{1,0:T(8,128)} %get-tuple-element.131), channel_id=1, source_target_pairs={{0,1},{1,0},{2,3},{3,2},{4,5},{5,4},{6,7},{7,6},{8,9},{9,8},{10,11... | collective-permute-start | bytes 73736 | tf_op jit(solution)/shard_map/ppermute | solution.py:41
  (74 other events, 520.3 us)
Sparse Core Ops, SparseCore 0:
  28.1 105.7 all-gather.2
  138.4 89.9 all-gather.4
  303.1 148.7 reduce-scatter.2
  455.8 98.6 reduce-scatter.4

commit v6 on v5

--- a/solution.py
+++ b/solution.py
@@ -1074,7 +1074,7 @@
 def products(normed, d_z, rounded_out, cot):
     length = normed.shape[0]
     rows = D // STRIPS
-    each = 2
+    each = 1
     whole = lambda i: (0, 0)
     across = lambda i: (0, i)
     return pl.pallas_call(
@@ -1088,7 +1088,7 @@
         ],
         out_specs=pl.BlockSpec((each, rows + 2 * LANES, OWN), lambda i: (i, 0, 0)),
         out_shape=jax.ShapeDtypeStruct((STRIPS, rows + 2 * LANES, OWN), bf16),
-        compiler_params=pltpu.CompilerParams(vmem_limit_bytes=56 * 2**20),
+        compiler_params=pltpu.CompilerParams(vmem_limit_bytes=38 * 2**20),
         cost_estimate=pl.CostEstimate(
             flops=4 * length * D * OWN, bytes_accessed=2**25, transcendentals=0
         ),

time: 581 us -> 580 us (level)
  no operation moved by 1% of the time
where the time goes in v6:
time: 580 us; the launch traced here: 574 us
  Pallas kernels  218 us (38%)
  waiting for transfers between devices  187 us (32%)
  matrix products  42.1 us (7%)
  other arithmetic  40.1 us (7%)
  local copies, waits for them, and re-layouts  36.4 us (6%)
  starting transfers between devices  35.6 us (6%)
  between operations  15.5 us (3%)
    ppermute x33, waiting for transfers between devices, xor_seq(): return lax.ppermute(value, 'seq', [(s, s ^ bits) for s in range(PART)])  103 us
    pallas_call x1, Pallas kernels, recurrence_backward(): pl.pallas_call(backward_kernel, grid_spec=pltpu.PrefetchScalarGridSpec(nu...  61.8 us
    ppermute x6, waiting for transfers between devices, dp_shift_z(): return lax.ppermute(value, 'dp', pairs)  54.5 us
    pallas_call x1, Pallas kernels, recurrence_forward(): pl.pallas_call(forward_kernel, grid_spec=pltpu.PrefetchScalarGridSpec(num...  31.1 us
    pallas_call x1, Pallas kernels, input_gradient(): pl.pallas_call(input_gradient_kernel, grid_spec=pltpu.PrefetchScalarGridS...  27.8 us
    pallas_call x1, Pallas kernels, products(): pl.pallas_call(products_kernel, grid=(STRIPS // each,), in_specs=[pl.Bloc...  27.4 us
    dot_general x3, matrix products, dot_nn(): lax.dot_general(a, b, (((1,), (0,)), ((), ())), preferred_element_type=f32)  25.7 us
    ppermute x33, starting transfers between devices, xor_seq(): return lax.ppermute(value, 'seq', [(s, s ^ bits) for s in range(PART)])  19.7 us
  transfers between devices with their start and end apart: 48, of which 22 were waited for; matrix products, arithmetic and copies ran while one was open for 17% of the time, Pallas kernels for 27%

profile of v6, /device:TPU:8, one launch (start us, length us, event | category | flops | bytes accessed | tf_op | source)
XLA Modules:
  0.0 574.4 jit_solution(15002379934455323639)
XLA Ops:
  15.6 7.2 %collective-permute-done.refs_0_ = bf16[2,64,1152]{2,1,0:T(8,128)(2,1)S(1)} collective-permute-done((bf16[2,64,1152]{2,1,0:T(8,128)(2,1)}, bf16[2,64,1152]{2,1,0:T(8,128)(2,1)S(1)}, u32[]{:S(2)}, u32[]{:S(2)}) %collective-permute-start) | collective-permute-done | bytes 294944 | tf_op jit(solution)/shard_map/ppermute | solution.py:41
  35.4 49.5 %collective-permute-done.4.refs_2_ = bf16[128,2048]{1,0:T(8,128)(2,1)} collective-permute-done((bf16[128,2048]{1,0:T(8,128)(2,1)S(1)}, bf16[128,2048]{1,0:T(8,128)(2,1)}, u32[]{:S(2)}, u32[]{:S(2)}) %collective-permute-start.4) | collective-permute-done | bytes 524320 | tf_op jit(solution)/shard_map/ppermute | solution.py:97
  88.3 6.7 %collective-permute-done.7.refs_0_ = bf16[2,64,1024]{2,1,0:T(8,128)(2,1)S(1)} collective-permute-done((bf16[2,64,1024]{2,1,0:T(8,128)(2,1)S(1)}, bf16[2,64,1024]{2,1,0:T(8,128)(2,1)S(1)}, u32[]{:S(2)}, u32[]{:S(2)}) %collective-permute-start.7) | collective-permute-done | bytes 262176 | tf_op jit(solution)/shard_map/ppermute | solution.py:41
  101.6 25.0 %collective-permute-done.10.refs_2_ = bf16[256,2048]{1,0:T(8,128)(2,1)S(1)} collective-permute-done((bf16[256,2048]{1,0:T(8,128)(2,1)}, bf16[256,2048]{1,0:T(8,128)(2,1)S(1)}, u32[]{:S(2)}, u32[]{:S(2)}) %collective-permute-start.10) | collective-permute-done | bytes 1048608 | tf_op jit(solution)/shard_map/ppermute | solution.py:41
  126.7 7.2 %all-gather.3.cloned.1.call-done.refs_3_.wc_ref = bf16[2048,1152]{1,0:T(8,128)(2,1)} async-done(((bf16[256,1152]{1,0:T(8,128)(2,1)}), bf16[2048,1152]{1,0:T(8,128)(2,1)}) %all-gather.3.cloned.1.call-update) | async-done | bytes 4718608 | tf_op jit(solution)/shard_map/all_gather | solution.py:235
  141.1 8.4 %all_positions.1.n_ref = bf16[2048,2048]{1,0:T(8,128)(2,1)S(1)} custom-call(s32[4]{0:T(128)S(1)} %pad_add_fusion.order_ref, bf16[512,2048]{1,0:T(8,128)(2,1)S(1)} %bitcast.189, bf16[512,2048]{1,0:T(8,128)(2,1)} %collective-permute-done.9.refs_1_, bf16[512,2048]{1,0:T(8,128)(2,1)} %get-tuple-element.80.refs_2_, ...), custom_call_target="tpu_custom_call" | custom-call | flops 16777216 | bytes 16777216 | tf_op jit(solution)/shard_map/all_positions/pallas_call | solution.py:296
  154.6 10.9 %select_convert_fusion.refs_1_ = bf16[2048,1024]{1,0:T(8,128)(2,1)} fusion(pred[1024]{0:T(1024)(128)(4,1)S(1)} %fusion.36, bf16[2048,2048]{1,0:T(8,128)(2,1)S(1)} %all_positions.1.n_ref, bf16[2048,1152]{1,0:T(8,128)(2,1)S(1)} %bitcast.210), kind=kOutput, calls=%fused_computation | convolution fusion | flops 8594128896 | bytes 16778240 | tf_op jit(solution)/shard_map/dot_general | solution.py:393
  170.4 31.1 %recurrence_forward.1 = (f32[2048,1024]{1,0:T(8,128)}, bf16[2048,1024]{1,0:T(8,128)(2,1)}, bf16[8,128,1024]{2,1,0:T(8,128)(2,1)}) custom-call(s32[1]{0:T(128)} %bitcast.1.me_ref, bf16[2048,1024]{1,0:T(8,128)(2,1)} %get-tuple-element.81.ci_ref.prev_ref, bf16[1024,128]{1,0:T(8,128)(2,1)} %copy-done.9, bf16[1024,128]{1,0:T(8,128)(2,1)} %get-tuple-element.82.b1, ...), custom_call_target="tpu_custom_call" | custom-call | flops 40000000000 | bytes 16777216 | tf_op jit(solution)/shard_map/recurrence_forward/pallas_call | solution.py:629
  201.6 7.0 %collective-permute-done.19.refs_3_ = bf16[128,2048]{1,0:T(8,128)(2,1)} collective-permute-done((bf16[128,2048]{1,0:T(8,128)(2,1)}, bf16[128,2048]{1,0:T(8,128)(2,1)}, u32[]{:S(2)}, u32[]{:S(2)}) %collective-permute-start.19) | collective-permute-done | bytes 524320 | tf_op jit(solution)/shard_map/ppermute | solution.py:101
  212.9 5.5 assemble.1.wo_ref
  218.5 16.4 %pull_out.1 = (bf16[2048,2048]{1,0:T(8,128)(2,1)}, f32[2048,1024]{1,0:T(8,128)}) custom-call(s32[4]{0:T(128)S(1)} %pad_add_fusion.order_ref, bf16[512,2048]{1,0:T(8,128)(2,1)} %bitcast.203, bf16[512,2048]{1,0:T(8,128)(2,1)} %collective-permute-done.15.sibling, bf16[256,2048]{1,0:T(8,128)(2,1)S(1)} %copy-done.8, ...), custom_call_target="tpu_custom_call" | custom-call | flops 8589934592 | bytes 33554432 | tf_op jit(solution)/shard_map/pull_out/pallas_call | solution.py:912
  234.9 19.3 %gate_forward.1 = (f32[2048,1024]{1,0:T(8,128)}, f32[8,2048]{1,0:T(8,128)S(1)}) custom-call(bf16[2048,2048]{1,0:T(8,128)(2,1)} %copy-done.1, f32[2048,1024]{1,0:T(8,128)} %get-tuple-element.86.y_ref, f32[2048,1024]{1,0:T(8,128)} %get-tuple-element.98.d_ref, bf16[2048,1024]{1,0:T(8,128)(2,1)} %all-gather.5.cloned.1.call-done.wg_ref, ...), custom_call_target="tpu_custom_call" | custom-call | flops 8589934592 | bytes 33554432 | tf_op jit(solution)/shard_map/gate_forward/pallas_call | solution.py:948
  260.1 11.8 %gate_backward.1 = (bf16[2048,1024]{1,0:T(8,128)(2,1)S(1)}, bf16[2048,1024]{1,0:T(8,128)(2,1)S(1)}, bf16[2048,1024]{1,0:T(8,128)(2,1)S(1)}, f32[8,1024]{1,0:T(8,128)S(1)}) custom-call(f32[2048,1024]{1,0:T(8,128)S(1)} %bitcast.191, f32[2048,1024]{1,0:T(8,128)} %get-tuple-element.100.z_ref, f32[2048,1024]{1,0:T(8,128)} %get-tuple-element.98.d_ref, ...), custom_call_target="tpu_custom_call" | custom-call | flops 62914560 | bytes 37748736 | tf_op jit(solution)/shard_map/gate_backward/pallas_call | solution.py:1005
  273.9 27.4 %products.1.refs_1_ = bf16[8,512,1024]{2,1,0:T(8,128)(2,1)} custom-call(bf16[2048,2048]{1,0:T(8,128)(2,1)} %copy-done.1, bf16[2048,1024]{1,0:T(8,128)(2,1)S(1)} %get-tuple-element.103.z_ref, bf16[2048,1024]{1,0:T(8,128)(2,1)S(1)} %get-tuple-element.104.r_ref.refs_2_, bf16[2048,2048]{1,0:T(8,128)(2,1)} %get-tuple-element.105.t_ref), custom_call_target="tpu_custom_call" | custom-call | flops 17179869184 | bytes 33554432 | tf_op jit(solution)/shard_map/products/pallas_call | solution.py:1080
  301.4 61.8 %recurrence_backward.1 = (bf16[2048,1152]{1,0:T(8,128)(2,1)}, bf16[4,1024,128]{2,1,0:T(8,128)(2,1)}, f32[2048,128]{1,0:T(8,128)}, f32[8,1024]{1,0:T(8,128)}, f32[8,128]{1,0:T(8,128)}) custom-call(s32[1]{0:T(128)} %bitcast.1.me_ref, bf16[2048,1024]{1,0:T(8,128)(2,1)} %get-tuple-element.81.ci_ref.prev_ref, ...), custom_call_target="tpu_custom_call" | custom-call | flops 70000001024 | bytes 16777216 | tf_op jit(solution)/shard_map/recurrence_backward/pallas_call | solution.py:828
  363.2 12.4 %convolution_convert_fusion.1 = bf16[2048,2048]{1,0:T(8,128)(2,1)S(1)} fusion(bf16[2048,1024]{1,0:T(8,128)(2,1)} %get-tuple-element.109, bf16[1024,2048]{1,0:T(8,128)(2,1)} %assemble.1.wo_ref), kind=kOutput, calls=%fused_computation.2 | convolution fusion | flops 8594128896 | bytes 16777216 | tf_op jit(solution)/shard_map/dot_general | solution.py:393
  381.6 6.9 %collective-permute-done.26 = bf16[2,1024,128]{2,1,0:T(8,128)(2,1)} collective-permute-done((bf16[2,1024,128]{2,1,0:T(8,128)(2,1)}, bf16[2,1024,128]{2,1,0:T(8,128)(2,1)}, u32[]{:S(2)}, u32[]{:S(2)}) %collective-permute-start.26) | collective-permute-done | bytes 524320 | tf_op jit(solution)/shard_map/ppermute | solution.py:41
  407.2 16.4 %convolution_convert_fusion.refs_1_ = bf16[2048,1152]{1,0:T(8,128)(2,1)} fusion(bf16[2048,2048]{1,0:T(8,128)(2,1)} %copy-done.1, bf16[2048,1152]{1,0:T(8,128)(2,1)} %get-tuple-element.115.refs_0_), kind=kOutput, calls=%fused_computation.1 | convolution fusion | flops 9666035712 | bytes 17825792 | tf_op jit(solution)/shard_map/dot_general | solution.py:401
  423.6 27.8 %input_gradient.1 = (bf16[1024,2048]{1,0:T(8,128)(2,1)}, bf16[1024,2048]{1,0:T(8,128)(2,1)}) custom-call(s32[1]{0:T(128)S(6)} %select_n.316.core_ref, bf16[2048,1024]{1,0:T(8,128)(2,1)} %copy-done.13, bf16[2048,1152]{1,0:T(8,128)(2,1)} %get-tuple-element.116.p_ref, bf16[2048,1024]{1,0:T(8,128)(2,1)} %all-gather.5.cloned.1.call-done.wg_ref, ...), custom_call_target="tpu_custom_call" | custom-call | flops 10000000000 | bytes 4194304 | tf_op jit(solution)/shard_map/input_gradient/pallas_call | solution.py:1038
  454.0 4.9 collective-permute-done.29
  478.2 33.1 %collective-permute-done.34.refs_1_ = bf16[512,2048]{1,0:T(8,128)(2,1)} collective-permute-done((bf16[512,2048]{1,0:T(8,128)(2,1)}, bf16[512,2048]{1,0:T(8,128)(2,1)}, u32[]{:S(2)}, u32[]{:S(2)}) %collective-permute-start.34) | collective-permute-done | bytes 2097184 | tf_op jit(solution)/shard_map/ppermute | solution.py:41
  512.0 4.7 fusion.2
  517.3 8.6 %fusion.15 = (bf16[1,512,2048]{2,1,0:T(8,128)(2,1)}, bf16[1,512,2048]{2,1,0:T(8,128)(2,1)}) fusion(bf16[512,2048]{1,0:T(8,128)(2,1)} %get-tuple-element.128.refs_1_, f32[512]{0:T(512)S(1)} %broadcast_multiply_fusion, f32[512]{0:T(512)S(1)} %get-tuple-element.169, f32[2048]{0:T(1024)S(1)} %copy-done.37, f32[512]{0:T(512)S(1)} %get-tuple-element.168, ...), kind=kLoop, calls=%fused_computation.25 | loop fusion | flops 22020096 | bytes 20985868 | tf_op jit(solution)/shard_map/broadcast_in_dim | solution.py:1356
  540.3 12.5 %reduce-scatter.5.cloned.1.call-done.refs_0_ = bf16[256,1152]{1,0:T(8,128)(2,1)} async-done(((bf16[2048,1152]{1,0:T(8,128)(2,1)}), bf16[256,1152]{1,0:T(8,128)(2,1)}) %reduce-scatter.5.cloned.1.call-update) | async-done | bytes 589840 | tf_op jit(solution)/shard_map/reduce_scatter | solution.py:354
  (319 shorter events, 136.2 us)
Async XLA Ops:
  7.2 126.7 %all-gather.3.cloned.1.call-start = ((), (), s32[]{:S(2)}) async-start(), calls=%async_computation.2 | async-start | bytes 5308416 | tf_op jit(solution)/shard_map/all_gather | solution.py:235
  7.2 15.5 %collective-permute-start.1 = (bf16[128,2048]{1,0:T(8,128)(2,1)}, bf16[128,2048]{1,0:T(8,128)(2,1)S(1)}, u32[]{:S(2)}, u32[]{:S(2)}) collective-permute-start(bf16[128,2048]{1,0:T(8,128)(2,1)} %refs_0_.1), channel_id=1, source_target_pairs={{0,8},{4,12},{8,16},{12,20},{16,24},{20,28},{24,0},{28,4},{1,9},{5... | collective-permute-start | bytes 1572872 | tf_op jit(solution)/shard_map/ppermute | solution.py:97
  28.0 207.0 %all-gather.5.cloned.1.call-start = ((), (), s32[]{:S(2)}) async-start(), calls=%async_computation.3 | async-start | bytes 4718592 | tf_op jit(solution)/shard_map/all_gather | solution.py:248
  29.4 56.6 %collective-permute-start.3 = (bf16[512,2048]{1,0:T(8,128)(2,1)}, bf16[512,2048]{1,0:T(8,128)(2,1)}, u32[]{:S(2)}, u32[]{:S(2)}) collective-permute-start(bf16[512,2048]{1,0:T(8,128)(2,1)} %after.7), channel_id=1, source_target_pairs={{0,2},{1,3},{2,0},{3,1},{4,6},{5,7},{6,4},{7,5},{8,10},{9,11},{10,... | collective-permute-start | bytes 6291464 | tf_op jit(solution)/shard_map/ppermute | solution.py:41
  30.9 54.1 %collective-permute-start.4 = (bf16[128,2048]{1,0:T(8,128)(2,1)S(1)}, bf16[128,2048]{1,0:T(8,128)(2,1)}, u32[]{:S(2)}, u32[]{:S(2)}) collective-permute-start(bf16[128,2048]{1,0:T(8,128)(2,1)S(1)} %copy-done.25), channel_id=1, source_target_pairs={{0,16},{4,20},{8,24},{12,28},{16,0},{20,4},{24,8},{28,12},{1,17},{... | collective-permute-start | bytes 1572872 | tf_op jit(solution)/shard_map/ppermute | solution.py:97
  32.3 53.7 %collective-permute-start.5 = (bf16[128,2048]{1,0:T(8,128)(2,1)S(1)}, bf16[128,2048]{1,0:T(8,128)(2,1)}, u32[]{:S(2)}, u32[]{:S(2)}) collective-permute-start(bf16[128,2048]{1,0:T(8,128)(2,1)S(1)} %copy-done.25), channel_id=1, source_target_pairs={{0,24},{4,28},{8,0},{12,4},{16,8},{20,12},{24,16},{28,20},{1,25},{... | collective-permute-start | bytes 1572872 | tf_op jit(solution)/shard_map/ppermute | solution.py:97
  33.9 52.1 %collective-permute-start.6 = (bf16[128,2048]{1,0:T(8,128)(2,1)S(1)}, bf16[128,2048]{1,0:T(8,128)(2,1)S(1)}, u32[]{:S(2)}, u32[]{:S(2)}) collective-permute-start(bf16[128,2048]{1,0:T(8,128)(2,1)S(1)} %copy-done.25), channel_id=1, source_target_pairs={{0,4},{4,0},{8,12},{12,8},{16,20},{20,16},{24,28},{28,24},{1,5},{5... | collective-permute-start | bytes 1572872 | tf_op jit(solution)/shard_map/ppermute | solution.py:101
  100.9 25.8 %collective-permute-start.10 = (bf16[256,2048]{1,0:T(8,128)(2,1)}, bf16[256,2048]{1,0:T(8,128)(2,1)S(1)}, u32[]{:S(2)}, u32[]{:S(2)}) collective-permute-start(bf16[256,2048]{1,0:T(8,128)(2,1)} %get-tuple-element.79), channel_id=1, source_target_pairs={{0,2},{1,3},{2,0},{3,1},{4,6},{5,7},{6,4},{7,5},{8,10},{9,11},{10,... | collective-permute-start | bytes 3145736 | tf_op jit(solution)/shard_map/ppermute | solution.py:41
  101.5 39.1 %collective-permute-start.9 = (bf16[512,2048]{1,0:T(8,128)(2,1)S(1)}, bf16[512,2048]{1,0:T(8,128)(2,1)}, u32[]{:S(2)}, u32[]{:S(2)}) collective-permute-start(bf16[512,2048]{1,0:T(8,128)(2,1)S(1)} %bitcast.188), channel_id=1, source_target_pairs={{0,1},{1,0},{2,3},{3,2},{4,5},{5,4},{6,7},{7,6},{8,9},{9,8},{10,11... | collective-permute-start | bytes 6291464 | tf_op jit(solution)/shard_map/ppermute | solution.py:41
  134.0 84.4 %collective-permute-start.15 = (bf16[512,2048]{1,0:T(8,128)(2,1)}, bf16[512,2048]{1,0:T(8,128)(2,1)}, u32[]{:S(2)}, u32[]{:S(2)}) collective-permute-start(bf16[512,2048]{1,0:T(8,128)(2,1)} %bitcast.202), channel_id=1, source_target_pairs={{0,1},{1,0},{2,3},{3,2},{4,5},{5,4},{6,7},{7,6},{8,9},{9,8},{10,11... | collective-permute-start | bytes 6291464 | tf_op jit(solution)/shard_map/ppermute | solution.py:41
  137.7 63.8 %collective-permute-start.17 = (bf16[128,2048]{1,0:T(8,128)(2,1)}, bf16[128,2048]{1,0:T(8,128)(2,1)}, u32[]{:S(2)}, u32[]{:S(2)}) collective-permute-start(bf16[128,2048]{1,0:T(8,128)(2,1)} %get-tuple-element.89.refs_1_), channel_id=1, source_target_pairs={{0,4},{4,0},{8,12},{12,8},{16,20},{20,16},{24,28},{28,24},{1,5},{5... | collective-permute-start | bytes 1572872 | tf_op jit(solution)/shard_map/ppermute | solution.py:101
  138.3 313.2 %reduce-scatter.3.cloned.1.call-start = ((), (), s32[]{:S(2)}) async-start(), calls=%async_computation.4 | async-start | bytes 9437184 | tf_op jit(solution)/shard_map/reduce_scatter | solution.py:354
  152.6 12.9 %collective-permute-start.12 = (bf16[1024,128]{1,0:T(8,128)(2,1)S(1)}, bf16[1024,128]{1,0:T(8,128)(2,1)S(1)}, u32[]{:S(2)}, u32[]{:S(2)}) collective-permute-start(bf16[1024,128]{1,0:T(8,128)(2,1)S(1)} %bc_forward.1.b0), channel_id=1, source_target_pairs={{0,1},{1,0},{2,3},{3,2},{4,5},{5,4},{6,7},{7,6},{8,9},{9,8},{10,11... | collective-permute-start | bytes 786440 | tf_op jit(solution)/shard_map/ppermute | solution.py:41
  152.7 14.4 %collective-permute-start.13 = (bf16[1024,128]{1,0:T(8,128)(2,1)S(1)}, bf16[1024,128]{1,0:T(8,128)(2,1)S(1)}, u32[]{:S(2)}, u32[]{:S(2)}) collective-permute-start(bf16[1024,128]{1,0:T(8,128)(2,1)S(1)} %bc_forward.1.b0), channel_id=1, source_target_pairs={{0,2},{1,3},{2,0},{3,1},{4,6},{5,7},{6,4},{7,5},{8,10},{9,11},{10,... | collective-permute-start | bytes 786440 | tf_op jit(solution)/shard_map/ppermute | solution.py:41
  154.3 13.4 %collective-permute-start.14 = (bf16[1024,128]{1,0:T(8,128)(2,1)S(1)}, bf16[1024,128]{1,0:T(8,128)(2,1)S(1)}, u32[]{:S(2)}, u32[]{:S(2)}) collective-permute-start(bf16[1024,128]{1,0:T(8,128)(2,1)S(1)} %bc_forward.1.b0), channel_id=1, source_target_pairs={{0,3},{1,2},{2,1},{3,0},{4,7},{5,6},{6,5},{7,4},{8,11},{9,10},{10,... | collective-permute-start | bytes 786440 | tf_op jit(solution)/shard_map/ppermute | solution.py:41
  165.5 36.1 %collective-permute-start.18 = (bf16[128,2048]{1,0:T(8,128)(2,1)}, bf16[128,2048]{1,0:T(8,128)(2,1)}, u32[]{:S(2)}, u32[]{:S(2)}) collective-permute-start(bf16[128,2048]{1,0:T(8,128)(2,1)} %get-tuple-element.90.refs_2_), channel_id=1, source_target_pairs={{0,4},{4,0},{8,12},{12,8},{16,20},{20,16},{24,28},{28,24},{1,5},{5... | collective-permute-start | bytes 1572872 | tf_op jit(solution)/shard_map/ppermute | solution.py:101
  167.1 41.6 %collective-permute-start.19 = (bf16[128,2048]{1,0:T(8,128)(2,1)}, bf16[128,2048]{1,0:T(8,128)(2,1)}, u32[]{:S(2)}, u32[]{:S(2)}) collective-permute-start(bf16[128,2048]{1,0:T(8,128)(2,1)} %get-tuple-element.91.refs_3_), channel_id=1, source_target_pairs={{0,4},{4,0},{8,12},{12,8},{16,20},{20,16},{24,28},{28,24},{1,5},{5... | collective-permute-start | bytes 1572872 | tf_op jit(solution)/shard_map/ppermute | solution.py:101
  168.3 40.4 %collective-permute-start.16 = (bf16[256,2048]{1,0:T(8,128)(2,1)}, bf16[256,2048]{1,0:T(8,128)(2,1)}, u32[]{:S(2)}, u32[]{:S(2)}) collective-permute-start(bf16[256,2048]{1,0:T(8,128)(2,1)} %get-tuple-element.88), channel_id=1, source_target_pairs={{0,2},{1,3},{2,0},{3,1},{4,6},{5,7},{6,4},{7,5},{8,10},{9,11},{10,... | collective-permute-start | bytes 3145736 | tf_op jit(solution)/shard_map/ppermute | solution.py:41
  201.6 16.9 %collective-permute-start.20 = (bf16[256,2048]{1,0:T(8,128)(2,1)S(1)}, bf16[256,2048]{1,0:T(8,128)(2,1)}, u32[]{:S(2)}, u32[]{:S(2)}) collective-permute-start(bf16[256,2048]{1,0:T(8,128)(2,1)S(1)} %copy-done.8), channel_id=1, source_target_pairs={{0,1},{1,0},{2,3},{3,2},{4,5},{5,4},{6,7},{7,6},{8,9},{9,8},{10,11... | collective-permute-start | bytes 3145736 | tf_op jit(solution)/shard_map/ppermute | solution.py:41
  301.3 251.5 %reduce-scatter.5.cloned.1.call-start = ((), (), s32[]{:S(2)}) async-start(), calls=%async_computation.5 | async-start | bytes 5308416 | tf_op jit(solution)/shard_map/reduce_scatter | solution.py:354
  380.2 11.9 %collective-permute-start.25 = (bf16[2,512,2048]{2,1,0:T(8,128)(2,1)}, bf16[2,512,2048]{2,1,0:T(8,128)(2,1)}, u32[]{:S(2)}, u32[]{:S(2)}) collective-permute-start(bf16[2,512,2048]{2,1,0:T(8,128)(2,1)} %dynamic-slice_bitcast_fusion), channel_id=1, source_target_pairs={{0,1},{1,0},{2,3},{3,2},{4,5},{5,4},{6,7},{7,6},{8,9},{9,8},{10,11... | collective-permute-start | bytes 12582920 | tf_op jit(solution)/shard_map/ppermute | solution.py:41
  399.8 51.6 %collective-permute-start.28 = (bf16[512,2048]{1,0:T(8,128)(2,1)}, bf16[512,2048]{1,0:T(8,128)(2,1)}, u32[]{:S(2)}, u32[]{:S(2)}) collective-permute-start(bf16[512,2048]{1,0:T(8,128)(2,1)} %get-tuple-element.111), channel_id=1, source_target_pairs={{0,2},{1,3},{2,0},{3,1},{4,6},{5,7},{6,4},{7,5},{8,10},{9,11},{10,... | collective-permute-start | bytes 6291464 | tf_op jit(solution)/shard_map/ppermute | solution.py:41
  463.4 48.0 %collective-permute-start.34 = (bf16[512,2048]{1,0:T(8,128)(2,1)}, bf16[512,2048]{1,0:T(8,128)(2,1)}, u32[]{:S(2)}, u32[]{:S(2)}) collective-permute-start(bf16[512,2048]{1,0:T(8,128)(2,1)} %get-tuple-element.127), channel_id=1, source_target_pairs={{0,2},{1,3},{2,0},{3,1},{4,6},{5,7},{6,4},{7,5},{8,10},{9,11},{10,... | collective-permute-start | bytes 6291464 | tf_op jit(solution)/shard_map/ppermute | solution.py:41
  512.0 13.8 %collective-permute-start.43 = (f32[48,128]{1,0:T(8,128)}, f32[48,128]{1,0:T(8,128)S(1)}, u32[]{:S(2)}, u32[]{:S(2)}) collective-permute-start(f32[48,128]{1,0:T(8,128)} %get-tuple-element.131), channel_id=1, source_target_pairs={{0,1},{1,0},{2,3},{3,2},{4,5},{5,4},{6,7},{7,6},{8,9},{9,8},{10,11... | collective-permute-start | bytes 73736 | tf_op jit(solution)/shard_map/ppermute | solution.py:41
  (74 other events, 571.1 us)
Sparse Core Ops, SparseCore 0:
  28.1 105.7 all-gather.2
  138.4 89.9 all-gather.4
  301.5 148.6 reduce-scatter.2
  454.1 98.6 reduce-scatter.4
